TPU v7x, 32 devices: a whole 2x2x4 slice. The times are simulated.
32 devices in a mesh: ctx: 16 (over z, y, x), head: 2 (over core).
Axes of the slice: x: 2, y: 2, z: 4, core: 2. Of those that a mesh axis runs over, the one named last changes fastest.
Arguments:
- queries: bfloat16 [8192, 512], P('ctx', 'head'), may hold values from -12 to 12
- keys: bfloat16 [8192, 512], P('ctx', 'head'), may hold values from -12 to 12
- values: bfloat16 [8192, 1024], P('ctx', 'head'), may hold values from -6 to 6
- input_pre: float32 [8192, 2], P('ctx', 'head'), may hold values from -6 to 98
- forget_pre: float32 [8192, 2], P('ctx', 'head'), may hold values from -2 to 16
- output_pre: float32 [8192, 2], P('ctx', 'head'), may hold values from -8 to 8
- w_out: bfloat16 [1024, 1024], P('ctx', 'head'), may hold values from -0.25 to 0.25
Outputs:
- layer_out: bfloat16 [8192, 1024], P('ctx', 'head')
All inputs are finite; a program needn't handle non-finite values.
Results may differ from a plain program's by a relative error of at most 0.0062.
Values may be sent and summed in bfloat16 or wider, within the bound.
No kernel may reach another device: no remote copies, remote signals or barrier semaphores. Data moves between devices by JAX's collectives and lax.ppermute only.
A program may use at most 128 MiB of HBM per device.

v0:
```python
import jax
import jax.numpy as jnp
from jax import lax
from jax.sharding import PartitionSpec as P


def carried_in(part, axis, combine, identity):
    place = lax.axis_index(axis)
    gathered = jax.tree.map(lambda a: lax.all_gather(a, axis), part)
    state = jax.tree.map(lambda a, e: jnp.zeros_like(a) + jnp.asarray(e, a.dtype), part, identity)

    def one(hop, state):
        return combine(
            state, jax.tree.map(lambda a: lax.dynamic_index_in_dim(a, hop, 0, False), gathered)
        )

    return lax.fori_loop(0, place, one, state)


def combine(earlier, later):
    mem_a, norm_a, top_a, decay_a = earlier
    mem_b, norm_b, top_b, decay_b = later
    top_log = jnp.maximum(decay_b + top_a, top_b)
    keep_old = jnp.exp(decay_b + top_a - top_log)
    fresh_w = jnp.exp(top_b - top_log)
    return (
        keep_old * mem_a + fresh_w * mem_b,
        keep_old * norm_a + fresh_w * norm_b,
        top_log,
        decay_a + decay_b,
    )


def local(queries, keys, values, input_pre, forget_pre, output_pre, w_out):
    tok_rows, width_k = queries.shape
    width_v = values.shape[1]
    score_scale = width_k ** (-0.5)
    input_gain = input_pre[:, 0]
    log_forget_gate = jax.nn.log_sigmoid(forget_pre[:, 0])
    cum_decay = jnp.cumsum(log_forget_gate)
    block_decay = cum_decay[-1:]
    rest_gain = block_decay - cum_decay + input_gain
    top_local = jnp.max(rest_gain, keepdims=True)
    key_weight = jnp.exp(rest_gain - top_local)
    scaled = keys.astype(jnp.float32) * key_weight[:, None]
    memory_local = lax.dot_general(
        scaled.astype(jnp.bfloat16),
        values,
        (((0,), (0,)), ((), ())),
        preferred_element_type=jnp.float32,
    )
    norm_local = jnp.sum(scaled, axis=0)
    identity = (
        jnp.zeros((width_k, width_v), jnp.float32),
        jnp.zeros((width_k,), jnp.float32),
        jnp.full((1,), -1e30, jnp.float32),
        jnp.zeros((1,), jnp.float32),
    )
    memory, norm_vec, top_prev, _ = carried_in(
        (memory_local, norm_local, top_local, block_decay), "ctx", combine, identity
    )
    scores = (
        lax.dot_general(queries, keys, (((1,), (1,)), ((), ())), preferred_element_type=jnp.float32)
        * score_scale
    )
    causal = jnp.arange(tok_rows)[:, None] >= jnp.arange(tok_rows)[None, :]
    rel_gain = jnp.where(
        causal, cum_decay[:, None] - cum_decay[None, :] + input_gain[None, :], -1e30
    )
    top_tok = jnp.maximum(cum_decay + top_prev, jnp.max(rel_gain, axis=1))
    weighted = jnp.exp(rel_gain - top_tok[:, None]) * scores
    den_in = jnp.sum(weighted, axis=1)
    numerator_input = jnp.dot(
        weighted.astype(jnp.bfloat16), values, preferred_element_type=jnp.float32
    )
    lift = jnp.exp(cum_decay + top_prev - top_tok)
    num_out = (
        jnp.dot(queries, memory.astype(jnp.bfloat16), preferred_element_type=jnp.float32)
        * score_scale
    )
    normalizer_output = (
        jnp.dot(queries.astype(jnp.float32), norm_vec, precision=lax.Precision.HIGHEST)
        * score_scale
    )
    numer = numerator_input + lift[:, None] * num_out
    denom = jnp.maximum(jnp.abs(den_in + lift * normalizer_output), jnp.exp(-top_tok))
    hidden = numer / denom[:, None]
    gated_out = (jax.nn.sigmoid(output_pre[:, 0])[:, None] * hidden).astype(jnp.bfloat16)
    gated_whole = lax.all_gather(gated_out, "head", axis=1, tiled=True)
    mixed_out = jnp.dot(
        gated_whole,
        lax.all_gather(w_out, "ctx", axis=0, tiled=True),
        preferred_element_type=jnp.float32,
    )
    return mixed_out.astype(jnp.bfloat16)


def solution(mesh):
    in_specs = (
        P("ctx", "head"),
        P("ctx", "head"),
        P("ctx", "head"),
        P("ctx", "head"),
        P("ctx", "head"),
        P("ctx", "head"),
        P("ctx", "head"),
    )
    out_specs = P("ctx", "head")
    return jax.shard_map(local, mesh=mesh, in_specs=in_specs, out_specs=out_specs, check_vma=False)
```

profile of v0, /device:TPU:0, one launch (start us, length us, event | category | flops | bytes accessed | tf_op | source)
XLA Modules:
  0.0 213.5 jit_solution(15157650038060218964)
XLA Ops:
  6.5 0.0 copy-start
  6.5 0.0 copy-start.3
  6.5 0.0 copy-start.1
  6.5 0.0 copy-start.2
  6.5 0.0 all-gather.12.cloned.1.call-start
  6.6 0.8 neg.27
  7.4 0.3 reduce-window.9
  7.7 0.1 slice.10
  7.8 0.1 slice_reduce_fusion
  7.9 0.1 add_bitcast_fusion
  8.0 1.3 dynamic-slice
  9.3 1.3 fusion.15
  10.6 0.7 add_subtract_fusion
  11.3 2.0 add_reduce_fusion
  13.3 1.3 subtract_exponential_fusion.1
  14.6 0.0 copy-done
  14.6 2.2 %fusion.9 = f32[256,512]{1,0:T(8,128)} fusion(bf16[512,512]{1,0:T(8,128)(2,1)S(1)} %copy-done, bf16[512,256]{1,0:T(8,128)(2,1)} %param.10, f32[512]{0:T(512)S(1)} %bitcast.55), kind=kOutput, calls=%fused_computation.21 | convolution fusion | flops 134610944 | bytes 1312768 | tf_op jit(solution)/shard_map/dot_general | solution.py:46
  16.8 0.0 all-gather.12.cloned.1.call-update
  16.8 0.0 all-gather.10.cloned.1.call-start
  16.9 0.7 all-gather.10.cloned.1.call-update
  17.6 0.0 all-gather.8.cloned.1.call-start
  17.6 1.1 fusion.7
  18.7 0.9 fusion.5
  19.6 42.6 %all-gather.3 = f32[16,1,256]{2,1,0:T(1,128)S(1)} all-gather(f32[1,1,256]{2,1,0:T(1,128)S(1)} %bitcast.65), channel_id=4, replica_groups=mesh['ctx'=16,'head'=2] {'ctx'}, dimensions={0}, use_global_device_ids=true | all-gather | bytes 17408 | tf_op jit(solution)/shard_map/all_gather | solution.py:9
  62.2 0.7 add_divide_fusion
  62.9 1.4 dynamic-update-slice.1
  64.4 37.4 %all-reduce.2 = (f32[16]{0:T(128)S(1)}, f32[16]{0:T(128)S(1)}) all-reduce(f32[16]{0:T(128)S(1)} %get-tuple-element.107, f32[16]{0:T(128)S(1)} %dynamic-update-slice.1), channel_id=2, replica_groups=mesh['ctx'=16,'head'=2] {'ctx'}, use_global_device_ids=true, to_apply=%add | all-reduce | flops 32 | bytes 256
  101.7 31.7 %all-gather.12.cloned.1.call-done = f32[4096,512]{1,0:T(8,128)} async-done(((f32[256,512]{1,0:T(8,128)}), f32[4096,512]{1,0:T(8,128)}) %all-gather.12.cloned.1.call-update) | async-done | bytes 8388624 | tf_op jit(solution)/shard_map/all_gather | solution.py:9
  133.5 0.0 copy-done.2
  133.5 0.3 fusion.17
  133.8 0.0 copy-done.3
  133.8 0.0 copy-done.1
  133.8 0.4 fusion.16
  134.3 0.3 fusion.2
  134.6 1.3 fusion.4
  135.9 0.0 all-gather.8.cloned.1.call-update
  135.9 53.9 %all-gather.10.cloned.1.call-done = bf16[1024,512]{1,0:T(8,128)(2,1)} async-done(((bf16[64,512]{1,0:T(8,128)(2,1)}), bf16[1024,512]{1,0:T(8,128)(2,1)}) %all-gather.10.cloned.1.call-update) | async-done | bytes 1048592 | tf_op jit(solution)/shard_map/all_gather | solution.py:92
  189.8 14.2 %all-gather.8.cloned.1.call-done = bf16[512,1024]{1,0:T(8,128)(2,1)} async-done(((bf16[512,512]{1,0:T(8,128)(2,1)}), bf16[512,1024]{1,0:T(8,128)(2,1)}) %all-gather.8.cloned.1.call-update) | async-done | bytes 1048592 | tf_op jit(solution)/shard_map/all_gather | solution.py:89
  204.0 3.0 %convolution_convert_fusion = bf16[512,512]{1,0:T(8,128)(2,1)} fusion(bf16[512,1024]{1,0:T(8,128)(2,1)} %all-gather.8.cloned.1.call-done, bf16[1024,512]{1,0:T(8,128)(2,1)} %all-gather.10.cloned.1.call-done), kind=kOutput, calls=%fused_computation.13 | convolution fusion | flops 537133056 | bytes 2621440 | tf_op jit(solution)/shard_map/dot_general | solution.py:90
  (10 shorter events, 0.1 us)
Async XLA Ops:
  6.5 8.1 %copy-start = (bf16[512,512]{1,0:T(8,128)(2,1)S(1)}, bf16[512,512]{1,0:T(8,128)(2,1)}, u32[]{:S(2)}) copy-start(bf16[512,512]{1,0:T(8,128)(2,1)} %param.11) | copy-start | bytes 1572868
  6.5 127.3 %copy-start.3 = (f32[512,1]{0,1:T(1,128)S(1)}, f32[512,1]{0,1:T(1,128)}, u32[]{:S(2)}) copy-start(f32[512,1]{0,1:T(1,128)} %param.12) | copy-start | bytes 6148
  6.5 127.3 %copy-start.1 = (bf16[512,256]{1,0:T(8,128)(2,1)S(1)}, bf16[512,256]{1,0:T(8,128)(2,1)}, u32[]{:S(2)}) copy-start(bf16[512,256]{1,0:T(8,128)(2,1)} %param.10) | copy-start | bytes 786436
  6.5 127.0 %copy-start.2 = (bf16[512,256]{1,0:T(8,128)(2,1)S(1)}, bf16[512,256]{1,0:T(8,128)(2,1)}, u32[]{:S(2)}) copy-start(bf16[512,256]{1,0:T(8,128)(2,1)} %param.9) | copy-start | bytes 786436
  6.5 126.9 %all-gather.12.cloned.1.call-start = ((), (), s32[]{:S(2)}) async-start(), calls=%async_computation.2 | async-start | bytes 8912896 | tf_op jit(solution)/shard_map/all_gather | solution.py:9
  16.8 172.9 %all-gather.10.cloned.1.call-start = ((), (), s32[]{:S(2)}) async-start(), calls=%async_computation.1 | async-start | bytes 1114112 | tf_op jit(solution)/shard_map/all_gather | solution.py:92
  17.6 186.4 %all-gather.8.cloned.1.call-start = ((), (), s32[]{:S(2)}) async-start(), calls=%async_computation | async-start | bytes 1572864 | tf_op jit(solution)/shard_map/all_gather | solution.py:89
Sparse Core Ops, SparseCore 0:
  17.0 116.4 all-gather.11
  136.2 53.5 all-gather.9
  191.3 12.5 all-gather.7
where the time goes:
time: 215 us; the launch traced here: 214 us
  waiting for transfers between devices  100 us (47%)
  blocking collectives  79.9 us (37%)
  between operations  13.2 us (6%)
  other arithmetic  7.97 us (4%)
  matrix products  7.53 us (4%)
  local copies, waits for them, and re-layouts  4.27 us (2%)
    all_gather x1, waiting for transfers between devices, local(): lax.all_gather(w_out, 'ctx', axis=0, tiled=True)  53.9 us
    all_gather x1, blocking collectives, carried_in(): gathered = jax.tree.map(lambda a: lax.all_gather(a, axis), part)  42.6 us
    unnamed x1, blocking collectives  37.4 us
    all_gather x1, waiting for transfers between devices, carried_in(): gathered = jax.tree.map(lambda a: lax.all_gather(a, axis), part)  31.7 us
    all_gather x1, waiting for transfers between devices, local(): gated_whole = lax.all_gather(gated_out, 'head', axis=1, tiled=True)  14.2 us
  transfers between devices with their start and end apart: 3, of which 3 were waited for; matrix products, arithmetic and copies ran while one was open for 3% of the time, Pallas kernels for 0%

commit v1 on v0

v1 whole, which is shorter than its diff:
```python
import functools

import jax
import jax.numpy as jnp
from jax import lax
from jax.experimental import pallas as pl
from jax.experimental.pallas import tpu as pltpu
from jax.sharding import PartitionSpec as P

AUX = 16
LANES = 128
NEG = -1e30


def split_groups(n):
    inner = max(a for a in range(1, n + 1) if n % a == 0 and a * a <= n)
    return inner, n // inner


def is_pow2(n):
    return n & (n - 1) == 0


def source(i, k, n):
    return i ^ k if is_pow2(n) else (i + k) % n


def target(i, k, n):
    return i ^ k if is_pow2(n) else (i + n - k) % n


def inner_pairs(n, inner, k):
    return [(j, j - j % inner + target(j % inner, k, inner)) for j in range(n)]


def outer_pairs(n, inner, k):
    outer = n // inner
    return [(j, target(j // inner, k, outer) * inner + j % inner) for j in range(n)]


def pieces3(x):
    hi = x.astype(jnp.bfloat16)
    rest = x - hi.astype(jnp.float32)
    mid = rest.astype(jnp.bfloat16)
    low = (rest - mid.astype(jnp.float32)).astype(jnp.bfloat16)
    return hi, mid, low


def write_aux(ref, at, norm, top, decay):
    lanes = ref.shape[1]
    pad = jnp.zeros((1, lanes - norm.shape[1]), jnp.float32)
    norm = jnp.concatenate([norm, pad], axis=1) if lanes > norm.shape[1] else norm
    wide = [jnp.broadcast_to(x, (1, lanes)) for x in (norm, top, decay)]
    rows = [p.astype(jnp.float32) for x in wide for p in pieces3(x)]
    rows.append(jnp.zeros((AUX - len(rows), lanes), jnp.float32))
    ref[pl.ds(at, AUX), :] = jnp.concatenate(rows, axis=0).astype(jnp.bfloat16)


def read_aux(ref, at):
    aux = ref[pl.ds(at, AUX), :].astype(jnp.float32)
    return [aux[i : i + 1] + aux[i + 1 : i + 2] + aux[i + 2 : i + 3] for i in (0, 3, 6)]


def summary_kernel(inner, forget_ref, input_ref, keys_ref, values_ref, *rest):
    gates_ref, outs, memory = rest[0], rest[1:-1], rest[-1]
    member = lax.rem(lax.axis_index("ctx"), inner)
    rows = forget_ref.shape[0]
    forget = forget_ref[...]
    log_keep = jnp.minimum(forget, 0.0) - jnp.log1p(jnp.exp(-jnp.abs(forget)))
    tri = lax.broadcasted_iota(jnp.int32, (LANES, LANES), 0) <= lax.broadcasted_iota(
        jnp.int32, (LANES, LANES), 1
    )
    parts = jnp.concatenate([p.astype(jnp.float32) for p in pieces3(log_keep)], axis=0)
    sums = jnp.dot(
        parts.astype(jnp.bfloat16),
        tri.astype(jnp.bfloat16),
        preferred_element_type=jnp.float32,
    )
    inside = sums[:rows] + sums[rows : 2 * rows] + sums[2 * rows : 3 * rows]
    base = jnp.zeros((1, 1), jnp.float32)
    cum = []
    for r in range(rows):
        row = inside[r : r + 1]
        cum.append(row + base)
        base = base + row[:, LANES - 1 :]
    cum_decay = jnp.concatenate(cum, axis=0)
    gain = input_ref[...] - cum_decay
    top_gain = jnp.max(jnp.max(gain, axis=1, keepdims=True), axis=0, keepdims=True)
    weight = jnp.exp(gain - top_gain)
    gates_ref[0:rows, :] = gain
    gates_ref[rows : 2 * rows, :] = cum_decay
    along = jnp.concatenate([weight[r : r + 1] for r in range(rows)], axis=1)
    keys = keys_ref[...]
    scaled = (keys.astype(jnp.float32).T * along).astype(jnp.bfloat16)
    memory[...] = jnp.dot(scaled, values_ref[...], preferred_element_type=jnp.float32)
    three = [p.astype(jnp.float32) for p in pieces3(along)]
    three.append(jnp.zeros((AUX - 3, along.shape[1]), jnp.float32))
    norms = jnp.dot(
        jnp.concatenate(three, axis=0).astype(jnp.bfloat16),
        keys,
        preferred_element_type=jnp.float32,
    )
    norm = norms[0:1] + norms[1:2] + norms[2:3]
    piece = memory.shape[0] // inner
    for k, out_ref in enumerate(outs):
        start = pl.multiple_of(target(member, k, inner) * piece, piece)
        out_ref[0:piece, :] = memory[pl.ds(start, piece), :].astype(jnp.bfloat16)
        write_aux(out_ref, piece, norm, base + top_gain, base)


def group_total_kernel(inner, *refs):
    ins, out_ref = refs[:-1], refs[-1]
    member = lax.rem(lax.axis_index("ctx"), inner)
    piece = out_ref.shape[0] - AUX
    where = [source(member, k, inner) for k in range(inner)]
    norms, tops, decays = zip(*[read_aux(r, piece) for r in ins])
    logs = []
    for k in range(inner):
        log = tops[k]
        for o in range(inner):
            if o != k:
                log = log + jnp.where(where[o] > where[k], decays[o], 0.0)
        logs.append(log)
    top = functools.reduce(jnp.maximum, logs)
    total, norm = 0.0, 0.0
    for k in range(inner):
        weight = jnp.exp(logs[k] - top)
        total = total + weight * ins[k][0:piece, :].astype(jnp.float32)
        norm = norm + weight * norms[k]
    out_ref[0:piece, :] = total.astype(jnp.bfloat16)
    write_aux(out_ref, piece, norm, top, functools.reduce(jnp.add, decays))


def prefix_kernel(inner, outer, *refs):
    blocks, totals = refs[:inner], refs[inner : inner + outer - 1]
    outs, state_ref = refs[inner + outer - 1 : -1], refs[-1]
    place = lax.axis_index("ctx")
    member, group = lax.rem(place, inner), lax.div(place, inner)
    piece = blocks[0].shape[0] - AUX
    at = [source(group, k, outer) for k in range(1, outer)]
    t_norm, t_top, t_decay = zip(*[read_aux(r, piece) for r in totals])
    logs = []
    for k in range(outer - 1):
        log = t_top[k]
        for o in range(outer - 1):
            if o != k:
                between = jnp.logical_and(at[o] > at[k], at[o] < group)
                log = log + jnp.where(between, t_decay[o], 0.0)
        logs.append(jnp.where(at[k] < group, log, NEG))
    far_top = functools.reduce(jnp.maximum, logs)
    far, far_norm = 0.0, 0.0
    for k in range(outer - 1):
        weight = jnp.where(at[k] < group, jnp.exp(logs[k] - far_top), 0.0)
        far = far + weight * totals[k][0:piece, :].astype(jnp.float32)
        far_norm = far_norm + weight * t_norm[k]
    where = [source(member, k, inner) for k in range(inner)]
    norms, tops, decays = zip(*[read_aux(r, piece) for r in blocks])
    for t in range(inner):
        end = target(member, t, inner)
        far_log = far_top
        for o in range(inner):
            far_log = far_log + jnp.where(where[o] < end, decays[o], 0.0)
        logs = []
        for k in range(inner):
            log = tops[k]
            for o in range(inner):
                if o != k:
                    between = jnp.logical_and(where[o] > where[k], where[o] < end)
                    log = log + jnp.where(between, decays[o], 0.0)
            logs.append(jnp.where(where[k] < end, log, NEG))
        top = jnp.maximum(functools.reduce(jnp.maximum, logs), far_log)
        top = jnp.maximum(top, NEG)
        weight = jnp.exp(far_log - top)
        memory, norm = weight * far, weight * far_norm
        for k in range(inner):
            weight = jnp.where(where[k] < end, jnp.exp(logs[k] - top), 0.0)
            memory = memory + weight * blocks[k][0:piece, :].astype(jnp.float32)
            norm = norm + weight * norms[k]
        outs[t][...] = memory.astype(jnp.bfloat16)
        if t == 0:
            lanes = state_ref.shape[1]
            pad = jnp.zeros((6, lanes), jnp.float32)
            state_ref[...] = jnp.concatenate([top, norm, pad], axis=0)


def inside_kernel(gates_ref, output_ref, queries_ref, keys_ref, values_ref, num_ref, cols_ref):
    rows = output_ref.shape[0]
    scale = queries_ref.shape[1] ** (-0.5)
    down = lax.broadcasted_iota(jnp.int32, (LANES, LANES), 0)
    across = lax.broadcasted_iota(jnp.int32, (LANES, LANES), 1)
    causal, same = down >= across, down == across
    lane = lax.broadcasted_iota(jnp.int32, (LANES, LANES), 1)
    gain = gates_ref[0:rows, :]
    cum_decay = gates_ref[rows : 2 * rows, :]
    open_gate = jax.nn.sigmoid(output_ref[...])

    def column(row):
        return jnp.sum(jnp.where(same, row, 0.0), axis=1, keepdims=True)

    before = jnp.full((1, 1), NEG, jnp.float32)
    for i in range(rows):
        here = slice(i * LANES, (i + 1) * LANES)
        a_row = gain[i : i + 1]
        peak = jnp.max(jnp.where(causal, a_row, NEG), axis=1, keepdims=True)
        peak = jnp.maximum(peak, before)
        before = jnp.maximum(before, jnp.max(a_row, axis=1, keepdims=True))
        width = (i + 1) * LANES
        scores = lax.dot_general(
            queries_ref[here, :],
            keys_ref[0:width, :],
            (((1,), (1,)), ((), ())),
            preferred_element_type=jnp.float32,
        )
        parts, den = [], 0.0
        for j in range(i + 1):
            diff = gain[j : j + 1] - peak
            if j == i:
                diff = jnp.where(causal, diff, NEG)
            part = jnp.exp(diff) * (scores[:, j * LANES : (j + 1) * LANES] * scale)
            den = den + part
            parts.append(part.astype(jnp.bfloat16))
        weighted = parts[0] if i == 0 else jnp.concatenate(parts, axis=1)
        den = jnp.sum(den, axis=1, keepdims=True)
        num_ref[here, :] = jnp.dot(
            weighted, values_ref[0:width, :], preferred_element_type=jnp.float32
        )
        cols = jnp.where(lane == 0, den, peak)
        cols = jnp.where(lane == 2, column(cum_decay[i : i + 1]), cols)
        cols_ref[here, :] = jnp.where(lane == 3, column(open_gate[i : i + 1]), cols)


def output_kernel(inner, state_ref, queries_ref, num_ref, cols_ref, *rest):
    pieces, out_ref, memory = rest[:inner], rest[inner], rest[inner + 1]
    member = lax.rem(lax.axis_index("ctx"), inner)
    piece = pieces[0].shape[0]
    for k in range(inner):
        start = pl.multiple_of(source(member, k, inner) * piece, piece)
        memory[pl.ds(start, piece), :] = pieces[k][...]
    width = queries_ref.shape[1]
    scale = width ** (-0.5)
    top_prev = state_ref[0:1, 0:1]
    norm = state_ref[1:2, 0:width]
    step = LANES
    for i in range(queries_ref.shape[0] // step):
        here = slice(i * step, (i + 1) * step)
        q = queries_ref[here, :]
        num_out = jnp.dot(q, memory[...], preferred_element_type=jnp.float32)
        den_out = jnp.sum(q.astype(jnp.float32) * norm, axis=1, keepdims=True)
        cols = cols_ref[here, :]
        den_in, peak = cols[:, 0:1], cols[:, 1:2]
        cum_decay, open_gate = cols[:, 2:3], cols[:, 3:4]
        top = jnp.maximum(peak, top_prev)
        keep, lift = jnp.exp(peak - top), jnp.exp(top_prev - top) * scale
        den = jnp.abs(keep * den_in + lift * den_out)
        ratio = open_gate / jnp.maximum(den, jnp.exp(-(cum_decay + top)))
        gated = (keep * ratio) * num_ref[here, :] + (lift * ratio) * num_out
        out_ref[here, :] = gated.astype(jnp.bfloat16)


def project_kernel(heads, order, rows, *refs):
    gated, bufs = refs[:heads], refs[heads:-2]
    out_ref, weights = refs[-2], refs[-1]
    place, head = lax.axis_index("ctx"), lax.axis_index("head")
    at = 0
    for buf in bufs:
        for s in range(buf.shape[0] // rows):
            block = place ^ order[at] if order is not None else at
            start = pl.multiple_of(block * rows, rows)
            weights[pl.ds(start, rows), :] = buf[s * rows : (s + 1) * rows, :]
            at += 1
    width = gated[0].shape[1]
    total = 0.0
    for k in range(heads):
        start = pl.multiple_of(source(head, k, heads) * width, width)
        total = total + jnp.dot(
            gated[k][...], weights[pl.ds(start, width), :], preferred_element_type=jnp.float32
        )
    out_ref[...] = total.astype(jnp.bfloat16)


def call(kernel, out_shape, args, scratch=(), flops=0, moved=0):
    return pl.pallas_call(
        kernel,
        out_shape=out_shape,
        in_specs=[pl.BlockSpec(memory_space=pltpu.VMEM)] * len(args),
        out_specs=jax.tree.map(lambda _: pl.BlockSpec(memory_space=pltpu.VMEM), out_shape),
        scratch_shapes=scratch,
        compiler_params=pltpu.CompilerParams(vmem_limit_bytes=24 * 2**20),
        cost_estimate=pl.CostEstimate(flops=flops, bytes_accessed=moved, transcendentals=0),
    )(*args)


def shape(dims, dtype):
    return jax.ShapeDtypeStruct(dims, dtype)


def local(n_ctx, n_head, queries, keys, values, input_pre, forget_pre, output_pre, w_out):
    tok, width_k = queries.shape
    width_v = values.shape[1]
    inner, outer = split_groups(n_ctx)
    piece = width_k // inner
    bf16, f32 = jnp.bfloat16, jnp.float32
    gate_rows = tok // LANES
    forget, gate_in, gate_out = (
        g.reshape(gate_rows, LANES) for g in (forget_pre, input_pre, output_pre)
    )

    steps = [1 << b for b in reversed(range(n_ctx.bit_length() - 1))] if is_pow2(n_ctx) else []
    order = [0] if is_pow2(n_ctx) else None
    w_held, w_bufs = w_out, [w_out]
    for i, s in enumerate(steps):
        got = lax.ppermute(w_held, "ctx", [(j, j ^ s) for j in range(n_ctx)])
        order = order + [o ^ s for o in order]
        w_bufs = [w_held, got]
        if i < len(steps) - 1:
            w_held = jnp.concatenate(w_bufs, axis=0)
    if order is None:
        w_bufs = [lax.all_gather(w_out, "ctx", axis=0, tiled=True)]

    message = shape((piece + AUX, width_v), bf16)
    gates, *sends = call(
        functools.partial(summary_kernel, inner),
        [shape((2 * gate_rows, LANES), f32)] + [message] * inner,
        (forget, gate_in, keys, values),
        [pltpu.VMEM((width_k, width_v), f32)],
        2 * tok * width_k * width_v,
        2 * tok * (width_k + width_v),
    )
    blocks = [sends[0]] + [
        lax.ppermute(sends[k], "ctx", inner_pairs(n_ctx, inner, k)) for k in range(1, inner)
    ]
    num_in, cols = call(
        inside_kernel,
        [shape((tok, width_v), f32), shape((tok, LANES), f32)],
        (gates, gate_out, queries, keys, values),
        (),
        2 * tok * tok * (width_k + width_v),
        2 * tok * (2 * width_k + 3 * width_v),
    )
    total = call(functools.partial(group_total_kernel, inner), message, blocks)
    totals = [
        lax.ppermute(total, "ctx", outer_pairs(n_ctx, inner, k)) for k in range(1, outer)
    ]
    *prefixes, state = call(
        functools.partial(prefix_kernel, inner, outer),
        [shape((piece, width_v), bf16)] * inner + [shape((8, width_v), f32)],
        (*blocks, *totals),
    )
    parts = [prefixes[0]] + [
        lax.ppermute(prefixes[k], "ctx", inner_pairs(n_ctx, inner, k)) for k in range(1, inner)
    ]
    gated = call(
        functools.partial(output_kernel, inner),
        shape((tok, width_v), bf16),
        (state, queries, num_in, cols, *parts),
        [pltpu.VMEM((width_k, width_v), bf16)],
        2 * tok * width_k * width_v,
    )
    others = [
        lax.ppermute(gated, "head", [(j, target(j, k, n_head)) for j in range(n_head)])
        for k in range(1, n_head)
    ]
    return call(
        functools.partial(project_kernel, n_head, order, w_out.shape[0]),
        shape((tok, w_out.shape[1]), bf16),
        (gated, *others, *w_bufs),
        [pltpu.VMEM((n_ctx * w_out.shape[0], w_out.shape[1]), bf16)],
    )


def solution(mesh):
    spec = P("ctx", "head")
    return jax.shard_map(
        functools.partial(local, mesh.shape["ctx"], mesh.shape["head"]),
        mesh=mesh,
        in_specs=(spec,) * 7,
        out_specs=spec,
        check_vma=False,
    )
```

time: 215 us -> 56.1 us (0.26)
  blocking collectives: 79.9 us -> 0 us
  waiting for transfers between devices: 100 us -> 27.6 us
  starting transfers between devices: 0.11 us -> 20.1 us
  between operations: 13.2 us -> 0.13 us
  matrix products: 7.53 us -> 0 us
  other arithmetic: 7.97 us -> 0.87 us
  Pallas kernels: 0 us -> 5.43 us
  local copies, waits for them, and re-layouts: 4.27 us -> 1.79 us
    all_gather x3 -> x0, waiting for transfers between devices: 99.8 us -> none  [the longest x1 53.9 us: local(): lax.all_gather(w_out, 'ctx', axis=0, tiled=True)]
    all_gather x1 -> x0, blocking collectives: 42.6 us -> none  [carried_in(): gathered = jax.tree.map(lambda a: lax.all_gather(a, axis), part)]
    unnamed x1 -> x0, blocking collectives: 37.4 us -> none
    ppermute x0 -> x14, waiting for transfers between devices: none -> 27.6 us  [the longest x4 16.4 us: local(): got = lax.ppermute(w_held, 'ctx', [(j, j ^ s) for j in range(n_ctx)])]
    ppermute x0 -> x14, starting transfers between devices: none -> 20.1 us  [the longest x4 8.17 us: local(): got = lax.ppermute(w_held, 'ctx', [(j, j ^ s) for j in range(n_ctx)])]
    dot_general x6 -> x0, matrix products: 7.53 us -> none  [the longest x1 3.05 us: local(): jnp.dot(gated_whole, lax.all_gather(w_out, 'ctx', axis=0, tiled=True), pr...]
    pallas_call x0 -> x6, Pallas kernels: none -> 5.43 us  [call(): pl.pallas_call(kernel, out_shape=out_shape, in_specs=[pl.BlockSpec(memory...]
    reduce_max x2 -> x0, other arithmetic: 2.9 us -> none  [the longest x1 2 us: local(): top_local = jnp.max(rest_gain, keepdims=True)]
  transfers between devices with their start and end apart: 3 -> 14, of which waited for: 3 -> 9; matrix products, arithmetic and copies ran while one was open for 3% -> 0% of each run, Pallas kernels for 0% -> 7%
where the time goes in v1:
time: 56.1 us; the launch traced here: 55.9 us
  waiting for transfers between devices  27.6 us (49%)
  starting transfers between devices  20.1 us (36%)
  Pallas kernels  5.43 us (10%)
  local copies, waits for them, and re-layouts  1.79 us (3%)
  other arithmetic  0.87 us (2%)
    ppermute x4, waiting for transfers between devices, local(): got = lax.ppermute(w_held, 'ctx', [(j, j ^ s) for j in range(n_ctx)])  16.4 us
    ppermute x4, starting transfers between devices, local(): got = lax.ppermute(w_held, 'ctx', [(j, j ^ s) for j in range(n_ctx)])  8.17 us
    pallas_call x6, Pallas kernels, call(): pl.pallas_call(kernel, out_shape=out_shape, in_specs=[pl.BlockSpec(memory...  5.43 us
    ppermute x3, waiting for transfers between devices, local(): lax.ppermute(total, 'ctx', outer_pairs(n_ctx, inner, k))  5.37 us
    ppermute x3, starting transfers between devices, local(): lax.ppermute(total, 'ctx', outer_pairs(n_ctx, inner, k))  4.71 us
    ppermute x3, starting transfers between devices, local(): lax.ppermute(sends[k], 'ctx', inner_pairs(n_ctx, inner, k))  3.55 us
    ppermute x3, starting transfers between devices, local(): lax.ppermute(prefixes[k], 'ctx', inner_pairs(n_ctx, inner, k))  3.55 us
    ppermute x3, waiting for transfers between devices, local(): lax.ppermute(prefixes[k], 'ctx', inner_pairs(n_ctx, inner, k))  3.14 us
  transfers between devices with their start and end apart: 14, of which 9 were waited for; matrix products, arithmetic and copies ran while one was open for 0% of the time, Pallas kernels for 7%

profile of v1, /device:TPU:0, one launch (start us, length us, event | category | flops | bytes accessed | tf_op | source)
XLA Modules:
  0.0 55.9 jit_solution(11875732105323759740)
XLA Ops:
  0.0 0.0 copy-start.2
  0.0 4.0 %collective-permute-start.10 = (bf16[64,512]{1,0:T(8,128)(2,1)}, bf16[64,512]{1,0:T(8,128)(2,1)S(1)}, u32[]{:S(2)}, u32[]{:S(2)}) collective-permute-start(bf16[64,512]{1,0:T(8,128)(2,1)} %param.13), channel_id=1, source_target_pairs={{0,16},{2,18},{4,20},{6,22},{8,24},{10,26},{12,28},{14,30},{16,0},... | collective-permute-start | bytes 196616 | tf_op jit(solution)/shard_map/ppermute | solution.py:312
  4.0 3.9 %collective-permute-done.10 = bf16[64,512]{1,0:T(8,128)(2,1)S(1)} collective-permute-done((bf16[64,512]{1,0:T(8,128)(2,1)}, bf16[64,512]{1,0:T(8,128)(2,1)S(1)}, u32[]{:S(2)}, u32[]{:S(2)}) %collective-permute-start.10) | collective-permute-done | bytes 65568 | tf_op jit(solution)/shard_map/ppermute | solution.py:312
  7.9 0.8 %pad_maximum_fusion.1 = bf16[128,512]{1,0:T(8,128)(2,1)S(1)} fusion(bf16[64,512]{1,0:T(8,128)(2,1)S(1)} %collective-permute-done.10, bf16[64,512]{1,0:T(8,128)(2,1)} %param.13), kind=kLoop, calls=%fused_computation.1 | loop fusion | flops 262144 | bytes 262144 | tf_op jit(solution)/shard_map/concatenate | solution.py:316
  8.7 0.0 copy-start.4
  8.8 0.7 %collective-permute-start.11 = (bf16[128,512]{1,0:T(8,128)(2,1)S(1)}, bf16[128,512]{1,0:T(8,128)(2,1)S(1)}, u32[]{:S(2)}, u32[]{:S(2)}) collective-permute-start(bf16[128,512]{1,0:T(8,128)(2,1)S(1)} %pad_maximum_fusion.1), channel_id=1, source_target_pairs={{0,8},{2,10},{4,12},{6,14},{8,0},{10,2},{12,4},{14,6},{16,24},{18,... | collective-permute-start | bytes 393224 | tf_op jit(solution)/shard_map/ppermute | solution.py:312
  9.5 0.0 copy-done.2
  9.5 0.0 copy-done.4
  9.5 0.0 copy-start
  9.5 1.0 %copy-done = bf16[512,512]{1,0:T(8,128)(2,1)S(1)} copy-done((bf16[512,512]{1,0:T(8,128)(2,1)S(1)}, bf16[512,512]{1,0:T(8,128)(2,1)}, u32[]{:S(2)}) %copy-start) | copy-done | bytes 524312
  10.6 0.0 copy-start.5
  10.6 0.7 %copy-done.5 = f32[512,1]{0,1:T(1,128)S(1)} copy-done((f32[512,1]{0,1:T(1,128)S(1)}, f32[512,1]{0,1:T(1,128)}, u32[]{:S(2)}) %copy-start.5) | copy-done | bytes 2072
  11.2 0.0 copy-start.7
  11.2 0.0 copy-start.3
  11.2 0.6 %shard_map.73 = (f32[8,128]{1,0:T(8,128)S(1)}, bf16[80,512]{1,0:T(8,128)(2,1)S(1)}, bf16[80,512]{1,0:T(8,128)(2,1)S(1)}, bf16[80,512]{1,0:T(8,128)(2,1)S(1)}, bf16[80,512]{1,0:T(8,128)(2,1)S(1)}) custom-call(f32[4,128]{1,0:T(4,128)S(1)} %bitcast.3, f32[4,128]{1,0:T(4,128)S(1)} %bitcast.4, bf16[512,256]{1,0:T(8,128)(2,1)S(1)} %copy-done.2, ...), custom_call_target="tpu_custom_call" | custom-call | flops 134217728 | bytes 786432 | tf_op jit(solution)/shard_map/pallas_call | solution.py:282
  11.9 0.0 copy-start.1
  11.9 1.7 %collective-permute-start = (bf16[80,512]{1,0:T(8,128)(2,1)S(1)}, bf16[80,512]{1,0:T(8,128)(2,1)S(1)}, u32[]{:S(2)}, u32[]{:S(2)}) collective-permute-start(bf16[80,512]{1,0:T(8,128)(2,1)S(1)} %get-tuple-element.18), channel_id=1, source_target_pairs={{0,2},{2,0},{4,6},{6,4},{8,10},{10,8},{12,14},{14,12},{16,18},{18,... | collective-permute-start | bytes 245768 | tf_op jit(solution)/shard_map/ppermute | solution.py:330
  13.6 1.6 %collective-permute-start.1 = (bf16[80,512]{1,0:T(8,128)(2,1)S(1)}, bf16[80,512]{1,0:T(8,128)(2,1)S(1)}, u32[]{:S(2)}, u32[]{:S(2)}) collective-permute-start(bf16[80,512]{1,0:T(8,128)(2,1)S(1)} %get-tuple-element.19), channel_id=1, source_target_pairs={{0,4},{2,6},{4,0},{6,2},{8,12},{10,14},{12,8},{14,10},{16,20},{18,... | collective-permute-start | bytes 245768 | tf_op jit(solution)/shard_map/ppermute | solution.py:330
  15.1 0.3 collective-permute-start.2
  15.4 0.0 copy-done.7
  15.4 0.0 collective-permute-done.11
  15.5 0.0 copy-start.6
  15.5 1.7 %collective-permute-start.12 = (bf16[256,512]{1,0:T(8,128)(2,1)S(1)}, bf16[256,512]{1,0:T(8,128)(2,1)S(1)}, u32[]{:S(2)}, u32[]{:S(2)}) collective-permute-start(bf16[256,512]{1,0:T(8,128)(2,1)S(1)} %pad_maximum_fusion), channel_id=1, source_target_pairs={{0,4},{2,6},{4,0},{6,2},{8,12},{10,14},{12,8},{14,10},{16,20},{18,... | collective-permute-start | bytes 786440 | tf_op jit(solution)/shard_map/ppermute | solution.py:312
  17.2 0.0 copy-done.3
  17.2 0.0 copy-done.1
  17.2 0.0 copy-done.6
  17.2 0.9 %shard_map.76 = (f32[512,512]{1,0:T(8,128)S(1)}, f32[512,128]{1,0:T(8,128)S(1)}) custom-call(f32[8,128]{1,0:T(8,128)S(1)} %get-tuple-element.22.gates_ref, f32[4,128]{1,0:T(4,128)S(1)} %bitcast.5, bf16[512,256]{1,0:T(8,128)(2,1)S(1)} %copy-done.3, bf16[512,256]{1,0:T(8,128)(2,1)S(1)} %copy-done.2, bf16[512,512]{1,0:T(8,128)(2,1)S(1)} %copy-done.1), custom_call_target="tpu_custom_call" | custom-call | flops 402653184 | bytes 2097152 | tf_op jit(solution)/shard_map/pallas_call | solution.py:282
  18.1 0.0 collective-permute-done.refs_1_
  18.1 2.5 %collective-permute-done.1.refs_2_ = bf16[80,512]{1,0:T(8,128)(2,1)S(1)} collective-permute-done((bf16[80,512]{1,0:T(8,128)(2,1)S(1)}, bf16[80,512]{1,0:T(8,128)(2,1)S(1)}, u32[]{:S(2)}, u32[]{:S(2)}) %collective-permute-start.1) | collective-permute-done | bytes 81952 | tf_op jit(solution)/shard_map/ppermute | solution.py:330
  20.6 0.0 collective-permute-done.2.refs_3_
  20.6 0.1 shard_map.74
  20.7 1.4 %collective-permute-start.3 = (bf16[80,512]{1,0:T(8,128)(2,1)S(1)}, bf16[80,512]{1,0:T(8,128)(2,1)S(1)}, u32[]{:S(2)}, u32[]{:S(2)}) collective-permute-start(bf16[80,512]{1,0:T(8,128)(2,1)S(1)} %shard_map.74), channel_id=1, source_target_pairs={{0,8},{2,10},{4,12},{6,14},{8,0},{10,2},{12,4},{14,6},{16,24},{18,... | collective-permute-start | bytes 245768 | tf_op jit(solution)/shard_map/ppermute | solution.py:342
  22.2 2.4 %collective-permute-start.4 = (bf16[80,512]{1,0:T(8,128)(2,1)S(1)}, bf16[80,512]{1,0:T(8,128)(2,1)S(1)}, u32[]{:S(2)}, u32[]{:S(2)}) collective-permute-start(bf16[80,512]{1,0:T(8,128)(2,1)S(1)} %shard_map.74), channel_id=1, source_target_pairs={{0,16},{2,18},{4,20},{6,22},{8,24},{10,26},{12,28},{14,30},{16,0},... | collective-permute-start | bytes 245768 | tf_op jit(solution)/shard_map/ppermute | solution.py:342
  24.6 0.9 %collective-permute-start.5 = (bf16[80,512]{1,0:T(8,128)(2,1)S(1)}, bf16[80,512]{1,0:T(8,128)(2,1)S(1)}, u32[]{:S(2)}, u32[]{:S(2)}) collective-permute-start(bf16[80,512]{1,0:T(8,128)(2,1)S(1)} %shard_map.74), channel_id=1, source_target_pairs={{0,24},{2,26},{4,28},{6,30},{8,16},{10,18},{12,20},{14,22},{16,8},... | collective-permute-start | bytes 245768 | tf_op jit(solution)/shard_map/ppermute | solution.py:342
  25.5 0.0 collective-permute-done.3.refs_4_
  25.5 2.6 %collective-permute-done.4.refs_5_ = bf16[80,512]{1,0:T(8,128)(2,1)S(1)} collective-permute-done((bf16[80,512]{1,0:T(8,128)(2,1)S(1)}, bf16[80,512]{1,0:T(8,128)(2,1)S(1)}, u32[]{:S(2)}, u32[]{:S(2)}) %collective-permute-start.4) | collective-permute-done | bytes 81952 | tf_op jit(solution)/shard_map/ppermute | solution.py:342
  28.0 2.8 %collective-permute-done.5.refs_6_ = bf16[80,512]{1,0:T(8,128)(2,1)S(1)} collective-permute-done((bf16[80,512]{1,0:T(8,128)(2,1)S(1)}, bf16[80,512]{1,0:T(8,128)(2,1)S(1)}, u32[]{:S(2)}, u32[]{:S(2)}) %collective-permute-start.5) | collective-permute-done | bytes 81952 | tf_op jit(solution)/shard_map/ppermute | solution.py:342
  30.8 0.5 shard_map.75
  31.3 0.5 collective-permute-start.6
  31.8 1.0 %collective-permute-start.7 = (bf16[64,512]{1,0:T(8,128)(2,1)S(1)}, bf16[64,512]{1,0:T(8,128)(2,1)S(1)}, u32[]{:S(2)}, u32[]{:S(2)}) collective-permute-start(bf16[64,512]{1,0:T(8,128)(2,1)S(1)} %get-tuple-element.27), channel_id=1, source_target_pairs={{0,4},{2,6},{4,0},{6,2},{8,12},{10,14},{12,8},{14,10},{16,20},{18,... | collective-permute-start | bytes 196616 | tf_op jit(solution)/shard_map/ppermute | solution.py:350
  32.9 2.0 %collective-permute-start.8 = (bf16[64,512]{1,0:T(8,128)(2,1)S(1)}, bf16[64,512]{1,0:T(8,128)(2,1)S(1)}, u32[]{:S(2)}, u32[]{:S(2)}) collective-permute-start(bf16[64,512]{1,0:T(8,128)(2,1)S(1)} %get-tuple-element.28), channel_id=1, source_target_pairs={{0,6},{2,4},{4,2},{6,0},{8,14},{10,12},{12,10},{14,8},{16,22},{18,... | collective-permute-start | bytes 196616 | tf_op jit(solution)/shard_map/ppermute | solution.py:350
  34.9 0.8 %collective-permute-done.6.rest_1_ = bf16[64,512]{1,0:T(8,128)(2,1)S(1)} collective-permute-done((bf16[64,512]{1,0:T(8,128)(2,1)S(1)}, bf16[64,512]{1,0:T(8,128)(2,1)S(1)}, u32[]{:S(2)}, u32[]{:S(2)}) %collective-permute-start.6) | collective-permute-done | bytes 65568 | tf_op jit(solution)/shard_map/ppermute | solution.py:350
  35.6 0.4 collective-permute-done.7.rest_2_
  36.1 1.9 %collective-permute-done.8.rest_3_ = bf16[64,512]{1,0:T(8,128)(2,1)S(1)} collective-permute-done((bf16[64,512]{1,0:T(8,128)(2,1)S(1)}, bf16[64,512]{1,0:T(8,128)(2,1)S(1)}, u32[]{:S(2)}, u32[]{:S(2)}) %collective-permute-start.8) | collective-permute-done | bytes 65568 | tf_op jit(solution)/shard_map/ppermute | solution.py:350
  38.0 1.7 %shard_map.77.refs_0_ = bf16[512,512]{1,0:T(8,128)(2,1)S(1)} custom-call(f32[8,512]{1,0:T(8,128)S(1)} %get-tuple-element.21.state_ref, bf16[512,256]{1,0:T(8,128)(2,1)S(1)} %copy-done.3, f32[512,512]{1,0:T(8,128)S(1)} %get-tuple-element.23.num_ref, f32[512,128]{1,0:T(8,128)S(1)} %get-tuple-element.24.cols_ref, ...), custom_call_target="tpu_custom_call" | custom-call | flops 134217728 | tf_op jit(solution)/shard_map/pallas_call | solution.py:282
  39.8 0.1 collective-permute-start.9
  39.9 0.0 collective-permute-done.12
  39.9 1.7 %collective-permute-start.13 = (bf16[512,512]{1,0:T(8,128)(2,1)S(1)}, bf16[512,512]{1,0:T(8,128)(2,1)S(1)}, u32[]{:S(2)}, u32[]{:S(2)}) collective-permute-start(bf16[512,512]{1,0:T(8,128)(2,1)S(1)} %constant_dynamic-update-slice_fusion.refs_2_), channel_id=1, source_target_pairs={{0,2},{2,0},{4,6},{6,4},{8,10},{10,8},{12,14},{14,12},{16,18},{18,... | collective-permute-start | bytes 1572872 | tf_op jit(solution)/shard_map/ppermute | solution.py:312
  41.6 0.2 collective-permute-done.9.refs_1_
  41.8 12.5 %collective-permute-done.13.refs_3_ = bf16[512,512]{1,0:T(8,128)(2,1)S(1)} collective-permute-done((bf16[512,512]{1,0:T(8,128)(2,1)S(1)}, bf16[512,512]{1,0:T(8,128)(2,1)S(1)}, u32[]{:S(2)}, u32[]{:S(2)}) %collective-permute-start.13) | collective-permute-done | bytes 524320 | tf_op jit(solution)/shard_map/ppermute | solution.py:312
  54.3 1.6 %shard_map.78 = bf16[512,512]{1,0:T(8,128)(2,1)} custom-call(bf16[512,512]{1,0:T(8,128)(2,1)S(1)} %shard_map.77.refs_0_, bf16[512,512]{1,0:T(8,128)(2,1)S(1)} %collective-permute-done.9.refs_1_, bf16[512,512]{1,0:T(8,128)(2,1)S(1)} %constant_dynamic-update-slice_fusion.refs_2_, bf16[512,512]{1,0:T(8,128)(2,1)S(1)} %collective-permute-done.13.refs_3_), custom_call_target="tpu_custom_call" | custom-call | tf_op jit(solution)/shard_map/pallas_call | solution.py:282
  (5 shorter events, 0.1 us)
Async XLA Ops:
  0.0 9.5 %copy-start.2 = (bf16[512,256]{1,0:T(8,128)(2,1)S(1)}, bf16[512,256]{1,0:T(8,128)(2,1)}, u32[]{:S(2)}) copy-start(bf16[512,256]{1,0:T(8,128)(2,1)} %keys_ref.3) | copy-start | bytes 786436
  0.0 7.9 %collective-permute-start.10 = (bf16[64,512]{1,0:T(8,128)(2,1)}, bf16[64,512]{1,0:T(8,128)(2,1)S(1)}, u32[]{:S(2)}, u32[]{:S(2)}) collective-permute-start(bf16[64,512]{1,0:T(8,128)(2,1)} %param.13), channel_id=1, source_target_pairs={{0,16},{2,18},{4,20},{6,22},{8,24},{10,26},{12,28},{14,30},{16,0},... | collective-permute-start | bytes 196616 | tf_op jit(solution)/shard_map/ppermute | solution.py:312
  8.7 0.8 %copy-start.4 = (f32[512,1]{0,1:T(1,128)S(1)}, f32[512,1]{0,1:T(1,128)}, u32[]{:S(2)}) copy-start(f32[512,1]{0,1:T(1,128)} %param.11) | copy-start | bytes 6148
  8.8 6.7 %collective-permute-start.11 = (bf16[128,512]{1,0:T(8,128)(2,1)S(1)}, bf16[128,512]{1,0:T(8,128)(2,1)S(1)}, u32[]{:S(2)}, u32[]{:S(2)}) collective-permute-start(bf16[128,512]{1,0:T(8,128)(2,1)S(1)} %pad_maximum_fusion.1), channel_id=1, source_target_pairs={{0,8},{2,10},{4,12},{6,14},{8,0},{10,2},{12,4},{14,6},{16,24},{18,... | collective-permute-start | bytes 393224 | tf_op jit(solution)/shard_map/ppermute | solution.py:312
  9.5 1.0 %copy-start = (bf16[512,512]{1,0:T(8,128)(2,1)S(1)}, bf16[512,512]{1,0:T(8,128)(2,1)}, u32[]{:S(2)}) copy-start(bf16[512,512]{1,0:T(8,128)(2,1)} %values_ref.3) | copy-start | bytes 1572868
  10.6 0.7 %copy-start.5 = (f32[512,1]{0,1:T(1,128)S(1)}, f32[512,1]{0,1:T(1,128)}, u32[]{:S(2)}) copy-start(f32[512,1]{0,1:T(1,128)} %param.10) | copy-start | bytes 6148
  11.2 4.2 %copy-start.7 = (bf16[64,512]{1,0:T(8,128)(2,1)S(1)}, bf16[64,512]{1,0:T(8,128)(2,1)}, u32[]{:S(2)}) copy-start(bf16[64,512]{1,0:T(8,128)(2,1)} %param.13) | copy-start | bytes 196612
  11.2 6.0 %copy-start.3 = (bf16[512,256]{1,0:T(8,128)(2,1)S(1)}, bf16[512,256]{1,0:T(8,128)(2,1)}, u32[]{:S(2)}) copy-start(bf16[512,256]{1,0:T(8,128)(2,1)} %queries_ref.3) | copy-start | bytes 786436
  11.9 5.4 %copy-start.1 = (bf16[512,512]{1,0:T(8,128)(2,1)S(1)}, bf16[512,512]{1,0:T(8,128)(2,1)}, u32[]{:S(2)}) copy-start(bf16[512,512]{1,0:T(8,128)(2,1)} %values_ref.3) | copy-start | bytes 1572868
  11.9 6.2 %collective-permute-start = (bf16[80,512]{1,0:T(8,128)(2,1)S(1)}, bf16[80,512]{1,0:T(8,128)(2,1)S(1)}, u32[]{:S(2)}, u32[]{:S(2)}) collective-permute-start(bf16[80,512]{1,0:T(8,128)(2,1)S(1)} %get-tuple-element.18), channel_id=1, source_target_pairs={{0,2},{2,0},{4,6},{6,4},{8,10},{10,8},{12,14},{14,12},{16,18},{18,... | collective-permute-start | bytes 245768 | tf_op jit(solution)/shard_map/ppermute | solution.py:330
  13.6 7.0 %collective-permute-start.1 = (bf16[80,512]{1,0:T(8,128)(2,1)S(1)}, bf16[80,512]{1,0:T(8,128)(2,1)S(1)}, u32[]{:S(2)}, u32[]{:S(2)}) collective-permute-start(bf16[80,512]{1,0:T(8,128)(2,1)S(1)} %get-tuple-element.19), channel_id=1, source_target_pairs={{0,4},{2,6},{4,0},{6,2},{8,12},{10,14},{12,8},{14,10},{16,20},{18,... | collective-permute-start | bytes 245768 | tf_op jit(solution)/shard_map/ppermute | solution.py:330
  15.1 5.5 %collective-permute-start.2 = (bf16[80,512]{1,0:T(8,128)(2,1)S(1)}, bf16[80,512]{1,0:T(8,128)(2,1)S(1)}, u32[]{:S(2)}, u32[]{:S(2)}) collective-permute-start(bf16[80,512]{1,0:T(8,128)(2,1)S(1)} %get-tuple-element.20), channel_id=1, source_target_pairs={{0,6},{2,4},{4,2},{6,0},{8,14},{10,12},{12,10},{14,8},{16,22},{18,... | collective-permute-start | bytes 245768 | tf_op jit(solution)/shard_map/ppermute | solution.py:330
  15.5 1.7 %copy-start.6 = (f32[512,1]{0,1:T(1,128)S(1)}, f32[512,1]{0,1:T(1,128)}, u32[]{:S(2)}) copy-start(f32[512,1]{0,1:T(1,128)} %param.12) | copy-start | bytes 6148
  15.5 24.4 %collective-permute-start.12 = (bf16[256,512]{1,0:T(8,128)(2,1)S(1)}, bf16[256,512]{1,0:T(8,128)(2,1)S(1)}, u32[]{:S(2)}, u32[]{:S(2)}) collective-permute-start(bf16[256,512]{1,0:T(8,128)(2,1)S(1)} %pad_maximum_fusion), channel_id=1, source_target_pairs={{0,4},{2,6},{4,0},{6,2},{8,12},{10,14},{12,8},{14,10},{16,20},{18,... | collective-permute-start | bytes 786440 | tf_op jit(solution)/shard_map/ppermute | solution.py:312
  20.7 4.7 %collective-permute-start.3 = (bf16[80,512]{1,0:T(8,128)(2,1)S(1)}, bf16[80,512]{1,0:T(8,128)(2,1)S(1)}, u32[]{:S(2)}, u32[]{:S(2)}) collective-permute-start(bf16[80,512]{1,0:T(8,128)(2,1)S(1)} %shard_map.74), channel_id=1, source_target_pairs={{0,8},{2,10},{4,12},{6,14},{8,0},{10,2},{12,4},{14,6},{16,24},{18,... | collective-permute-start | bytes 245768 | tf_op jit(solution)/shard_map/ppermute | solution.py:342
  22.2 5.9 %collective-permute-start.4 = (bf16[80,512]{1,0:T(8,128)(2,1)S(1)}, bf16[80,512]{1,0:T(8,128)(2,1)S(1)}, u32[]{:S(2)}, u32[]{:S(2)}) collective-permute-start(bf16[80,512]{1,0:T(8,128)(2,1)S(1)} %shard_map.74), channel_id=1, source_target_pairs={{0,16},{2,18},{4,20},{6,22},{8,24},{10,26},{12,28},{14,30},{16,0},... | collective-permute-start | bytes 245768 | tf_op jit(solution)/shard_map/ppermute | solution.py:342
  24.6 6.2 %collective-permute-start.5 = (bf16[80,512]{1,0:T(8,128)(2,1)S(1)}, bf16[80,512]{1,0:T(8,128)(2,1)S(1)}, u32[]{:S(2)}, u32[]{:S(2)}) collective-permute-start(bf16[80,512]{1,0:T(8,128)(2,1)S(1)} %shard_map.74), channel_id=1, source_target_pairs={{0,24},{2,26},{4,28},{6,30},{8,16},{10,18},{12,20},{14,22},{16,8},... | collective-permute-start | bytes 245768 | tf_op jit(solution)/shard_map/ppermute | solution.py:342
  31.3 4.3 %collective-permute-start.6 = (bf16[64,512]{1,0:T(8,128)(2,1)S(1)}, bf16[64,512]{1,0:T(8,128)(2,1)S(1)}, u32[]{:S(2)}, u32[]{:S(2)}) collective-permute-start(bf16[64,512]{1,0:T(8,128)(2,1)S(1)} %get-tuple-element.26), channel_id=1, source_target_pairs={{0,2},{2,0},{4,6},{6,4},{8,10},{10,8},{12,14},{14,12},{16,18},{18,... | collective-permute-start | bytes 196616 | tf_op jit(solution)/shard_map/ppermute | solution.py:350
  31.8 4.3 %collective-permute-start.7 = (bf16[64,512]{1,0:T(8,128)(2,1)S(1)}, bf16[64,512]{1,0:T(8,128)(2,1)S(1)}, u32[]{:S(2)}, u32[]{:S(2)}) collective-permute-start(bf16[64,512]{1,0:T(8,128)(2,1)S(1)} %get-tuple-element.27), channel_id=1, source_target_pairs={{0,4},{2,6},{4,0},{6,2},{8,12},{10,14},{12,8},{14,10},{16,20},{18,... | collective-permute-start | bytes 196616 | tf_op jit(solution)/shard_map/ppermute | solution.py:350
  32.9 5.2 %collective-permute-start.8 = (bf16[64,512]{1,0:T(8,128)(2,1)S(1)}, bf16[64,512]{1,0:T(8,128)(2,1)S(1)}, u32[]{:S(2)}, u32[]{:S(2)}) collective-permute-start(bf16[64,512]{1,0:T(8,128)(2,1)S(1)} %get-tuple-element.28), channel_id=1, source_target_pairs={{0,6},{2,4},{4,2},{6,0},{8,14},{10,12},{12,10},{14,8},{16,22},{18,... | collective-permute-start | bytes 196616 | tf_op jit(solution)/shard_map/ppermute | solution.py:350
  39.8 2.0 %collective-permute-start.9 = (bf16[512,512]{1,0:T(8,128)(2,1)S(1)}, bf16[512,512]{1,0:T(8,128)(2,1)S(1)}, u32[]{:S(2)}, u32[]{:S(2)}) collective-permute-start(bf16[512,512]{1,0:T(8,128)(2,1)S(1)} %shard_map.77.refs_0_), channel_id=1, source_target_pairs={{0,1},{1,0},{2,3},{3,2},{4,5},{5,4},{6,7},{7,6},{8,9},{9,8},{10,11... | collective-permute-start | bytes 1572872 | tf_op jit(solution)/shard_map/ppermute | solution.py:360
  39.9 14.4 %collective-permute-start.13 = (bf16[512,512]{1,0:T(8,128)(2,1)S(1)}, bf16[512,512]{1,0:T(8,128)(2,1)S(1)}, u32[]{:S(2)}, u32[]{:S(2)}) collective-permute-start(bf16[512,512]{1,0:T(8,128)(2,1)S(1)} %constant_dynamic-update-slice_fusion.refs_2_), channel_id=1, source_target_pairs={{0,2},{2,0},{4,6},{6,4},{8,10},{10,8},{12,14},{14,12},{16,18},{18,... | collective-permute-start | bytes 1572872 | tf_op jit(solution)/shard_map/ppermute | solution.py:312

commit v2 on v1

v2 whole, which is shorter than its diff:
```python
import functools

import jax
import jax.numpy as jnp
from jax import lax
from jax.experimental import pallas as pl
from jax.experimental.pallas import tpu as pltpu
from jax.sharding import PartitionSpec as P

TILE = 16
LANES = 128
NEG = -1e30


def split_groups(n):
    inner = max(a for a in range(1, n + 1) if n % a == 0 and a * a <= n)
    return inner, n // inner


def is_pow2(n):
    return n & (n - 1) == 0


def source(i, k, n):
    return i ^ k if is_pow2(n) else (i + k) % n


def target(i, k, n):
    return i ^ k if is_pow2(n) else (i + n - k) % n


def inner_pairs(n, inner, k):
    return [(j, j - j % inner + target(j % inner, k, inner)) for j in range(n)]


def outer_pairs(n, inner, k):
    outer = n // inner
    return [(j, target(j // inner, k, outer) * inner + j % inner) for j in range(n)]


def pieces3(x):
    hi = x.astype(jnp.bfloat16)
    rest = x - hi.astype(jnp.float32)
    mid = rest.astype(jnp.bfloat16)
    low = (rest - mid.astype(jnp.float32)).astype(jnp.bfloat16)
    return hi, mid, low


def lane_blocks(x):
    return [x[:, i : i + LANES] for i in range(0, x.shape[1], LANES)]


def rows_for(width_k):
    rows = 3 * (width_k // LANES + 2)
    return rows + -rows % TILE


def write_tail(ref, at, norm, top, decay):
    wide = jnp.concatenate([norm] + [jnp.broadcast_to(x, (1, LANES)) for x in (top, decay)], axis=0)
    rows = [p.astype(jnp.float32) for p in pieces3(wide)]
    count = ref.shape[0] - at - 3 * wide.shape[0]
    if count:
        rows.append(jnp.zeros((count, LANES), jnp.float32))
    ref[at:, :] = jnp.concatenate(rows, axis=0).astype(jnp.bfloat16)


def read_tail(ref, at, width_k):
    tail = ref[at:, :].astype(jnp.float32)
    n = width_k // LANES
    tail = tail[0 : n + 2] + tail[n + 2 : 2 * n + 4] + tail[2 * n + 4 : 3 * n + 6]
    return tail[0:n], tail[n : n + 1], tail[n + 1 : n + 2]


def read_tails(refs, width_k):
    at = refs[0].shape[0] - rows_for(width_k)
    return at, zip(*[read_tail(r, at, width_k) for r in refs])


def summary_kernel(inner, *refs):
    given, gates_ref, outs = refs[:4], refs[4], refs[5 : 5 + inner]
    memory, sems = refs[5 + inner], refs[-1]
    held = forget_ref, input_ref, keys_ref, values_ref = refs[6 + inner : -1]
    copies = [
        pltpu.make_async_copy(src, dst, sems.at[i]) for i, (src, dst) in enumerate(zip(given, held))
    ]
    for copy in copies:
        copy.start()
    copies[0].wait()
    copies[1].wait()
    member = lax.rem(lax.axis_index("ctx"), inner)
    rows = forget_ref.shape[0]
    forget = forget_ref[...]
    log_keep = jnp.minimum(forget, 0.0) - jnp.log1p(jnp.exp(-jnp.abs(forget)))
    tri = lax.broadcasted_iota(jnp.int32, (LANES, LANES), 0) <= lax.broadcasted_iota(
        jnp.int32, (LANES, LANES), 1
    )
    parts = jnp.concatenate([p.astype(jnp.float32) for p in pieces3(log_keep)], axis=0)
    sums = jnp.dot(
        parts.astype(jnp.bfloat16),
        tri.astype(jnp.bfloat16),
        preferred_element_type=jnp.float32,
    )
    inside = sums[:rows] + sums[rows : 2 * rows] + sums[2 * rows : 3 * rows]
    base = jnp.zeros((1, 1), jnp.float32)
    cum = []
    for r in range(rows):
        row = inside[r : r + 1]
        cum.append(row + base)
        base = base + row[:, LANES - 1 :]
    cum_decay = jnp.concatenate(cum, axis=0)
    gain = input_ref[...] - cum_decay
    top_gain = jnp.max(jnp.max(gain, axis=1, keepdims=True), axis=0, keepdims=True)
    weight = jnp.exp(gain - top_gain)
    gates_ref[0:rows, :] = gain
    gates_ref[rows : 2 * rows, :] = cum_decay
    along = jnp.concatenate([weight[r : r + 1] for r in range(rows)], axis=1)
    three = [p.astype(jnp.float32) for p in pieces3(along)]
    three.append(jnp.zeros((TILE - 3, along.shape[1]), jnp.float32))
    three = jnp.concatenate(three, axis=0).astype(jnp.bfloat16)
    copies[2].wait()
    keys = keys_ref[...]
    scaled = (keys.astype(jnp.float32).T * along).astype(jnp.bfloat16)
    norms = jnp.dot(three, keys, preferred_element_type=jnp.float32)
    norm = jnp.concatenate(lane_blocks(norms[0:1] + norms[1:2] + norms[2:3]), axis=0)
    copies[3].wait()
    memory[...] = jnp.dot(scaled, values_ref[...], preferred_element_type=jnp.float32)
    piece = memory.shape[0] // inner
    for k, out_ref in enumerate(outs):
        start = pl.multiple_of(target(member, k, inner) * piece, piece)
        wide = memory[pl.ds(start, piece), :].astype(jnp.bfloat16)
        for i, block in enumerate(lane_blocks(wide)):
            out_ref[i * piece : (i + 1) * piece, :] = block
        write_tail(out_ref, wide.size // LANES, norm, base + top_gain, base)


def chain_logs(where, tops, decays, end):
    logs = []
    for k in range(len(where)):
        log = tops[k]
        for o in range(len(where)):
            if o != k:
                between = jnp.logical_and(where[o] > where[k], where[o] < end)
                log = log + jnp.where(between, decays[o], 0.0)
        logs.append(jnp.where(where[k] < end, log, NEG))
    return logs


def chain_sum(where, logs, top, end, refs, at, norms):
    total, norm = 0.0, 0.0
    for k in range(len(where)):
        weight = jnp.where(where[k] < end, jnp.exp(logs[k] - top), 0.0)
        total = total + weight * refs[k][0:at, :].astype(jnp.float32)
        norm = norm + weight * norms[k]
    return total, norm


def group_total_kernel(inner, width_k, *refs):
    ins, out_ref = refs[:-1], refs[-1]
    member = lax.rem(lax.axis_index("ctx"), inner)
    where = [source(member, k, inner) for k in range(inner)]
    at, (norms, tops, decays) = read_tails(ins, width_k)
    logs = chain_logs(where, tops, decays, inner)
    top = functools.reduce(jnp.maximum, logs)
    total, norm = chain_sum(where, logs, top, inner, ins, at, norms)
    out_ref[0:at, :] = total.astype(jnp.bfloat16)
    write_tail(out_ref, at, norm, top, functools.reduce(jnp.add, decays))


def near_kernel(inner, width_k, *refs):
    ins, outs, stats_ref = refs[:inner], refs[inner:-1], refs[-1]
    member = lax.rem(lax.axis_index("ctx"), inner)
    where = [source(member, k, inner) for k in range(inner)]
    at, (norms, tops, decays) = read_tails(ins, width_k)
    for t in range(inner):
        end = target(member, t, inner)
        logs = chain_logs(where, tops, decays, end)
        top = functools.reduce(jnp.maximum, logs)
        total, norm = chain_sum(where, logs, top, end, ins, at, norms)
        outs[t][...] = total
        decay = 0.0
        for k in range(inner):
            decay = decay + jnp.where(where[k] < end, decays[k], 0.0)
        pad = jnp.zeros((8 - norm.shape[0] % 8 - 2, LANES), jnp.float32)
        stats_ref[t, :, :] = jnp.concatenate([top, decay, norm, pad], axis=0)


def far_kernel(inner, outer, width_k, stats_ref, *refs):
    totals, nears = refs[: outer - 1], refs[outer - 1 : outer - 1 + inner]
    outs, state_ref = refs[outer - 1 + inner : -1], refs[-1]
    group = lax.div(lax.axis_index("ctx"), inner)
    where = [source(group, k, outer) for k in range(1, outer)]
    at, (norms, tops, decays) = read_tails(totals, width_k)
    logs = chain_logs(where, tops, decays, group)
    far_top = functools.reduce(jnp.maximum, logs)
    far, far_norm = chain_sum(where, logs, far_top, group, totals, at, norms)
    n = width_k // LANES
    for t in range(inner):
        stats = stats_ref[t, :, :]
        far_log = far_top + stats[1:2]
        top = jnp.maximum(stats[0:1], far_log)
        w_near, w_far = jnp.exp(stats[0:1] - top), jnp.exp(far_log - top)
        outs[t][...] = (w_far * far + w_near * nears[t][...]).astype(jnp.bfloat16)
        if t == 0:
            norm = w_far * far_norm + w_near * stats[2 : 2 + n]
            pad = jnp.zeros((state_ref.shape[0] - 1 - n, LANES), jnp.float32)
            state_ref[...] = jnp.concatenate([top, norm, pad], axis=0)


def inside_kernel(gates_ref, output_ref, queries_ref, keys_ref, values_ref, num_ref, cols_ref):
    rows = output_ref.shape[0]
    scale = queries_ref.shape[1] ** (-0.5)
    down = lax.broadcasted_iota(jnp.int32, (LANES, LANES), 0)
    across = lax.broadcasted_iota(jnp.int32, (LANES, LANES), 1)
    causal, same = down >= across, down == across
    lane = lax.broadcasted_iota(jnp.int32, (LANES, LANES), 1)
    gain = gates_ref[0:rows, :]
    cum_decay = gates_ref[rows : 2 * rows, :]
    open_gate = jax.nn.sigmoid(output_ref[...])

    def column(row):
        return jnp.sum(jnp.where(same, row, 0.0), axis=1, keepdims=True)

    before = jnp.full((1, 1), NEG, jnp.float32)
    for i in range(rows):
        here = slice(i * LANES, (i + 1) * LANES)
        a_row = gain[i : i + 1]
        peak = jnp.max(jnp.where(causal, a_row, NEG), axis=1, keepdims=True)
        peak = jnp.maximum(peak, before)
        before = jnp.maximum(before, jnp.max(a_row, axis=1, keepdims=True))
        width = (i + 1) * LANES
        scores = lax.dot_general(
            queries_ref[here, :],
            keys_ref[0:width, :],
            (((1,), (1,)), ((), ())),
            preferred_element_type=jnp.float32,
        )
        parts, den = [], 0.0
        for j in range(i + 1):
            diff = gain[j : j + 1] - peak
            if j == i:
                diff = jnp.where(causal, diff, NEG)
            part = jnp.exp(diff) * (scores[:, j * LANES : (j + 1) * LANES] * scale)
            den = den + part
            parts.append(part.astype(jnp.bfloat16))
        weighted = parts[0] if i == 0 else jnp.concatenate(parts, axis=1)
        den = jnp.sum(den, axis=1, keepdims=True)
        num_ref[here, :] = jnp.dot(
            weighted, values_ref[0:width, :], preferred_element_type=jnp.float32
        )
        cols = jnp.where(lane == 0, den, peak)
        cols = jnp.where(lane == 2, column(cum_decay[i : i + 1]), cols)
        cols_ref[here, :] = jnp.where(lane == 3, column(open_gate[i : i + 1]), cols)


def rescale_kernel(state_ref, queries_ref, num_ref, cols_ref, done_ref, lift_ref):
    width = queries_ref.shape[1]
    n = width // LANES
    scale = width ** (-0.5)
    top_prev = state_ref[0:1, 0:1]
    norm = jnp.concatenate([state_ref[1 + i : 2 + i, :] for i in range(n)], axis=1)
    for i in range(queries_ref.shape[0] // LANES):
        here = slice(i * LANES, (i + 1) * LANES)
        den_out = jnp.sum(queries_ref[here, :].astype(jnp.float32) * norm, axis=1, keepdims=True)
        cols = cols_ref[here, :]
        den_in, peak = cols[:, 0:1], cols[:, 1:2]
        cum_decay, open_gate = cols[:, 2:3], cols[:, 3:4]
        top = jnp.maximum(peak, top_prev)
        keep, lift = jnp.exp(peak - top), jnp.exp(top_prev - top) * scale
        den = jnp.abs(keep * den_in + lift * den_out)
        ratio = open_gate / jnp.maximum(den, jnp.exp(-(cum_decay + top)))
        done_ref[here, :] = (keep * ratio) * num_ref[here, :]
        lift_ref[here, :] = jnp.broadcast_to(lift * ratio, (LANES, LANES))


def output_kernel(inner, queries_ref, done_ref, lift_ref, *rest):
    pieces, out_ref, memory = rest[:inner], rest[inner], rest[inner + 1]
    member = lax.rem(lax.axis_index("ctx"), inner)
    piece = memory.shape[0] // inner
    for k in range(inner):
        start = pl.multiple_of(source(member, k, inner) * piece, piece)
        for i in range(memory.shape[1] // LANES):
            memory[pl.ds(start, piece), i * LANES : (i + 1) * LANES] = pieces[k][
                i * piece : (i + 1) * piece, :
            ]
    for i in range(queries_ref.shape[0] // LANES):
        here = slice(i * LANES, (i + 1) * LANES)
        num_out = jnp.dot(queries_ref[here, :], memory[...], preferred_element_type=jnp.float32)
        gated = done_ref[here, :] + lift_ref[here, 0:1] * num_out
        out_ref[here, :] = gated.astype(jnp.bfloat16)


def own_kernel(heads, orders, rows, gated_ref, *refs):
    bufs, (part_ref, other_ref, weights) = refs[:-3], refs[-3:]
    place, head = lax.axis_index("ctx"), lax.axis_index("head")
    at = 0
    for buf in bufs:
        for s in range(buf.shape[0] // rows):
            even, odd = (order[at] for order in orders)
            block = place ^ (even if even == odd else jnp.where(head % 2 == 0, even, odd))
            start = pl.multiple_of(block * rows, rows)
            weights[pl.ds(start, rows), :] = buf[s * rows : (s + 1) * rows, :]
            at += 1
    width = gated_ref.shape[1]
    for k in range(1, heads):
        start = pl.multiple_of(source(head, k, heads) * width, width)
        other_ref[(k - 1) * width : k * width, :] = weights[pl.ds(start, width), :]
    mine = weights[pl.ds(pl.multiple_of(head * width, width), width), :]
    part_ref[...] = jnp.dot(gated_ref[...], mine, preferred_element_type=jnp.float32)


def others_kernel(part_ref, other_ref, *refs):
    gated, out_ref = refs[:-1], refs[-1]
    total, at = part_ref[...], 0
    for g in gated:
        weights = other_ref[at : at + g.shape[1], :]
        total = total + jnp.dot(g[...], weights, preferred_element_type=jnp.float32)
        at += g.shape[1]
    out_ref[...] = total.astype(jnp.bfloat16)


def join_kernel(a_ref, b_ref, out_ref):
    rows = a_ref.shape[0]
    out_ref[0:rows, :] = a_ref[...]
    out_ref[rows:, :] = b_ref[...]


def call(kernel, out_shape, args, scratch=(), micros=1.0, after=(), plain=(), mib=24):
    skip = len(after)
    anywhere, vmem = pl.BlockSpec(memory_space=pl.ANY), pl.BlockSpec(memory_space=pltpu.VMEM)
    hbm = pl.BlockSpec(memory_space=pltpu.HBM)
    return pl.pallas_call(
        lambda *refs: kernel(*refs[skip:]),
        out_shape=out_shape,
        in_specs=[anywhere] * skip + [hbm if i in plain else vmem for i in range(len(args))],
        out_specs=jax.tree.map(lambda _: vmem, out_shape),
        scratch_shapes=scratch,
        compiler_params=pltpu.CompilerParams(vmem_limit_bytes=mib * 2**20),
        cost_estimate=pl.CostEstimate(
            flops=int(micros * 1.1e9), bytes_accessed=int(micros * 3.7e6), transcendentals=0
        ),
    )(*after, *args)


def shape(dims, dtype):
    return jax.ShapeDtypeStruct(dims, dtype)


def join(pair, after=()):
    rows, width = pair[0].shape
    return call(join_kernel, shape((2 * rows, width), pair[0].dtype), pair, micros=0.5, after=after)


def doubling_steps(n_ctx):
    assert is_pow2(n_ctx) and n_ctx >= 4
    return [1 << b for b in reversed(range(2, n_ctx.bit_length() - 1))]


def local(n_ctx, n_head, queries, keys, values, input_pre, forget_pre, output_pre, w_out):
    tok, width_k = queries.shape
    width_v = values.shape[1]
    inner, outer = split_groups(n_ctx)
    piece = width_k // inner
    bf16, f32 = jnp.bfloat16, jnp.float32
    gate_rows = tok // LANES
    forget, gate_in, gate_out = (
        g.reshape(gate_rows, LANES) for g in (forget_pre, input_pre, output_pre)
    )

    steps = doubling_steps(n_ctx)
    w_bufs, order = [w_out], [0]

    def trade(held, even, odd):
        pairs = [
            (j * n_head + h, (j ^ (odd if h % 2 else even)) * n_head + h)
            for j in range(n_ctx)
            for h in range(n_head)
        ]
        return lax.ppermute(held, ("ctx", "head"), pairs)

    def gather_step(after):
        held = join(w_bufs, after) if len(w_bufs) > 1 else w_bufs[0]
        if steps:
            step = steps.pop(0)
            w_bufs[:] = [held, trade(held, step, step)]
            order.extend([x ^ step for x in order])
        else:
            first, second = trade(held, 2, 1), trade(held, 1, 2)
            w_bufs[:] = [held, first, second, trade(first, 1, 2)]
        return [held]

    gather_step([])
    memory_rows = piece * width_v // LANES
    message = shape((memory_rows + rows_for(width_k), LANES), bf16)
    gates, *sends = call(
        functools.partial(summary_kernel, inner),
        [shape((2 * gate_rows, LANES), f32)] + [message] * inner,
        (forget, gate_in, keys, values),
        [
            pltpu.VMEM((width_k, width_v), f32),
            *[pltpu.VMEM(x.shape, x.dtype) for x in (forget, gate_in, keys, values)],
            pltpu.SemaphoreType.DMA((4,)),
        ],
        micros=2.0,
        plain=(0, 1, 2, 3),
        mib=60,
    )
    ready = gather_step([gates])
    blocks = [sends[0]] + [
        lax.ppermute(sends[k], "ctx", inner_pairs(n_ctx, inner, k)) for k in range(1, inner)
    ]
    num_in, cols = call(
        inside_kernel,
        [shape((tok, width_v), f32), shape((tok, LANES), f32)],
        (gates, gate_out, queries, keys, values),
        micros=8.0,
        after=ready,
    )
    total = call(functools.partial(group_total_kernel, inner, width_k), message, blocks)
    while steps:
        gather_step([total])
    ready = gather_step([total])
    totals = [
        lax.ppermute(total, "ctx", outer_pairs(n_ctx, inner, k)) for k in range(1, outer)
    ]
    *nears, stats = call(
        functools.partial(near_kernel, inner, width_k),
        [shape((memory_rows, LANES), f32)] * inner + [shape((inner, 8, LANES), f32)],
        blocks,
        micros=0.3,
        after=[*ready, cols],
    )
    *prefixes, state = call(
        functools.partial(far_kernel, inner, outer, width_k),
        [shape((memory_rows, LANES), bf16)] * inner + [shape((8, LANES), f32)],
        (stats, *totals, *nears),
        micros=0.1,
        after=w_bufs[1:2],
    )
    parts = [prefixes[0]] + [
        lax.ppermute(prefixes[k], "ctx", inner_pairs(n_ctx, inner, k)) for k in range(1, inner)
    ]
    done, lift = call(
        rescale_kernel,
        [shape((tok, width_v), f32), shape((tok, LANES), f32)],
        (state, queries, num_in, cols),
        micros=8.0,
        after=w_bufs[1:4],
    )
    gated = call(
        functools.partial(output_kernel, inner),
        shape((tok, width_v), bf16),
        (queries, done, lift, *parts),
        [pltpu.VMEM((width_k, width_v), bf16)],
        micros=0.1,
    )
    others = [
        lax.ppermute(gated, "head", [(j, target(j, k, n_head)) for j in range(n_head)])
        for k in range(1, n_head)
    ]
    cols_out = w_out.shape[1]
    w_orders = [[x ^ s for s in (0, a, b, a ^ b) for x in order] for a, b in ((2, 1), (1, 2))]
    part, other_rows = call(
        functools.partial(own_kernel, n_head, w_orders, w_out.shape[0]),
        [shape((tok, cols_out), f32), shape(((n_head - 1) * width_v, cols_out), bf16)],
        (gated, *w_bufs),
        [pltpu.VMEM((n_ctx * w_out.shape[0], cols_out), bf16)],
        micros=2.0,
    )
    return call(
        others_kernel, shape((tok, cols_out), bf16), (part, other_rows, *others), micros=1.0
    )


def solution(mesh):
    spec = P("ctx", "head")
    return jax.shard_map(
        functools.partial(local, mesh.shape["ctx"], mesh.shape["head"]),
        mesh=mesh,
        in_specs=(spec,) * 7,
        out_specs=spec,
        check_vma=False,
    )
```

time: 56.1 us -> 37.1 us (0.66)
  waiting for transfers between devices: 27.6 us -> 6.8 us
  starting transfers between devices: 20.1 us -> 22.4 us
  Pallas kernels: 5.43 us -> 7.55 us
  local copies, waits for them, and re-layouts: 1.79 us -> 0.04 us
  other arithmetic: 0.87 us -> 0 us
    ppermute x4 -> x5, waiting for transfers between devices: 16.4 us -> 1.39 us  [trade(): return lax.ppermute(held, ('ctx', 'head'), pairs)]
    ppermute x3, waiting for transfers between devices: 5.37 us -> 0.01 us  [local(): lax.ppermute(total, 'ctx', outer_pairs(n_ctx, inner, k))]
    ppermute x4 -> x5, starting transfers between devices: 8.17 us -> 10.8 us  [trade(): return lax.ppermute(held, ('ctx', 'head'), pairs)]
    ppermute x3, waiting for transfers between devices: 3.14 us -> 0.81 us  [local(): lax.ppermute(prefixes[k], 'ctx', inner_pairs(n_ctx, inner, k))]
    pallas_call x6 -> x11, Pallas kernels: 5.43 us -> 7.55 us  [call(): pl.pallas_call(lambda *refs: kernel(*refs[skip:]), out_shape=out_shape, i...]
    unnamed x19 -> x14, local copies, waits for them, and re-layouts: 1.77 us -> 0.04 us
    ppermute x1, waiting for transfers between devices: 0.19 us -> 1.34 us  [local(): lax.ppermute(gated, 'head', [(j, target(j, k, n_head)) for j in range(n_h...]
    concatenate x2 -> x0, other arithmetic: 0.87 us -> none  [local(): w_held = jnp.concatenate(w_bufs, axis=0)]
  transfers between devices with their start and end apart: 14 -> 15, of which waited for: 9 -> 6; matrix products, arithmetic and copies ran while one was open for 0% -> 0% of each run, Pallas kernels for 7% -> 16%
where the time goes in v2:
time: 37.1 us; the launch traced here: 37 us
  starting transfers between devices  22.4 us (60%)
  Pallas kernels  7.55 us (20%)
  waiting for transfers between devices  6.8 us (18%)
    ppermute x5, starting transfers between devices, trade(): return lax.ppermute(held, ('ctx', 'head'), pairs)  10.8 us
    pallas_call x11, Pallas kernels, call(): pl.pallas_call(lambda *refs: kernel(*refs[skip:]), out_shape=out_shape, i...  7.55 us
    ppermute x3, starting transfers between devices, local(): lax.ppermute(total, 'ctx', outer_pairs(n_ctx, inner, k))  4.39 us
    ppermute x3, starting transfers between devices, local(): lax.ppermute(sends[k], 'ctx', inner_pairs(n_ctx, inner, k))  3.55 us
    ppermute x3, starting transfers between devices, local(): lax.ppermute(prefixes[k], 'ctx', inner_pairs(n_ctx, inner, k))  3.55 us
    ppermute x3, waiting for transfers between devices, local(): lax.ppermute(sends[k], 'ctx', inner_pairs(n_ctx, inner, k))  3.25 us
    ppermute x5, waiting for transfers between devices, trade(): return lax.ppermute(held, ('ctx', 'head'), pairs)  1.39 us
    ppermute x1, waiting for transfers between devices, local(): lax.ppermute(gated, 'head', [(j, target(j, k, n_head)) for j in range(n_h...  1.34 us
  transfers between devices with their start and end apart: 15, of which 6 were waited for; matrix products, arithmetic and copies ran while one was open for 0% of the time, Pallas kernels for 16%

profile of v2, /device:TPU:0, one launch (start us, length us, event | category | flops | bytes accessed | tf_op | source)
XLA Modules:
  0.0 37.0 jit_solution(16243239656465411666)
XLA Ops:
  0.0 4.0 %collective-permute-start.3 = (bf16[64,512]{1,0:T(8,128)(2,1)}, bf16[64,512]{1,0:T(8,128)(2,1)S(1)}, u32[]{:S(2)}, u32[]{:S(2)}) collective-permute-start(bf16[64,512]{1,0:T(8,128)(2,1)} %refs_1_.1), channel_id=1, source_target_pairs={{0,16},{1,17},{2,18},{3,19},{4,20},{5,21},{6,22},{7,23},{8,24},{9,... | collective-permute-start | bytes 196616 | tf_op jit(solution)/shard_map/ppermute | solution.py:378
  4.0 0.0 copy-start.3
  4.0 2.3 %shard_map.73 = (f32[8,128]{1,0:T(8,128)}, bf16[272,128]{1,0:T(8,128)(2,1)}, bf16[272,128]{1,0:T(8,128)(2,1)}, bf16[272,128]{1,0:T(8,128)(2,1)}, bf16[272,128]{1,0:T(8,128)(2,1)}) custom-call(f32[4,128]{1,0:T(4,128)} %bitcast.4, f32[4,128]{1,0:T(4,128)} %bitcast.5, bf16[512,256]{1,0:T(8,128)(2,1)} %refs_4_.2, bf16[512,512]{1,0:T(8,128)(2,1)} %refs_5_.1), custom_call_target="tpu_custom_call" | custom-call | flops 2200000000 | bytes 7400000 | tf_op jit(solution)/shard_map/pallas_call | solution.py:331
  6.4 0.0 copy-start.6
  6.4 1.6 %collective-permute-start = (bf16[272,128]{1,0:T(8,128)(2,1)}, bf16[272,128]{1,0:T(8,128)(2,1)S(1)}, u32[]{:S(2)}, u32[]{:S(2)}) collective-permute-start(bf16[272,128]{1,0:T(8,128)(2,1)} %get-tuple-element.27), channel_id=1, source_target_pairs={{0,2},{2,0},{4,6},{6,4},{8,10},{10,8},{12,14},{14,12},{16,18},{18,... | collective-permute-start | bytes 208904 | tf_op jit(solution)/shard_map/ppermute | solution.py:409
  7.9 1.5 %collective-permute-start.1 = (bf16[272,128]{1,0:T(8,128)(2,1)}, bf16[272,128]{1,0:T(8,128)(2,1)S(1)}, u32[]{:S(2)}, u32[]{:S(2)}) collective-permute-start(bf16[272,128]{1,0:T(8,128)(2,1)} %get-tuple-element.28), channel_id=1, source_target_pairs={{0,4},{2,6},{4,0},{6,2},{8,12},{10,14},{12,8},{14,10},{16,20},{18,... | collective-permute-start | bytes 208904 | tf_op jit(solution)/shard_map/ppermute | solution.py:409
  9.4 0.5 %collective-permute-start.2 = (bf16[272,128]{1,0:T(8,128)(2,1)}, bf16[272,128]{1,0:T(8,128)(2,1)S(1)}, u32[]{:S(2)}, u32[]{:S(2)}) collective-permute-start(bf16[272,128]{1,0:T(8,128)(2,1)} %get-tuple-element.29), channel_id=1, source_target_pairs={{0,6},{2,4},{4,2},{6,0},{8,14},{10,12},{12,10},{14,8},{16,22},{18,... | collective-permute-start | bytes 208904 | tf_op jit(solution)/shard_map/ppermute | solution.py:409
  9.9 0.0 collective-permute-done.3.refs_2_
  9.9 0.0 copy-done.3
  9.9 0.0 copy-done.6
  9.9 0.0 copy-start.5
  10.0 1.6 %collective-permute-start.4 = (bf16[128,512]{1,0:T(8,128)(2,1)S(1)}, bf16[128,512]{1,0:T(8,128)(2,1)S(1)}, u32[]{:S(2)}, u32[]{:S(2)}) collective-permute-start(bf16[128,512]{1,0:T(8,128)(2,1)S(1)} %shard_map.75.refs_1_.refs_0_), channel_id=1, source_target_pairs={{0,8},{1,9},{2,10},{3,11},{4,12},{5,13},{6,14},{7,15},{8,0},{9,1},... | collective-permute-start | bytes 393224 | tf_op jit(solution)/shard_map/ppermute | solution.py:378
  11.6 0.0 collective-permute-done.refs_1_.refs_3_
  11.6 1.6 %collective-permute-done.1.refs_2_.refs_4_ = bf16[272,128]{1,0:T(8,128)(2,1)S(1)} collective-permute-done((bf16[272,128]{1,0:T(8,128)(2,1)}, bf16[272,128]{1,0:T(8,128)(2,1)S(1)}, u32[]{:S(2)}, u32[]{:S(2)}) %collective-permute-start.1) | collective-permute-done | bytes 69664 | tf_op jit(solution)/shard_map/ppermute | solution.py:409
  13.2 1.7 %collective-permute-done.2.refs_3_.refs_5_ = bf16[272,128]{1,0:T(8,128)(2,1)S(1)} collective-permute-done((bf16[272,128]{1,0:T(8,128)(2,1)}, bf16[272,128]{1,0:T(8,128)(2,1)S(1)}, u32[]{:S(2)}, u32[]{:S(2)}) %collective-permute-start.2) | collective-permute-done | bytes 69664 | tf_op jit(solution)/shard_map/ppermute | solution.py:409
  14.9 0.0 copy-done.5
  14.9 0.1 shard_map.74.refs_0_
  15.0 0.0 copy-start
  15.0 0.0 copy-start.1
  15.0 0.0 copy-start.2
  15.0 0.0 copy-start.4
  15.0 0.0 collective-permute-done.4.refs_2_
  15.1 1.5 %collective-permute-start.5 = (bf16[256,512]{1,0:T(8,128)(2,1)S(1)}, bf16[256,512]{1,0:T(8,128)(2,1)S(1)}, u32[]{:S(2)}, u32[]{:S(2)}) collective-permute-start(bf16[256,512]{1,0:T(8,128)(2,1)S(1)} %shard_map.76.refs_0_.refs_1_), channel_id=1, source_target_pairs={{0,4},{1,3},{2,6},{3,1},{4,0},{5,7},{6,2},{7,5},{8,12},{9,11},{10,... | collective-permute-start | bytes 786440 | tf_op jit(solution)/shard_map/ppermute | solution.py:378
  16.6 1.4 %collective-permute-start.10 = (bf16[272,128]{1,0:T(8,128)(2,1)S(1)}, bf16[272,128]{1,0:T(8,128)(2,1)S(1)}, u32[]{:S(2)}, u32[]{:S(2)}) collective-permute-start(bf16[272,128]{1,0:T(8,128)(2,1)S(1)} %shard_map.74.refs_0_), channel_id=1, source_target_pairs={{0,24},{2,26},{4,28},{6,30},{8,16},{10,18},{12,20},{14,22},{16,8},... | collective-permute-start | bytes 208904 | tf_op jit(solution)/shard_map/ppermute | solution.py:423
  18.0 1.6 %collective-permute-start.9 = (bf16[272,128]{1,0:T(8,128)(2,1)S(1)}, bf16[272,128]{1,0:T(8,128)(2,1)S(1)}, u32[]{:S(2)}, u32[]{:S(2)}) collective-permute-start(bf16[272,128]{1,0:T(8,128)(2,1)S(1)} %shard_map.74.refs_0_), channel_id=1, source_target_pairs={{0,16},{2,18},{4,20},{6,22},{8,24},{10,26},{12,28},{14,30},{16,0},... | collective-permute-start | bytes 208904 | tf_op jit(solution)/shard_map/ppermute | solution.py:423
  19.6 1.3 %collective-permute-start.8 = (bf16[272,128]{1,0:T(8,128)(2,1)S(1)}, bf16[272,128]{1,0:T(8,128)(2,1)S(1)}, u32[]{:S(2)}, u32[]{:S(2)}) collective-permute-start(bf16[272,128]{1,0:T(8,128)(2,1)S(1)} %shard_map.74.refs_0_), channel_id=1, source_target_pairs={{0,8},{2,10},{4,12},{6,14},{8,0},{10,2},{12,4},{14,6},{16,24},{18,... | collective-permute-start | bytes 208904 | tf_op jit(solution)/shard_map/ppermute | solution.py:423
  21.0 1.5 %collective-permute-start.6 = (bf16[256,512]{1,0:T(8,128)(2,1)S(1)}, bf16[256,512]{1,0:T(8,128)(2,1)S(1)}, u32[]{:S(2)}, u32[]{:S(2)}) collective-permute-start(bf16[256,512]{1,0:T(8,128)(2,1)S(1)} %shard_map.76.refs_0_.refs_1_), channel_id=1, source_target_pairs={{0,2},{1,5},{2,0},{3,7},{4,6},{5,1},{6,4},{7,3},{8,10},{9,13},{10,... | collective-permute-start | bytes 786440 | tf_op jit(solution)/shard_map/ppermute | solution.py:378
  22.5 0.4 collective-permute-done.5.refs_0_.refs_2_
  22.8 2.1 %collective-permute-start.7 = (bf16[256,512]{1,0:T(8,128)(2,1)S(1)}, bf16[256,512]{1,0:T(8,128)(2,1)S(1)}, u32[]{:S(2)}, u32[]{:S(2)}) collective-permute-start(bf16[256,512]{1,0:T(8,128)(2,1)S(1)} %collective-permute-done.5.refs_0_.refs_2_), channel_id=1, source_target_pairs={{0,2},{1,5},{2,0},{3,7},{4,6},{5,1},{6,4},{7,3},{8,10},{9,13},{10,... | collective-permute-start | bytes 786440 | tf_op jit(solution)/shard_map/ppermute | solution.py:378
  25.0 0.0 copy-done
  25.0 0.0 copy-done.1
  25.0 0.0 copy-done.2
  25.0 0.0 copy-done.4
  25.0 0.9 %shard_map.77 = (f32[512,512]{1,0:T(8,128)S(1)}, f32[512,128]{1,0:T(8,128)S(1)}) custom-call(bf16[128,512]{1,0:T(8,128)(2,1)S(1)} %shard_map.75.refs_1_.refs_0_, f32[8,128]{1,0:T(8,128)S(1)} %copy-done.6, f32[4,128]{1,0:T(4,128)S(1)} %bitcast.3, bf16[512,256]{1,0:T(8,128)(2,1)S(1)} %copy-done, bf16[512,256]{1,0:T(8,128)(2,1)S(1)} %copy-done.2, ...), custom_call_target="tpu_custom_call" | custom-call | flops 8800000000 | bytes 29600000 | tf_op jit(solution)/shard_map/pallas_call | solution.py:331
  25.9 0.3 shard_map.78
  26.1 0.0 collective-permute-done.10.refs_4_
  26.1 0.0 collective-permute-done.9.refs_3_
  26.1 0.0 collective-permute-done.8.refs_2_
  26.1 0.1 shard_map.79
  26.3 0.1 collective-permute-start.11
  26.4 1.9 %collective-permute-start.12 = (bf16[256,128]{1,0:T(8,128)(2,1)S(1)}, bf16[256,128]{1,0:T(8,128)(2,1)S(1)}, u32[]{:S(2)}, u32[]{:S(2)}) collective-permute-start(bf16[256,128]{1,0:T(8,128)(2,1)S(1)} %get-tuple-element.43), channel_id=1, source_target_pairs={{0,4},{2,6},{4,0},{6,2},{8,12},{10,14},{12,8},{14,10},{16,20},{18,... | collective-permute-start | bytes 196616 | tf_op jit(solution)/shard_map/ppermute | solution.py:440
  28.2 1.6 %collective-permute-start.13 = (bf16[256,128]{1,0:T(8,128)(2,1)S(1)}, bf16[256,128]{1,0:T(8,128)(2,1)S(1)}, u32[]{:S(2)}, u32[]{:S(2)}) collective-permute-start(bf16[256,128]{1,0:T(8,128)(2,1)S(1)} %get-tuple-element.44), channel_id=1, source_target_pairs={{0,6},{2,4},{4,2},{6,0},{8,14},{10,12},{12,10},{14,8},{16,22},{18,... | collective-permute-start | bytes 196616 | tf_op jit(solution)/shard_map/ppermute | solution.py:440
  29.8 0.0 collective-permute-done.6.refs_1_.refs_3_
  29.8 1.0 %collective-permute-done.7.refs_2_.refs_4_ = bf16[256,512]{1,0:T(8,128)(2,1)S(1)} collective-permute-done((bf16[256,512]{1,0:T(8,128)(2,1)S(1)}, bf16[256,512]{1,0:T(8,128)(2,1)S(1)}, u32[]{:S(2)}, u32[]{:S(2)}) %collective-permute-start.7) | collective-permute-done | bytes 262176 | tf_op jit(solution)/shard_map/ppermute | solution.py:378
  30.9 1.7 %shard_map.80 = (f32[512,512]{1,0:T(8,128)S(1)}, f32[512,128]{1,0:T(8,128)S(1)}) custom-call(bf16[256,512]{1,0:T(8,128)(2,1)S(1)} %collective-permute-done.5.refs_0_.refs_2_, bf16[256,512]{1,0:T(8,128)(2,1)S(1)} %collective-permute-done.6.refs_1_.refs_3_, bf16[256,512]{1,0:T(8,128)(2,1)S(1)} %collective-permute-done.7.refs_2_.refs_4_, ...), custom_call_target="tpu_custom_call" | custom-call | flops 8800000000 | bytes 29600000 | tf_op jit(solution)/shard_map/pallas_call | solution.py:331
  32.6 0.0 collective-permute-done.11.refs_4_
  32.6 0.0 collective-permute-done.12.refs_5_
  32.6 0.8 %collective-permute-done.13.refs_6_ = bf16[256,128]{1,0:T(8,128)(2,1)S(1)} collective-permute-done((bf16[256,128]{1,0:T(8,128)(2,1)S(1)}, bf16[256,128]{1,0:T(8,128)(2,1)S(1)}, u32[]{:S(2)}, u32[]{:S(2)}) %collective-permute-start.13) | collective-permute-done | bytes 65568 | tf_op jit(solution)/shard_map/ppermute | solution.py:440
  33.4 0.4 shard_map.81.refs_0_
  33.8 0.1 collective-permute-start.14
  33.8 0.5 %shard_map.82 = (f32[512,512]{1,0:T(8,128)S(1)}, bf16[512,512]{1,0:T(8,128)(2,1)S(1)}) custom-call(bf16[512,512]{1,0:T(8,128)(2,1)S(1)} %shard_map.81.refs_0_, bf16[256,512]{1,0:T(8,128)(2,1)S(1)} %shard_map.76.refs_0_.refs_1_, bf16[256,512]{1,0:T(8,128)(2,1)S(1)} %collective-permute-done.5.refs_0_.refs_2_, ...), custom_call_target="tpu_custom_call" | custom-call | flops 2200000000 | bytes 7400000 | tf_op jit(solution)/shard_map/pallas_call | solution.py:331
  34.4 1.3 %collective-permute-done.14.refs_2_ = bf16[512,512]{1,0:T(8,128)(2,1)S(1)} collective-permute-done((bf16[512,512]{1,0:T(8,128)(2,1)S(1)}, bf16[512,512]{1,0:T(8,128)(2,1)S(1)}, u32[]{:S(2)}, u32[]{:S(2)}) %collective-permute-start.14) | collective-permute-done | bytes 524320 | tf_op jit(solution)/shard_map/ppermute | solution.py:457
  35.7 1.2 %shard_map.83 = bf16[512,512]{1,0:T(8,128)(2,1)} custom-call(f32[512,512]{1,0:T(8,128)S(1)} %get-tuple-element.45.refs_0_, bf16[512,512]{1,0:T(8,128)(2,1)S(1)} %get-tuple-element.46.refs_1_, bf16[512,512]{1,0:T(8,128)(2,1)S(1)} %collective-permute-done.14.refs_2_), custom_call_target="tpu_custom_call" | custom-call | flops 1100000000 | bytes 3700000 | tf_op jit(solution)/shard_map/pallas_call | solution.py:331
  (2 shorter events, 0.0 us)
Async XLA Ops:
  0.0 9.9 %collective-permute-start.3 = (bf16[64,512]{1,0:T(8,128)(2,1)}, bf16[64,512]{1,0:T(8,128)(2,1)S(1)}, u32[]{:S(2)}, u32[]{:S(2)}) collective-permute-start(bf16[64,512]{1,0:T(8,128)(2,1)} %refs_1_.1), channel_id=1, source_target_pairs={{0,16},{1,17},{2,18},{3,19},{4,20},{5,21},{6,22},{7,23},{8,24},{9,... | collective-permute-start | bytes 196616 | tf_op jit(solution)/shard_map/ppermute | solution.py:378
  4.0 5.9 %copy-start.3 = (bf16[64,512]{1,0:T(8,128)(2,1)S(1)}, bf16[64,512]{1,0:T(8,128)(2,1)}, u32[]{:S(2)}) copy-start(bf16[64,512]{1,0:T(8,128)(2,1)} %refs_1_.1) | copy-start | bytes 196612
  6.4 3.6 %copy-start.6 = (f32[8,128]{1,0:T(8,128)S(1)}, f32[8,128]{1,0:T(8,128)}, u32[]{:S(2)}) copy-start(f32[8,128]{1,0:T(8,128)} %get-tuple-element.30.refs_0_.refs_1_) | copy-start | bytes 12292
  6.4 5.2 %collective-permute-start = (bf16[272,128]{1,0:T(8,128)(2,1)}, bf16[272,128]{1,0:T(8,128)(2,1)S(1)}, u32[]{:S(2)}, u32[]{:S(2)}) collective-permute-start(bf16[272,128]{1,0:T(8,128)(2,1)} %get-tuple-element.27), channel_id=1, source_target_pairs={{0,2},{2,0},{4,6},{6,4},{8,10},{10,8},{12,14},{14,12},{16,18},{18,... | collective-permute-start | bytes 208904 | tf_op jit(solution)/shard_map/ppermute | solution.py:409
  7.9 5.3 %collective-permute-start.1 = (bf16[272,128]{1,0:T(8,128)(2,1)}, bf16[272,128]{1,0:T(8,128)(2,1)S(1)}, u32[]{:S(2)}, u32[]{:S(2)}) collective-permute-start(bf16[272,128]{1,0:T(8,128)(2,1)} %get-tuple-element.28), channel_id=1, source_target_pairs={{0,4},{2,6},{4,0},{6,2},{8,12},{10,14},{12,8},{14,10},{16,20},{18,... | collective-permute-start | bytes 208904 | tf_op jit(solution)/shard_map/ppermute | solution.py:409
  9.4 5.4 %collective-permute-start.2 = (bf16[272,128]{1,0:T(8,128)(2,1)}, bf16[272,128]{1,0:T(8,128)(2,1)S(1)}, u32[]{:S(2)}, u32[]{:S(2)}) collective-permute-start(bf16[272,128]{1,0:T(8,128)(2,1)} %get-tuple-element.29), channel_id=1, source_target_pairs={{0,6},{2,4},{4,2},{6,0},{8,14},{10,12},{12,10},{14,8},{16,22},{18,... | collective-permute-start | bytes 208904 | tf_op jit(solution)/shard_map/ppermute | solution.py:409
  9.9 4.9 %copy-start.5 = (bf16[272,128]{1,0:T(8,128)(2,1)S(1)}, bf16[272,128]{1,0:T(8,128)(2,1)}, u32[]{:S(2)}) copy-start(bf16[272,128]{1,0:T(8,128)(2,1)} %get-tuple-element.26.refs_0_.refs_2_) | copy-start | bytes 208900
  10.0 5.1 %collective-permute-start.4 = (bf16[128,512]{1,0:T(8,128)(2,1)S(1)}, bf16[128,512]{1,0:T(8,128)(2,1)S(1)}, u32[]{:S(2)}, u32[]{:S(2)}) collective-permute-start(bf16[128,512]{1,0:T(8,128)(2,1)S(1)} %shard_map.75.refs_1_.refs_0_), channel_id=1, source_target_pairs={{0,8},{1,9},{2,10},{3,11},{4,12},{5,13},{6,14},{7,15},{8,0},{9,1},... | collective-permute-start | bytes 393224 | tf_op jit(solution)/shard_map/ppermute | solution.py:378
  15.0 10.0 %copy-start = (bf16[512,256]{1,0:T(8,128)(2,1)S(1)}, bf16[512,256]{1,0:T(8,128)(2,1)}, u32[]{:S(2)}) copy-start(bf16[512,256]{1,0:T(8,128)(2,1)} %refs_0_.1) | copy-start | bytes 786436
  15.0 10.0 %copy-start.1 = (bf16[512,512]{1,0:T(8,128)(2,1)S(1)}, bf16[512,512]{1,0:T(8,128)(2,1)}, u32[]{:S(2)}) copy-start(bf16[512,512]{1,0:T(8,128)(2,1)} %refs_5_.1) | copy-start | bytes 1572868
  15.0 10.0 %copy-start.2 = (bf16[512,256]{1,0:T(8,128)(2,1)S(1)}, bf16[512,256]{1,0:T(8,128)(2,1)}, u32[]{:S(2)}) copy-start(bf16[512,256]{1,0:T(8,128)(2,1)} %refs_4_.2) | copy-start | bytes 786436
  15.0 10.0 %copy-start.4 = (f32[512,1]{0,1:T(1,128)S(1)}, f32[512,1]{0,1:T(1,128)}, u32[]{:S(2)}) copy-start(f32[512,1]{0,1:T(1,128)} %param.12) | copy-start | bytes 6148
  15.1 7.8 %collective-permute-start.5 = (bf16[256,512]{1,0:T(8,128)(2,1)S(1)}, bf16[256,512]{1,0:T(8,128)(2,1)S(1)}, u32[]{:S(2)}, u32[]{:S(2)}) collective-permute-start(bf16[256,512]{1,0:T(8,128)(2,1)S(1)} %shard_map.76.refs_0_.refs_1_), channel_id=1, source_target_pairs={{0,4},{1,3},{2,6},{3,1},{4,0},{5,7},{6,2},{7,5},{8,12},{9,11},{10,... | collective-permute-start | bytes 786440 | tf_op jit(solution)/shard_map/ppermute | solution.py:378
  16.6 9.5 %collective-permute-start.10 = (bf16[272,128]{1,0:T(8,128)(2,1)S(1)}, bf16[272,128]{1,0:T(8,128)(2,1)S(1)}, u32[]{:S(2)}, u32[]{:S(2)}) collective-permute-start(bf16[272,128]{1,0:T(8,128)(2,1)S(1)} %shard_map.74.refs_0_), channel_id=1, source_target_pairs={{0,24},{2,26},{4,28},{6,30},{8,16},{10,18},{12,20},{14,22},{16,8},... | collective-permute-start | bytes 208904 | tf_op jit(solution)/shard_map/ppermute | solution.py:423
  18.0 8.1 %collective-permute-start.9 = (bf16[272,128]{1,0:T(8,128)(2,1)S(1)}, bf16[272,128]{1,0:T(8,128)(2,1)S(1)}, u32[]{:S(2)}, u32[]{:S(2)}) collective-permute-start(bf16[272,128]{1,0:T(8,128)(2,1)S(1)} %shard_map.74.refs_0_), channel_id=1, source_target_pairs={{0,16},{2,18},{4,20},{6,22},{8,24},{10,26},{12,28},{14,30},{16,0},... | collective-permute-start | bytes 208904 | tf_op jit(solution)/shard_map/ppermute | solution.py:423
  19.6 6.5 %collective-permute-start.8 = (bf16[272,128]{1,0:T(8,128)(2,1)S(1)}, bf16[272,128]{1,0:T(8,128)(2,1)S(1)}, u32[]{:S(2)}, u32[]{:S(2)}) collective-permute-start(bf16[272,128]{1,0:T(8,128)(2,1)S(1)} %shard_map.74.refs_0_), channel_id=1, source_target_pairs={{0,8},{2,10},{4,12},{6,14},{8,0},{10,2},{12,4},{14,6},{16,24},{18,... | collective-permute-start | bytes 208904 | tf_op jit(solution)/shard_map/ppermute | solution.py:423
  21.0 8.9 %collective-permute-start.6 = (bf16[256,512]{1,0:T(8,128)(2,1)S(1)}, bf16[256,512]{1,0:T(8,128)(2,1)S(1)}, u32[]{:S(2)}, u32[]{:S(2)}) collective-permute-start(bf16[256,512]{1,0:T(8,128)(2,1)S(1)} %shard_map.76.refs_0_.refs_1_), channel_id=1, source_target_pairs={{0,2},{1,5},{2,0},{3,7},{4,6},{5,1},{6,4},{7,3},{8,10},{9,13},{10,... | collective-permute-start | bytes 786440 | tf_op jit(solution)/shard_map/ppermute | solution.py:378
  22.8 8.0 %collective-permute-start.7 = (bf16[256,512]{1,0:T(8,128)(2,1)S(1)}, bf16[256,512]{1,0:T(8,128)(2,1)S(1)}, u32[]{:S(2)}, u32[]{:S(2)}) collective-permute-start(bf16[256,512]{1,0:T(8,128)(2,1)S(1)} %collective-permute-done.5.refs_0_.refs_2_), channel_id=1, source_target_pairs={{0,2},{1,5},{2,0},{3,7},{4,6},{5,1},{6,4},{7,3},{8,10},{9,13},{10,... | collective-permute-start | bytes 786440 | tf_op jit(solution)/shard_map/ppermute | solution.py:378
  26.3 6.3 %collective-permute-start.11 = (bf16[256,128]{1,0:T(8,128)(2,1)S(1)}, bf16[256,128]{1,0:T(8,128)(2,1)S(1)}, u32[]{:S(2)}, u32[]{:S(2)}) collective-permute-start(bf16[256,128]{1,0:T(8,128)(2,1)S(1)} %get-tuple-element.42), channel_id=1, source_target_pairs={{0,2},{2,0},{4,6},{6,4},{8,10},{10,8},{12,14},{14,12},{16,18},{18,... | collective-permute-start | bytes 196616 | tf_op jit(solution)/shard_map/ppermute | solution.py:440
  26.4 6.2 %collective-permute-start.12 = (bf16[256,128]{1,0:T(8,128)(2,1)S(1)}, bf16[256,128]{1,0:T(8,128)(2,1)S(1)}, u32[]{:S(2)}, u32[]{:S(2)}) collective-permute-start(bf16[256,128]{1,0:T(8,128)(2,1)S(1)} %get-tuple-element.43), channel_id=1, source_target_pairs={{0,4},{2,6},{4,0},{6,2},{8,12},{10,14},{12,8},{14,10},{16,20},{18,... | collective-permute-start | bytes 196616 | tf_op jit(solution)/shard_map/ppermute | solution.py:440
  28.2 5.2 %collective-permute-start.13 = (bf16[256,128]{1,0:T(8,128)(2,1)S(1)}, bf16[256,128]{1,0:T(8,128)(2,1)S(1)}, u32[]{:S(2)}, u32[]{:S(2)}) collective-permute-start(bf16[256,128]{1,0:T(8,128)(2,1)S(1)} %get-tuple-element.44), channel_id=1, source_target_pairs={{0,6},{2,4},{4,2},{6,0},{8,14},{10,12},{12,10},{14,8},{16,22},{18,... | collective-permute-start | bytes 196616 | tf_op jit(solution)/shard_map/ppermute | solution.py:440
  33.8 2.0 %collective-permute-start.14 = (bf16[512,512]{1,0:T(8,128)(2,1)S(1)}, bf16[512,512]{1,0:T(8,128)(2,1)S(1)}, u32[]{:S(2)}, u32[]{:S(2)}) collective-permute-start(bf16[512,512]{1,0:T(8,128)(2,1)S(1)} %shard_map.81.refs_0_), channel_id=1, source_target_pairs={{0,1},{1,0},{2,3},{3,2},{4,5},{5,4},{6,7},{7,6},{8,9},{9,8},{10,11... | collective-permute-start | bytes 1572872 | tf_op jit(solution)/shard_map/ppermute | solution.py:457

commit v3 on v2

--- a/solution.py
+++ b/solution.py
@@ -206,20 +206,13 @@
             state_ref[...] = jnp.concatenate([top, norm, pad], axis=0)
 
 
-def inside_kernel(gates_ref, output_ref, queries_ref, keys_ref, values_ref, num_ref, cols_ref):
-    rows = output_ref.shape[0]
+def inside_kernel(gates_ref, output_ref, queries_ref, keys_ref, values_ref, num_ref, stats_ref):
+    rows = queries_ref.shape[0] // LANES
     scale = queries_ref.shape[1] ** (-0.5)
-    down = lax.broadcasted_iota(jnp.int32, (LANES, LANES), 0)
     across = lax.broadcasted_iota(jnp.int32, (LANES, LANES), 1)
-    causal, same = down >= across, down == across
-    lane = lax.broadcasted_iota(jnp.int32, (LANES, LANES), 1)
+    causal = lax.broadcasted_iota(jnp.int32, (LANES, LANES), 0) >= across
     gain = gates_ref[0:rows, :]
-    cum_decay = gates_ref[rows : 2 * rows, :]
-    open_gate = jax.nn.sigmoid(output_ref[...])
-
-    def column(row):
-        return jnp.sum(jnp.where(same, row, 0.0), axis=1, keepdims=True)
-
+    stats_ref[2 * rows : 3 * rows, :] = jax.nn.sigmoid(output_ref[...])
     before = jnp.full((1, 1), NEG, jnp.float32)
     for i in range(rows):
         here = slice(i * LANES, (i + 1) * LANES)
@@ -247,33 +240,44 @@
         num_ref[here, :] = jnp.dot(
             weighted, values_ref[0:width, :], preferred_element_type=jnp.float32
         )
-        cols = jnp.where(lane == 0, den, peak)
-        cols = jnp.where(lane == 2, column(cum_decay[i : i + 1]), cols)
-        cols_ref[here, :] = jnp.where(lane == 3, column(open_gate[i : i + 1]), cols)
-
-
-def rescale_kernel(state_ref, queries_ref, num_ref, cols_ref, done_ref, lift_ref):
-    width = queries_ref.shape[1]
+        turned = jnp.where(across == 0, den, peak).T
+        stats_ref[i : i + 1, :] = turned[0:1]
+        stats_ref[rows + i : rows + i + 1, :] = turned[1:2]
+
+
+def rescale_kernel(state_ref, gates_ref, stats_ref, queries_ref, num_ref, done_ref, lift_ref):
+    rows, width = gates_ref.shape[0] // 2, queries_ref.shape[1]
     n = width // LANES
     scale = width ** (-0.5)
-    top_prev = state_ref[0:1, 0:1]
+    top_prev = state_ref[0:1, :]
     norm = jnp.concatenate([state_ref[1 + i : 2 + i, :] for i in range(n)], axis=1)
-    for i in range(queries_ref.shape[0] // LANES):
+    three = [p.astype(jnp.float32) for p in pieces3(norm)]
+    three.append(jnp.zeros((TILE - 3, width), jnp.float32))
+    den_out = lax.dot_general(
+        jnp.concatenate(three, axis=0).astype(jnp.bfloat16),
+        queries_ref[...],
+        (((1,), (1,)), ((), ())),
+        preferred_element_type=jnp.float32,
+    )
+    den_out = jnp.concatenate(lane_blocks(den_out[0:1] + den_out[1:2] + den_out[2:3]), axis=0)
+    den_in, peak = stats_ref[0:rows, :], stats_ref[rows : 2 * rows, :]
+    top = jnp.maximum(peak, top_prev)
+    keep, lift = jnp.exp(peak - top), jnp.exp(top_prev - top) * scale
+    den = jnp.abs(keep * den_in + lift * den_out)
+    floor = jnp.exp(-(gates_ref[rows : 2 * rows, :] + top))
+    ratio = stats_ref[2 * rows : 3 * rows, :] / jnp.maximum(den, floor)
+    keep, lift = keep * ratio, lift * ratio
+    for i in range(rows):
         here = slice(i * LANES, (i + 1) * LANES)
-        den_out = jnp.sum(queries_ref[here, :].astype(jnp.float32) * norm, axis=1, keepdims=True)
-        cols = cols_ref[here, :]
-        den_in, peak = cols[:, 0:1], cols[:, 1:2]
-        cum_decay, open_gate = cols[:, 2:3], cols[:, 3:4]
-        top = jnp.maximum(peak, top_prev)
-        keep, lift = jnp.exp(peak - top), jnp.exp(top_prev - top) * scale
-        den = jnp.abs(keep * den_in + lift * den_out)
-        ratio = open_gate / jnp.maximum(den, jnp.exp(-(cum_decay + top)))
-        done_ref[here, :] = (keep * ratio) * num_ref[here, :]
-        lift_ref[here, :] = jnp.broadcast_to(lift * ratio, (LANES, LANES))
+        column = jnp.broadcast_to(keep[i : i + 1], (LANES, LANES)).T
+        for j in range(num_ref.shape[1] // LANES):
+            there = slice(j * LANES, (j + 1) * LANES)
+            done_ref[here, there] = column * num_ref[here, there]
+        lift_ref[here, :] = jnp.broadcast_to(lift[i : i + 1], (LANES, LANES)).T
 
 
 def output_kernel(inner, queries_ref, done_ref, lift_ref, *rest):
-    pieces, out_ref, memory = rest[:inner], rest[inner], rest[inner + 1]
+    pieces, outs, memory = rest[:inner], rest[inner:-1], rest[-1]
     member = lax.rem(lax.axis_index("ctx"), inner)
     piece = memory.shape[0] // inner
     for k in range(inner):
@@ -282,15 +286,19 @@
             memory[pl.ds(start, piece), i * LANES : (i + 1) * LANES] = pieces[k][
                 i * piece : (i + 1) * piece, :
             ]
-    for i in range(queries_ref.shape[0] // LANES):
-        here = slice(i * LANES, (i + 1) * LANES)
+    rows = outs[0].shape[0]
+    for i, out_ref in enumerate(outs):
+        here = slice(i * rows, (i + 1) * rows)
         num_out = jnp.dot(queries_ref[here, :], memory[...], preferred_element_type=jnp.float32)
-        gated = done_ref[here, :] + lift_ref[here, 0:1] * num_out
-        out_ref[here, :] = gated.astype(jnp.bfloat16)
-
-
-def own_kernel(heads, orders, rows, gated_ref, *refs):
-    bufs, (part_ref, other_ref, weights) = refs[:-3], refs[-3:]
+        column = lift_ref[here, :]
+        for j, block in enumerate(lane_blocks(num_out)):
+            there = slice(j * LANES, (j + 1) * LANES)
+            out_ref[:, there] = (done_ref[here, there] + column * block).astype(jnp.bfloat16)
+
+
+def project_kernel(heads, orders, rows, chunks, *refs):
+    gated = [refs[k * chunks : (k + 1) * chunks] for k in range(heads)]
+    bufs, (out_hbm, weights, held, sems) = refs[heads * chunks : -4], refs[-4:]
     place, head = lax.axis_index("ctx"), lax.axis_index("head")
     at = 0
     for buf in bufs:
@@ -300,41 +308,41 @@
             start = pl.multiple_of(block * rows, rows)
             weights[pl.ds(start, rows), :] = buf[s * rows : (s + 1) * rows, :]
             at += 1
-    width = gated_ref.shape[1]
-    for k in range(1, heads):
-        start = pl.multiple_of(source(head, k, heads) * width, width)
-        other_ref[(k - 1) * width : k * width, :] = weights[pl.ds(start, width), :]
-    mine = weights[pl.ds(pl.multiple_of(head * width, width), width), :]
-    part_ref[...] = jnp.dot(gated_ref[...], mine, preferred_element_type=jnp.float32)
-
-
-def others_kernel(part_ref, other_ref, *refs):
-    gated, out_ref = refs[:-1], refs[-1]
-    total, at = part_ref[...], 0
-    for g in gated:
-        weights = other_ref[at : at + g.shape[1], :]
-        total = total + jnp.dot(g[...], weights, preferred_element_type=jnp.float32)
-        at += g.shape[1]
-    out_ref[...] = total.astype(jnp.bfloat16)
-
-
-def join_kernel(a_ref, b_ref, out_ref):
-    rows = a_ref.shape[0]
-    out_ref[0:rows, :] = a_ref[...]
-    out_ref[rows:, :] = b_ref[...]
-
-
-def call(kernel, out_shape, args, scratch=(), micros=1.0, after=(), plain=(), mib=24):
+    tok, width = gated[0][0].shape
+    copies = []
+    for c in range(chunks):
+        total = 0.0
+        for k in range(heads):
+            start = pl.multiple_of(source(head, k, heads) * width, width)
+            part = weights[pl.ds(start, width), :]
+            total = total + jnp.dot(gated[k][c][...], part, preferred_element_type=jnp.float32)
+        held[c, :, :] = total.astype(jnp.bfloat16)
+        to = out_hbm.at[pl.ds(c * tok, tok), :]
+        copies.append(pltpu.make_async_copy(held.at[c], to, sems.at[c]))
+        copies[-1].start()
+    for copy in copies:
+        copy.wait()
+
+
+def join_kernel(*refs):
+    out_ref, at = refs[-1], 0
+    for ref in refs[:-1]:
+        out_ref[at : at + ref.shape[0], :] = ref[...]
+        at += ref.shape[0]
+
+
+def call(kernel, out_shape, args, scratch=(), micros=1.0, after=(), plain=(), to_hbm=False):
     skip = len(after)
-    anywhere, vmem = pl.BlockSpec(memory_space=pl.ANY), pl.BlockSpec(memory_space=pltpu.VMEM)
-    hbm = pl.BlockSpec(memory_space=pltpu.HBM)
+    anywhere, hbm, vmem = (
+        pl.BlockSpec(memory_space=m) for m in (pl.ANY, pltpu.HBM, pltpu.VMEM)
+    )
     return pl.pallas_call(
         lambda *refs: kernel(*refs[skip:]),
         out_shape=out_shape,
         in_specs=[anywhere] * skip + [hbm if i in plain else vmem for i in range(len(args))],
-        out_specs=jax.tree.map(lambda _: vmem, out_shape),
+        out_specs=jax.tree.map(lambda _: hbm if to_hbm else vmem, out_shape),
         scratch_shapes=scratch,
-        compiler_params=pltpu.CompilerParams(vmem_limit_bytes=mib * 2**20),
+        compiler_params=pltpu.CompilerParams(vmem_limit_bytes=24 * 2**20),
         cost_estimate=pl.CostEstimate(
             flops=int(micros * 1.1e9), bytes_accessed=int(micros * 3.7e6), transcendentals=0
         ),
@@ -345,9 +353,9 @@
     return jax.ShapeDtypeStruct(dims, dtype)
 
 
-def join(pair, after=()):
-    rows, width = pair[0].shape
-    return call(join_kernel, shape((2 * rows, width), pair[0].dtype), pair, micros=0.5, after=after)
+def join(parts, after=(), micros=0.5):
+    out = shape((sum(p.shape[0] for p in parts), parts[0].shape[1]), parts[0].dtype)
+    return call(join_kernel, out, parts, micros=micros, after=after)
 
 
 def doubling_steps(n_ctx):
@@ -365,11 +373,10 @@
     forget, gate_in, gate_out = (
         g.reshape(gate_rows, LANES) for g in (forget_pre, input_pre, output_pre)
     )
-
-    steps = doubling_steps(n_ctx)
-    w_bufs, order = [w_out], [0]
-
-    def trade(held, even, odd):
+    memory_rows = piece * width_v // LANES
+    message = shape((memory_rows + rows_for(width_k), LANES), bf16)
+
+    def over_ctx(held, even, odd):
         pairs = [
             (j * n_head + h, (j ^ (odd if h % 2 else even)) * n_head + h)
             for j in range(n_ctx)
@@ -377,24 +384,32 @@
         ]
         return lax.ppermute(held, ("ctx", "head"), pairs)
 
-    def gather_step(after):
-        held = join(w_bufs, after) if len(w_bufs) > 1 else w_bufs[0]
-        if steps:
-            step = steps.pop(0)
-            w_bufs[:] = [held, trade(held, step, step)]
-            order.extend([x ^ step for x in order])
-        else:
-            first, second = trade(held, 2, 1), trade(held, 1, 2)
-            w_bufs[:] = [held, first, second, trade(first, 1, 2)]
-        return [held]
-
-    gather_step([])
-    memory_rows = piece * width_v // LANES
-    message = shape((memory_rows + rows_for(width_k), LANES), bf16)
+    def in_group(sent):
+        return sent[:1] + [
+            lax.ppermute(sent[k], "ctx", inner_pairs(n_ctx, inner, k)) for k in range(1, inner)
+        ]
+
+    steps = doubling_steps(n_ctx)
+    order = [0]
+    w_parts = [w_out]
+
+    def double(after):
+        held = w_parts[0] if len(w_parts) == 1 else join(w_parts, after)
+        if not steps:
+            return held
+        step = steps.pop(0)
+        w_parts[:] = [held, over_ctx(held, step, step)]
+        order.extend([x ^ step for x in order])
+        return held
+
+    double([])
     gates, *sends = call(
         functools.partial(summary_kernel, inner),
         [shape((2 * gate_rows, LANES), f32)] + [message] * inner,
-        (forget, gate_in, keys, values),
+        [
+            pltpu.with_memory_space_constraint(x, pltpu.HBM)
+            for x in (forget, gate_in, keys, values)
+        ],
         [
             pltpu.VMEM((width_k, width_v), f32),
             *[pltpu.VMEM(x.shape, x.dtype) for x in (forget, gate_in, keys, values)],
@@ -402,72 +417,76 @@
         ],
         micros=2.0,
         plain=(0, 1, 2, 3),
-        mib=60,
-    )
-    ready = gather_step([gates])
-    blocks = [sends[0]] + [
-        lax.ppermute(sends[k], "ctx", inner_pairs(n_ctx, inner, k)) for k in range(1, inner)
-    ]
-    num_in, cols = call(
+    )
+    blocks = in_group(sends)
+    held = double([gates])
+    num_in, stats_in = call(
         inside_kernel,
-        [shape((tok, width_v), f32), shape((tok, LANES), f32)],
+        [shape((tok, width_v), f32), shape((3 * gate_rows, LANES), f32)],
         (gates, gate_out, queries, keys, values),
         micros=8.0,
-        after=ready,
-    )
-    total = call(functools.partial(group_total_kernel, inner, width_k), message, blocks)
-    while steps:
-        gather_step([total])
-    ready = gather_step([total])
+        after=[held],
+    )
+    total = call(
+        functools.partial(group_total_kernel, inner, width_k), message, blocks, after=[stats_in]
+    )
     totals = [
         lax.ppermute(total, "ctx", outer_pairs(n_ctx, inner, k)) for k in range(1, outer)
     ]
+    while steps:
+        double([total])
+    held = double([total])
+
+    one, other = (1, 2), (2, 1)
+    first = over_ctx(held, *one)
     *nears, stats = call(
         functools.partial(near_kernel, inner, width_k),
         [shape((memory_rows, LANES), f32)] * inner + [shape((inner, 8, LANES), f32)],
         blocks,
-        micros=0.3,
-        after=[*ready, cols],
-    )
+        micros=8.0,
+        after=[held, stats_in],
+    )
+    again = join([held], [stats])
+    second, third = over_ctx(again, *other), over_ctx(first, *other)
+    orders = [[x ^ s for s in (0, a, b, a ^ b) for x in order] for a, b in zip(one, other)]
     *prefixes, state = call(
         functools.partial(far_kernel, inner, outer, width_k),
         [shape((memory_rows, LANES), bf16)] * inner + [shape((8, LANES), f32)],
         (stats, *totals, *nears),
-        micros=0.1,
-        after=w_bufs[1:2],
-    )
-    parts = [prefixes[0]] + [
-        lax.ppermute(prefixes[k], "ctx", inner_pairs(n_ctx, inner, k)) for k in range(1, inner)
-    ]
+        micros=8.0,
+    )
+    parts = in_group(prefixes)
     done, lift = call(
         rescale_kernel,
         [shape((tok, width_v), f32), shape((tok, LANES), f32)],
-        (state, queries, num_in, cols),
+        (state, gates, stats_in, queries, num_in),
         micros=8.0,
-        after=w_bufs[1:4],
-    )
+        after=[first, second],
+    )
+    chunks = tok // LANES
     gated = call(
         functools.partial(output_kernel, inner),
-        shape((tok, width_v), bf16),
+        [shape((LANES, width_v), bf16)] * chunks,
         (queries, done, lift, *parts),
         [pltpu.VMEM((width_k, width_v), bf16)],
         micros=0.1,
     )
     others = [
-        lax.ppermute(gated, "head", [(j, target(j, k, n_head)) for j in range(n_head)])
+        lax.ppermute(g, "head", [(j, target(j, k, n_head)) for j in range(n_head)])
         for k in range(1, n_head)
+        for g in gated
     ]
-    cols_out = w_out.shape[1]
-    w_orders = [[x ^ s for s in (0, a, b, a ^ b) for x in order] for a, b in ((2, 1), (1, 2))]
-    part, other_rows = call(
-        functools.partial(own_kernel, n_head, w_orders, w_out.shape[0]),
-        [shape((tok, cols_out), f32), shape(((n_head - 1) * width_v, cols_out), bf16)],
-        (gated, *w_bufs),
-        [pltpu.VMEM((n_ctx * w_out.shape[0], cols_out), bf16)],
-        micros=2.0,
-    )
     return call(
-        others_kernel, shape((tok, cols_out), bf16), (part, other_rows, *others), micros=1.0
+        functools.partial(project_kernel, n_head, orders, w_out.shape[0], chunks),
+        shape((tok, w_out.shape[1]), bf16),
+        (*gated, *others, held, first, second, third),
+        [
+            pltpu.VMEM((n_ctx * w_out.shape[0], w_out.shape[1]), bf16),
+            pltpu.VMEM((chunks, LANES, w_out.shape[1]), bf16),
+            pltpu.SemaphoreType.DMA((chunks,)),
+        ],
+        micros=1.0,
+        to_hbm=True,
     )
 
 

time: 37.1 us -> 34.1 us (0.919)
  Pallas kernels: 7.55 us -> 5.32 us
  starting transfers between devices: 22.4 us -> 21.3 us
  waiting for transfers between devices: 6.8 us -> 7.21 us
    pallas_call x11, Pallas kernels: 7.55 us -> 5.32 us  [call(): pl.pallas_call(lambda *refs: kernel(*refs[skip:]), out_shape=out_shape, i...]
    ppermute x3, waiting for transfers between devices: 0.01 us -> 2.14 us  [local(): lax.ppermute(total, 'ctx', outer_pairs(n_ctx, inner, k))]
    ppermute x12 -> x15, waiting for transfers between devices: 6.79 us -> 5.08 us  [the longest x6 3.93 us: in_group(): lax.ppermute(sent[k], 'ctx', inner_pairs(n_ctx, inner, k))]
    ppermute x12 -> x15, starting transfers between devices: 18 us -> 16.8 us  [the longest x5 8.62 us: over_ctx(): return lax.ppermute(held, ('ctx', 'head'), pairs)]
  transfers between devices with their start and end apart: 15 -> 18, of which waited for: 6 -> 11; matrix products, arithmetic and copies ran while one was open for 0% -> 0% of each run, Pallas kernels for 16% -> 11%
where the time goes in v3:
time: 34.1 us; the launch traced here: 33.9 us
  starting transfers between devices  21.3 us (62%)
  waiting for transfers between devices  7.21 us (21%)
  Pallas kernels  5.32 us (16%)
    ppermute x5, starting transfers between devices, over_ctx(): return lax.ppermute(held, ('ctx', 'head'), pairs)  8.62 us
    ppermute x6, starting transfers between devices, in_group(): lax.ppermute(sent[k], 'ctx', inner_pairs(n_ctx, inner, k))  7.11 us
    pallas_call x11, Pallas kernels, call(): pl.pallas_call(lambda *refs: kernel(*refs[skip:]), out_shape=out_shape, i...  5.32 us
    ppermute x3, starting transfers between devices, local(): lax.ppermute(total, 'ctx', outer_pairs(n_ctx, inner, k))  4.45 us
    ppermute x6, waiting for transfers between devices, in_group(): lax.ppermute(sent[k], 'ctx', inner_pairs(n_ctx, inner, k))  3.93 us
    ppermute x3, waiting for transfers between devices, local(): lax.ppermute(total, 'ctx', outer_pairs(n_ctx, inner, k))  2.14 us
    ppermute x4, starting transfers between devices, local(): lax.ppermute(g, 'head', [(j, target(j, k, n_head)) for j in range(n_head)])  1.08 us
    ppermute x4, waiting for transfers between devices, local(): lax.ppermute(g, 'head', [(j, target(j, k, n_head)) for j in range(n_head)])  1.02 us
  transfers between devices with their start and end apart: 18, of which 11 were waited for; matrix products, arithmetic and copies ran while one was open for 0% of the time, Pallas kernels for 11%

profile of v3, /device:TPU:0, one launch (start us, length us, event | category | flops | bytes accessed | tf_op | source)
XLA Modules:
  0.0 33.9 jit_solution(752518742552369448)
XLA Ops:
  0.0 4.0 %collective-permute-start = (bf16[64,512]{1,0:T(8,128)(2,1)}, bf16[64,512]{1,0:T(8,128)(2,1)S(1)}, u32[]{:S(2)}, u32[]{:S(2)}) collective-permute-start(bf16[64,512]{1,0:T(8,128)(2,1)} %refs_1_.1), channel_id=1, source_target_pairs={{0,16},{1,17},{2,18},{3,19},{4,20},{5,21},{6,22},{7,23},{8,24},{9,... | collective-permute-start | bytes 196616 | tf_op jit(solution)/shard_map/ppermute | solution.py:385
  4.0 0.0 copy-start.3
  4.0 1.6 %shard_map.73 = (f32[8,128]{1,0:T(8,128)S(1)}, bf16[272,128]{1,0:T(8,128)(2,1)S(1)}, bf16[272,128]{1,0:T(8,128)(2,1)S(1)}, bf16[272,128]{1,0:T(8,128)(2,1)S(1)}, bf16[272,128]{1,0:T(8,128)(2,1)S(1)}) custom-call(f32[4,128]{1,0:T(4,128)} %bitcast.4, f32[4,128]{1,0:T(4,128)} %bitcast.5, bf16[512,256]{1,0:T(8,128)(2,1)} %refs_4_.1, bf16[512,512]{1,0:T(8,128)(2,1)} %refs_5_.2), custom_call_target="tpu_custom_call" | custom-call | flops 2200000000 | bytes 7400000 | tf_op jit(solution)/shard_map/pallas_call | solution.py:339
  5.7 1.6 %collective-permute-start.1 = (bf16[272,128]{1,0:T(8,128)(2,1)S(1)}, bf16[272,128]{1,0:T(8,128)(2,1)S(1)}, u32[]{:S(2)}, u32[]{:S(2)}) collective-permute-start(bf16[272,128]{1,0:T(8,128)(2,1)S(1)} %get-tuple-element.31), channel_id=1, source_target_pairs={{0,2},{2,0},{4,6},{6,4},{8,10},{10,8},{12,14},{14,12},{16,18},{18,... | collective-permute-start | bytes 208904 | tf_op jit(solution)/shard_map/ppermute | solution.py:389
  7.2 1.5 %collective-permute-start.2 = (bf16[272,128]{1,0:T(8,128)(2,1)S(1)}, bf16[272,128]{1,0:T(8,128)(2,1)S(1)}, u32[]{:S(2)}, u32[]{:S(2)}) collective-permute-start(bf16[272,128]{1,0:T(8,128)(2,1)S(1)} %get-tuple-element.32), channel_id=1, source_target_pairs={{0,4},{2,6},{4,0},{6,2},{8,12},{10,14},{12,8},{14,10},{16,20},{18,... | collective-permute-start | bytes 208904 | tf_op jit(solution)/shard_map/ppermute | solution.py:389
  8.8 0.5 %collective-permute-start.3 = (bf16[272,128]{1,0:T(8,128)(2,1)S(1)}, bf16[272,128]{1,0:T(8,128)(2,1)S(1)}, u32[]{:S(2)}, u32[]{:S(2)}) collective-permute-start(bf16[272,128]{1,0:T(8,128)(2,1)S(1)} %get-tuple-element.33), channel_id=1, source_target_pairs={{0,6},{2,4},{4,2},{6,0},{8,14},{10,12},{12,10},{14,8},{16,22},{18,... | collective-permute-start | bytes 208904 | tf_op jit(solution)/shard_map/ppermute | solution.py:389
  9.2 0.0 collective-permute-done.refs_2_
  9.3 0.0 copy-done.3
  9.3 0.0 copy-start
  9.3 0.0 copy-start.1
  9.3 0.0 copy-start.2
  9.3 0.0 copy-start.4
  9.3 1.6 %collective-permute-start.4 = (bf16[128,512]{1,0:T(8,128)(2,1)S(1)}, bf16[128,512]{1,0:T(8,128)(2,1)S(1)}, u32[]{:S(2)}, u32[]{:S(2)}) collective-permute-start(bf16[128,512]{1,0:T(8,128)(2,1)S(1)} %shard_map.74.refs_0_.refs_1_), channel_id=1, source_target_pairs={{0,8},{1,9},{2,10},{3,11},{4,12},{5,13},{6,14},{7,15},{8,0},{9,1},... | collective-permute-start | bytes 393224 | tf_op jit(solution)/shard_map/ppermute | solution.py:385
  10.9 0.0 copy-done
  11.0 0.0 copy-done.1
  11.0 0.0 copy-done.2
  11.0 0.0 copy-done.4
  11.0 0.9 %shard_map.75 = (f32[512,512]{1,0:T(8,128)S(1)}, f32[12,128]{1,0:T(8,128)S(1)}) custom-call(bf16[128,512]{1,0:T(8,128)(2,1)S(1)} %shard_map.74.refs_0_.refs_1_, f32[8,128]{1,0:T(8,128)S(1)} %get-tuple-element.28.refs_0_.refs_1_.refs_3_, f32[4,128]{1,0:T(4,128)S(1)} %bitcast.3, bf16[512,256]{1,0:T(8,128)(2,1)S(1)} %copy-done, bf16[512,256]{1,0:T(8,128)(2,1)S(1)} %copy-done.2, ...), custom_call_target="tpu_custom_call" | custom-call | flops 8800000000 | bytes 29600000 | tf_op jit(solution)/shard_map/pallas_call | solution.py:339
  11.9 0.0 collective-permute-done.1.refs_2_.refs_3_
  11.9 0.4 %collective-permute-done.2.refs_3_.refs_4_ = bf16[272,128]{1,0:T(8,128)(2,1)S(1)} collective-permute-done((bf16[272,128]{1,0:T(8,128)(2,1)S(1)}, bf16[272,128]{1,0:T(8,128)(2,1)S(1)}, u32[]{:S(2)}, u32[]{:S(2)}) %collective-permute-start.2) | collective-permute-done | bytes 69664 | tf_op jit(solution)/shard_map/ppermute | solution.py:389
  12.3 1.7 %collective-permute-done.3.refs_4_.refs_5_ = bf16[272,128]{1,0:T(8,128)(2,1)S(1)} collective-permute-done((bf16[272,128]{1,0:T(8,128)(2,1)S(1)}, bf16[272,128]{1,0:T(8,128)(2,1)S(1)}, u32[]{:S(2)}, u32[]{:S(2)}) %collective-permute-start.3) | collective-permute-done | bytes 69664 | tf_op jit(solution)/shard_map/ppermute | solution.py:389
  14.0 0.1 shard_map.76.refs_0_
  14.1 1.4 %collective-permute-start.9 = (bf16[272,128]{1,0:T(8,128)(2,1)S(1)}, bf16[272,128]{1,0:T(8,128)(2,1)S(1)}, u32[]{:S(2)}, u32[]{:S(2)}) collective-permute-start(bf16[272,128]{1,0:T(8,128)(2,1)S(1)} %shard_map.76.refs_0_), channel_id=1, source_target_pairs={{0,24},{2,26},{4,28},{6,30},{8,16},{10,18},{12,20},{14,22},{16,8},... | collective-permute-start | bytes 208904 | tf_op jit(solution)/shard_map/ppermute | solution.py:434
  15.5 1.7 %collective-permute-start.8 = (bf16[272,128]{1,0:T(8,128)(2,1)S(1)}, bf16[272,128]{1,0:T(8,128)(2,1)S(1)}, u32[]{:S(2)}, u32[]{:S(2)}) collective-permute-start(bf16[272,128]{1,0:T(8,128)(2,1)S(1)} %shard_map.76.refs_0_), channel_id=1, source_target_pairs={{0,16},{2,18},{4,20},{6,22},{8,24},{10,26},{12,28},{14,30},{16,0},... | collective-permute-start | bytes 208904 | tf_op jit(solution)/shard_map/ppermute | solution.py:434
  17.2 1.3 %collective-permute-start.7 = (bf16[272,128]{1,0:T(8,128)(2,1)S(1)}, bf16[272,128]{1,0:T(8,128)(2,1)S(1)}, u32[]{:S(2)}, u32[]{:S(2)}) collective-permute-start(bf16[272,128]{1,0:T(8,128)(2,1)S(1)} %shard_map.76.refs_0_), channel_id=1, source_target_pairs={{0,8},{2,10},{4,12},{6,14},{8,0},{10,2},{12,4},{14,6},{16,24},{18,... | collective-permute-start | bytes 208904 | tf_op jit(solution)/shard_map/ppermute | solution.py:434
  18.5 0.0 collective-permute-done.4.refs_2_
  18.6 0.6 %collective-permute-start.5 = (bf16[256,512]{1,0:T(8,128)(2,1)S(1)}, bf16[256,512]{1,0:T(8,128)(2,1)S(1)}, u32[]{:S(2)}, u32[]{:S(2)}) collective-permute-start(bf16[256,512]{1,0:T(8,128)(2,1)S(1)} %shard_map.77.refs_0_.refs_1_.refs_8_), channel_id=1, source_target_pairs={{0,2},{1,5},{2,0},{3,7},{4,6},{5,1},{6,4},{7,3},{8,10},{9,13},{10,... | collective-permute-start | bytes 786440 | tf_op jit(solution)/shard_map/ppermute | solution.py:385
  19.2 0.3 shard_map.78
  19.4 0.6 %collective-permute-start.6 = (bf16[256,512]{1,0:T(8,128)(2,1)S(1)}, bf16[256,512]{1,0:T(8,128)(2,1)S(1)}, u32[]{:S(2)}, u32[]{:S(2)}) collective-permute-start(bf16[256,512]{1,0:T(8,128)(2,1)S(1)} %shard_map.79), channel_id=1, source_target_pairs={{0,4},{1,3},{2,6},{3,1},{4,0},{5,7},{6,2},{7,5},{8,12},{9,11},{10,... | collective-permute-start | bytes 786440 | tf_op jit(solution)/shard_map/ppermute | solution.py:385
  20.0 0.3 collective-permute-done.9.refs_3_
  20.3 1.6 %collective-permute-done.8.refs_2_ = bf16[272,128]{1,0:T(8,128)(2,1)S(1)} collective-permute-done((bf16[272,128]{1,0:T(8,128)(2,1)S(1)}, bf16[272,128]{1,0:T(8,128)(2,1)S(1)}, u32[]{:S(2)}, u32[]{:S(2)}) %collective-permute-start.8) | collective-permute-done | bytes 69664 | tf_op jit(solution)/shard_map/ppermute | solution.py:434
  21.8 0.3 collective-permute-done.7.refs_1_
  22.2 0.1 shard_map.80
  22.3 0.9 %collective-permute-start.10 = (bf16[256,128]{1,0:T(8,128)(2,1)S(1)}, bf16[256,128]{1,0:T(8,128)(2,1)S(1)}, u32[]{:S(2)}, u32[]{:S(2)}) collective-permute-start(bf16[256,128]{1,0:T(8,128)(2,1)S(1)} %get-tuple-element.44), channel_id=1, source_target_pairs={{0,2},{2,0},{4,6},{6,4},{8,10},{10,8},{12,14},{14,12},{16,18},{18,... | collective-permute-start | bytes 196616 | tf_op jit(solution)/shard_map/ppermute | solution.py:389
  23.2 0.5 %collective-permute-start.11 = (bf16[256,128]{1,0:T(8,128)(2,1)S(1)}, bf16[256,128]{1,0:T(8,128)(2,1)S(1)}, u32[]{:S(2)}, u32[]{:S(2)}) collective-permute-start(bf16[256,128]{1,0:T(8,128)(2,1)S(1)} %get-tuple-element.45), channel_id=1, source_target_pairs={{0,4},{2,6},{4,0},{6,2},{8,12},{10,14},{12,8},{14,10},{16,20},{18,... | collective-permute-start | bytes 196616 | tf_op jit(solution)/shard_map/ppermute | solution.py:389
  23.7 2.2 %collective-permute-start.12 = (bf16[256,128]{1,0:T(8,128)(2,1)S(1)}, bf16[256,128]{1,0:T(8,128)(2,1)S(1)}, u32[]{:S(2)}, u32[]{:S(2)}) collective-permute-start(bf16[256,128]{1,0:T(8,128)(2,1)S(1)} %get-tuple-element.46), channel_id=1, source_target_pairs={{0,6},{2,4},{4,2},{6,0},{8,14},{10,12},{12,10},{14,8},{16,22},{18,... | collective-permute-start | bytes 196616 | tf_op jit(solution)/shard_map/ppermute | solution.py:389
  25.9 0.0 collective-permute-done.5.refs_0_.refs_9_
  25.9 1.8 %collective-permute-start.17 = (bf16[256,512]{1,0:T(8,128)(2,1)S(1)}, bf16[256,512]{1,0:T(8,128)(2,1)S(1)}, u32[]{:S(2)}, u32[]{:S(2)}) collective-permute-start(bf16[256,512]{1,0:T(8,128)(2,1)S(1)} %collective-permute-done.5.refs_0_.refs_9_), channel_id=1, source_target_pairs={{0,4},{1,3},{2,6},{3,1},{4,0},{5,7},{6,2},{7,5},{8,12},{9,11},{10,... | collective-permute-start | bytes 786440 | tf_op jit(solution)/shard_map/ppermute | solution.py:385
  27.6 0.0 collective-permute-done.6.refs_1_.refs_10_
  27.6 0.4 %shard_map.81 = (f32[512,512]{1,0:T(8,128)S(1)}, f32[512,128]{1,0:T(8,128)S(1)}) custom-call(bf16[256,512]{1,0:T(8,128)(2,1)S(1)} %collective-permute-done.5.refs_0_.refs_9_, bf16[256,512]{1,0:T(8,128)(2,1)S(1)} %collective-permute-done.6.refs_1_.refs_10_, f32[8,128]{1,0:T(8,128)S(1)} %get-tuple-element.39.refs_2_, ...), custom_call_target="tpu_custom_call" | custom-call | flops 8800000000 | bytes 29600000 | tf_op jit(solution)/shard_map/pallas_call | solution.py:339
  28.0 0.0 collective-permute-done.10.refs_4_
  28.0 0.0 collective-permute-done.11.refs_5_
  28.0 1.8 %collective-permute-done.12.refs_6_ = bf16[256,128]{1,0:T(8,128)(2,1)S(1)} collective-permute-done((bf16[256,128]{1,0:T(8,128)(2,1)S(1)}, bf16[256,128]{1,0:T(8,128)(2,1)S(1)}, u32[]{:S(2)}, u32[]{:S(2)}) %collective-permute-start.12) | collective-permute-done | bytes 65568 | tf_op jit(solution)/shard_map/ppermute | solution.py:389
  29.9 0.4 %shard_map.82 = (bf16[128,512]{1,0:T(8,128)(2,1)S(1)}, bf16[128,512]{1,0:T(8,128)(2,1)S(1)}, bf16[128,512]{1,0:T(8,128)(2,1)S(1)}, bf16[128,512]{1,0:T(8,128)(2,1)S(1)}) custom-call(bf16[512,256]{1,0:T(8,128)(2,1)S(1)} %copy-done, f32[512,512]{1,0:T(8,128)S(1)} %get-tuple-element.41.refs_1_, f32[512,128]{1,0:T(8,128)S(1)} %get-tuple-element.42.refs_2_, ...), custom_call_target="tpu_custom_call" | custom-call | flops 110000000 | bytes 370000 | tf_op jit(solution)/shard_map/pallas_call | solution.py:339
  30.2 0.1 collective-permute-start.13
  30.3 0.5 %collective-permute-start.14 = (bf16[128,512]{1,0:T(8,128)(2,1)S(1)}, bf16[128,512]{1,0:T(8,128)(2,1)S(1)}, u32[]{:S(2)}, u32[]{:S(2)}) collective-permute-start(bf16[128,512]{1,0:T(8,128)(2,1)S(1)} %get-tuple-element.48.refs_1_), channel_id=1, source_target_pairs={{0,1},{1,0},{2,3},{3,2},{4,5},{5,4},{6,7},{7,6},{8,9},{9,8},{10,11... | collective-permute-start | bytes 393224 | tf_op jit(solution)/shard_map/ppermute | solution.py:475
  30.8 0.1 collective-permute-start.15
  30.9 0.4 %collective-permute-start.16 = (bf16[128,512]{1,0:T(8,128)(2,1)S(1)}, bf16[128,512]{1,0:T(8,128)(2,1)S(1)}, u32[]{:S(2)}, u32[]{:S(2)}) collective-permute-start(bf16[128,512]{1,0:T(8,128)(2,1)S(1)} %get-tuple-element.50.refs_3_), channel_id=1, source_target_pairs={{0,1},{1,0},{2,3},{3,2},{4,5},{5,4},{6,7},{7,6},{8,9},{9,8},{10,11... | collective-permute-start | bytes 393224 | tf_op jit(solution)/shard_map/ppermute | solution.py:475
  31.3 0.3 collective-permute-done.13.refs_4_
  31.6 0.2 collective-permute-done.14.refs_5_
  31.8 0.3 collective-permute-done.15.refs_6_
  32.2 0.2 collective-permute-done.16.refs_7_
  32.3 0.1 collective-permute-done.17.refs_11_
  32.4 1.5 %shard_map.83 = bf16[512,512]{1,0:T(8,128)(2,1)} custom-call(bf16[128,512]{1,0:T(8,128)(2,1)S(1)} %get-tuple-element.47.refs_0_, bf16[128,512]{1,0:T(8,128)(2,1)S(1)} %get-tuple-element.48.refs_1_, bf16[128,512]{1,0:T(8,128)(2,1)S(1)} %get-tuple-element.49.refs_2_, bf16[128,512]{1,0:T(8,128)(2,1)S(1)} %get-tuple-element.50.refs_3_, ...), custom_call_target="tpu_custom_call" | custom-call | flops 1100000000 | bytes 3700000 | tf_op jit(solution)/shard_map/pallas_call | solution.py:339
  (3 shorter events, 0.0 us)
Async XLA Ops:
  0.0 9.3 %collective-permute-start = (bf16[64,512]{1,0:T(8,128)(2,1)}, bf16[64,512]{1,0:T(8,128)(2,1)S(1)}, u32[]{:S(2)}, u32[]{:S(2)}) collective-permute-start(bf16[64,512]{1,0:T(8,128)(2,1)} %refs_1_.1), channel_id=1, source_target_pairs={{0,16},{1,17},{2,18},{3,19},{4,20},{5,21},{6,22},{7,23},{8,24},{9,... | collective-permute-start | bytes 196616 | tf_op jit(solution)/shard_map/ppermute | solution.py:385
  4.0 5.2 %copy-start.3 = (bf16[64,512]{1,0:T(8,128)(2,1)S(1)}, bf16[64,512]{1,0:T(8,128)(2,1)}, u32[]{:S(2)}) copy-start(bf16[64,512]{1,0:T(8,128)(2,1)} %refs_1_.1) | copy-start | bytes 196612
  5.7 6.2 %collective-permute-start.1 = (bf16[272,128]{1,0:T(8,128)(2,1)S(1)}, bf16[272,128]{1,0:T(8,128)(2,1)S(1)}, u32[]{:S(2)}, u32[]{:S(2)}) collective-permute-start(bf16[272,128]{1,0:T(8,128)(2,1)S(1)} %get-tuple-element.31), channel_id=1, source_target_pairs={{0,2},{2,0},{4,6},{6,4},{8,10},{10,8},{12,14},{14,12},{16,18},{18,... | collective-permute-start | bytes 208904 | tf_op jit(solution)/shard_map/ppermute | solution.py:389
  7.2 5.1 %collective-permute-start.2 = (bf16[272,128]{1,0:T(8,128)(2,1)S(1)}, bf16[272,128]{1,0:T(8,128)(2,1)S(1)}, u32[]{:S(2)}, u32[]{:S(2)}) collective-permute-start(bf16[272,128]{1,0:T(8,128)(2,1)S(1)} %get-tuple-element.32), channel_id=1, source_target_pairs={{0,4},{2,6},{4,0},{6,2},{8,12},{10,14},{12,8},{14,10},{16,20},{18,... | collective-permute-start | bytes 208904 | tf_op jit(solution)/shard_map/ppermute | solution.py:389
  8.8 5.2 %collective-permute-start.3 = (bf16[272,128]{1,0:T(8,128)(2,1)S(1)}, bf16[272,128]{1,0:T(8,128)(2,1)S(1)}, u32[]{:S(2)}, u32[]{:S(2)}) collective-permute-start(bf16[272,128]{1,0:T(8,128)(2,1)S(1)} %get-tuple-element.33), channel_id=1, source_target_pairs={{0,6},{2,4},{4,2},{6,0},{8,14},{10,12},{12,10},{14,8},{16,22},{18,... | collective-permute-start | bytes 208904 | tf_op jit(solution)/shard_map/ppermute | solution.py:389
  9.3 1.7 %copy-start = (bf16[512,256]{1,0:T(8,128)(2,1)S(1)}, bf16[512,256]{1,0:T(8,128)(2,1)}, u32[]{:S(2)}) copy-start(bf16[512,256]{1,0:T(8,128)(2,1)} %refs_0_.1) | copy-start | bytes 786436
  9.3 1.7 %copy-start.1 = (bf16[512,512]{1,0:T(8,128)(2,1)S(1)}, bf16[512,512]{1,0:T(8,128)(2,1)}, u32[]{:S(2)}) copy-start(bf16[512,512]{1,0:T(8,128)(2,1)} %refs_5_.2) | copy-start | bytes 1572868
  9.3 1.7 %copy-start.2 = (bf16[512,256]{1,0:T(8,128)(2,1)S(1)}, bf16[512,256]{1,0:T(8,128)(2,1)}, u32[]{:S(2)}) copy-start(bf16[512,256]{1,0:T(8,128)(2,1)} %refs_4_.1) | copy-start | bytes 786436
  9.3 1.7 %copy-start.4 = (f32[512,1]{0,1:T(1,128)S(1)}, f32[512,1]{0,1:T(1,128)}, u32[]{:S(2)}) copy-start(f32[512,1]{0,1:T(1,128)} %param.12) | copy-start | bytes 6148
  9.3 9.2 %collective-permute-start.4 = (bf16[128,512]{1,0:T(8,128)(2,1)S(1)}, bf16[128,512]{1,0:T(8,128)(2,1)S(1)}, u32[]{:S(2)}, u32[]{:S(2)}) collective-permute-start(bf16[128,512]{1,0:T(8,128)(2,1)S(1)} %shard_map.74.refs_0_.refs_1_), channel_id=1, source_target_pairs={{0,8},{1,9},{2,10},{3,11},{4,12},{5,13},{6,14},{7,15},{8,0},{9,1},... | collective-permute-start | bytes 393224 | tf_op jit(solution)/shard_map/ppermute | solution.py:385
  14.1 6.2 %collective-permute-start.9 = (bf16[272,128]{1,0:T(8,128)(2,1)S(1)}, bf16[272,128]{1,0:T(8,128)(2,1)S(1)}, u32[]{:S(2)}, u32[]{:S(2)}) collective-permute-start(bf16[272,128]{1,0:T(8,128)(2,1)S(1)} %shard_map.76.refs_0_), channel_id=1, source_target_pairs={{0,24},{2,26},{4,28},{6,30},{8,16},{10,18},{12,20},{14,22},{16,8},... | collective-permute-start | bytes 208904 | tf_op jit(solution)/shard_map/ppermute | solution.py:434
  15.5 6.4 %collective-permute-start.8 = (bf16[272,128]{1,0:T(8,128)(2,1)S(1)}, bf16[272,128]{1,0:T(8,128)(2,1)S(1)}, u32[]{:S(2)}, u32[]{:S(2)}) collective-permute-start(bf16[272,128]{1,0:T(8,128)(2,1)S(1)} %shard_map.76.refs_0_), channel_id=1, source_target_pairs={{0,16},{2,18},{4,20},{6,22},{8,24},{10,26},{12,28},{14,30},{16,0},... | collective-permute-start | bytes 208904 | tf_op jit(solution)/shard_map/ppermute | solution.py:434
  17.2 5.0 %collective-permute-start.7 = (bf16[272,128]{1,0:T(8,128)(2,1)S(1)}, bf16[272,128]{1,0:T(8,128)(2,1)S(1)}, u32[]{:S(2)}, u32[]{:S(2)}) collective-permute-start(bf16[272,128]{1,0:T(8,128)(2,1)S(1)} %shard_map.76.refs_0_), channel_id=1, source_target_pairs={{0,8},{2,10},{4,12},{6,14},{8,0},{10,2},{12,4},{14,6},{16,24},{18,... | collective-permute-start | bytes 208904 | tf_op jit(solution)/shard_map/ppermute | solution.py:434
  18.6 7.3 %collective-permute-start.5 = (bf16[256,512]{1,0:T(8,128)(2,1)S(1)}, bf16[256,512]{1,0:T(8,128)(2,1)S(1)}, u32[]{:S(2)}, u32[]{:S(2)}) collective-permute-start(bf16[256,512]{1,0:T(8,128)(2,1)S(1)} %shard_map.77.refs_0_.refs_1_.refs_8_), channel_id=1, source_target_pairs={{0,2},{1,5},{2,0},{3,7},{4,6},{5,1},{6,4},{7,3},{8,10},{9,13},{10,... | collective-permute-start | bytes 786440 | tf_op jit(solution)/shard_map/ppermute | solution.py:385
  19.4 8.2 %collective-permute-start.6 = (bf16[256,512]{1,0:T(8,128)(2,1)S(1)}, bf16[256,512]{1,0:T(8,128)(2,1)S(1)}, u32[]{:S(2)}, u32[]{:S(2)}) collective-permute-start(bf16[256,512]{1,0:T(8,128)(2,1)S(1)} %shard_map.79), channel_id=1, source_target_pairs={{0,4},{1,3},{2,6},{3,1},{4,0},{5,7},{6,2},{7,5},{8,12},{9,11},{10,... | collective-permute-start | bytes 786440 | tf_op jit(solution)/shard_map/ppermute | solution.py:385
  22.3 5.7 %collective-permute-start.10 = (bf16[256,128]{1,0:T(8,128)(2,1)S(1)}, bf16[256,128]{1,0:T(8,128)(2,1)S(1)}, u32[]{:S(2)}, u32[]{:S(2)}) collective-permute-start(bf16[256,128]{1,0:T(8,128)(2,1)S(1)} %get-tuple-element.44), channel_id=1, source_target_pairs={{0,2},{2,0},{4,6},{6,4},{8,10},{10,8},{12,14},{14,12},{16,18},{18,... | collective-permute-start | bytes 196616 | tf_op jit(solution)/shard_map/ppermute | solution.py:389
  23.2 4.9 %collective-permute-start.11 = (bf16[256,128]{1,0:T(8,128)(2,1)S(1)}, bf16[256,128]{1,0:T(8,128)(2,1)S(1)}, u32[]{:S(2)}, u32[]{:S(2)}) collective-permute-start(bf16[256,128]{1,0:T(8,128)(2,1)S(1)} %get-tuple-element.45), channel_id=1, source_target_pairs={{0,4},{2,6},{4,0},{6,2},{8,12},{10,14},{12,8},{14,10},{16,20},{18,... | collective-permute-start | bytes 196616 | tf_op jit(solution)/shard_map/ppermute | solution.py:389
  23.7 6.2 %collective-permute-start.12 = (bf16[256,128]{1,0:T(8,128)(2,1)S(1)}, bf16[256,128]{1,0:T(8,128)(2,1)S(1)}, u32[]{:S(2)}, u32[]{:S(2)}) collective-permute-start(bf16[256,128]{1,0:T(8,128)(2,1)S(1)} %get-tuple-element.46), channel_id=1, source_target_pairs={{0,6},{2,4},{4,2},{6,0},{8,14},{10,12},{12,10},{14,8},{16,22},{18,... | collective-permute-start | bytes 196616 | tf_op jit(solution)/shard_map/ppermute | solution.py:389
  25.9 6.6 %collective-permute-start.17 = (bf16[256,512]{1,0:T(8,128)(2,1)S(1)}, bf16[256,512]{1,0:T(8,128)(2,1)S(1)}, u32[]{:S(2)}, u32[]{:S(2)}) collective-permute-start(bf16[256,512]{1,0:T(8,128)(2,1)S(1)} %collective-permute-done.5.refs_0_.refs_9_), channel_id=1, source_target_pairs={{0,4},{1,3},{2,6},{3,1},{4,0},{5,7},{6,2},{7,5},{8,12},{9,11},{10,... | collective-permute-start | bytes 786440 | tf_op jit(solution)/shard_map/ppermute | solution.py:385
  30.2 1.4 %collective-permute-start.13 = (bf16[128,512]{1,0:T(8,128)(2,1)S(1)}, bf16[128,512]{1,0:T(8,128)(2,1)S(1)}, u32[]{:S(2)}, u32[]{:S(2)}) collective-permute-start(bf16[128,512]{1,0:T(8,128)(2,1)S(1)} %get-tuple-element.47.refs_0_), channel_id=1, source_target_pairs={{0,1},{1,0},{2,3},{3,2},{4,5},{5,4},{6,7},{7,6},{8,9},{9,8},{10,11... | collective-permute-start | bytes 393224 | tf_op jit(solution)/shard_map/ppermute | solution.py:475
  30.3 1.5 %collective-permute-start.14 = (bf16[128,512]{1,0:T(8,128)(2,1)S(1)}, bf16[128,512]{1,0:T(8,128)(2,1)S(1)}, u32[]{:S(2)}, u32[]{:S(2)}) collective-permute-start(bf16[128,512]{1,0:T(8,128)(2,1)S(1)} %get-tuple-element.48.refs_1_), channel_id=1, source_target_pairs={{0,1},{1,0},{2,3},{3,2},{4,5},{5,4},{6,7},{7,6},{8,9},{9,8},{10,11... | collective-permute-start | bytes 393224 | tf_op jit(solution)/shard_map/ppermute | solution.py:475
  30.8 1.3 %collective-permute-start.15 = (bf16[128,512]{1,0:T(8,128)(2,1)S(1)}, bf16[128,512]{1,0:T(8,128)(2,1)S(1)}, u32[]{:S(2)}, u32[]{:S(2)}) collective-permute-start(bf16[128,512]{1,0:T(8,128)(2,1)S(1)} %get-tuple-element.49.refs_2_), channel_id=1, source_target_pairs={{0,1},{1,0},{2,3},{3,2},{4,5},{5,4},{6,7},{7,6},{8,9},{9,8},{10,11... | collective-permute-start | bytes 393224 | tf_op jit(solution)/shard_map/ppermute | solution.py:475
  30.9 1.5 %collective-permute-start.16 = (bf16[128,512]{1,0:T(8,128)(2,1)S(1)}, bf16[128,512]{1,0:T(8,128)(2,1)S(1)}, u32[]{:S(2)}, u32[]{:S(2)}) collective-permute-start(bf16[128,512]{1,0:T(8,128)(2,1)S(1)} %get-tuple-element.50.refs_3_), channel_id=1, source_target_pairs={{0,1},{1,0},{2,3},{3,2},{4,5},{5,4},{6,7},{7,6},{8,9},{9,8},{10,11... | collective-permute-start | bytes 393224 | tf_op jit(solution)/shard_map/ppermute | solution.py:475

commit v4 on v3

--- a/solution.py
+++ b/solution.py
@@ -22,15 +22,24 @@
 
 
 def source(i, k, n):
-    return i ^ k if is_pow2(n) else (i + k) % n
+    return i ^ (-k % n) if is_pow2(n) else (i + k) % n
 
 
 def target(i, k, n):
-    return i ^ k if is_pow2(n) else (i + n - k) % n
+    return i ^ (-k % n) if is_pow2(n) else (i + n - k) % n
+
+
+def exchange(i, j, n):
+    return lax.rem(n - (i ^ j) if is_pow2(n) else j + n - i, n)
 
 
 def inner_pairs(n, inner, k):
     return [(j, j - j % inner + target(j % inner, k, inner)) for j in range(n)]
+
+
+def far_order(outer):
+    order = list(range(1, outer))
+    return order[1::-1] + order[2:]
 
 
 def outer_pairs(n, inner, k):
@@ -188,7 +197,7 @@
     totals, nears = refs[: outer - 1], refs[outer - 1 : outer - 1 + inner]
     outs, state_ref = refs[outer - 1 + inner : -1], refs[-1]
     group = lax.div(lax.axis_index("ctx"), inner)
-    where = [source(group, k, outer) for k in range(1, outer)]
+    where = [source(group, k, outer) for k in far_order(outer)]
     at, (norms, tops, decays) = read_tails(totals, width_k)
     logs = chain_logs(where, tops, decays, group)
     far_top = functools.reduce(jnp.maximum, logs)
@@ -277,7 +286,7 @@
 
 
 def output_kernel(inner, queries_ref, done_ref, lift_ref, *rest):
-    pieces, outs, memory = rest[:inner], rest[inner:-1], rest[-1]
+    pieces, (out_ref, memory) = rest[:inner], rest[inner:]
     member = lax.rem(lax.axis_index("ctx"), inner)
     piece = memory.shape[0] // inner
     for k in range(inner):
@@ -286,39 +295,56 @@
             memory[pl.ds(start, piece), i * LANES : (i + 1) * LANES] = pieces[k][
                 i * piece : (i + 1) * piece, :
             ]
-    rows = outs[0].shape[0]
-    for i, out_ref in enumerate(outs):
-        here = slice(i * rows, (i + 1) * rows)
+    for i in range(queries_ref.shape[0] // LANES):
+        here = slice(i * LANES, (i + 1) * LANES)
         num_out = jnp.dot(queries_ref[here, :], memory[...], preferred_element_type=jnp.float32)
         column = lift_ref[here, :]
         for j, block in enumerate(lane_blocks(num_out)):
             there = slice(j * LANES, (j + 1) * LANES)
-            out_ref[:, there] = (done_ref[here, there] + column * block).astype(jnp.bfloat16)
-
-
-def project_kernel(heads, orders, rows, chunks, *refs):
-    gated = [refs[k * chunks : (k + 1) * chunks] for k in range(heads)]
-    bufs, (out_hbm, weights, held, sems) = refs[heads * chunks : -4], refs[-4:]
+            out_ref[here, there] = (done_ref[here, there] + column * block).astype(jnp.bfloat16)
+
+
+def own_kernel(heads, orders, rows, gated_ref, *refs):
+    bufs, (part_ref, other_ref, mine) = refs[:-3], refs[-3:]
     place, head = lax.axis_index("ctx"), lax.axis_index("head")
+    width = mine.shape[0]
+    each = width // rows
     at = 0
     for buf in bufs:
         for s in range(buf.shape[0] // rows):
             even, odd = (order[at] for order in orders)
             block = place ^ (even if even == odd else jnp.where(head % 2 == 0, even, odd))
-            start = pl.multiple_of(block * rows, rows)
-            weights[pl.ds(start, rows), :] = buf[s * rows : (s + 1) * rows, :]
+            owner, start = lax.div(block, each), pl.multiple_of(lax.rem(block, each) * rows, rows)
+            here = buf.at[s * rows : (s + 1) * rows, :]
+
+            @pl.when(owner == head)
+            def _():
+                mine[pl.ds(start, rows), :] = here[...]
+
+            @pl.when(owner != head)
+            def _():
+                away = (exchange(head, owner, heads) - 1) * width + start
+                other_ref[pl.ds(pl.multiple_of(away, rows), rows), :] = here[...]
+
             at += 1
-    tok, width = gated[0][0].shape
+    part_ref[...] = jnp.dot(gated_ref[...], mine[...], preferred_element_type=jnp.float32)
+
+
+def others_kernel(part_ref, other_ref, *refs):
+    gated, (out_hbm, held, sems) = refs[:-3], refs[-3:]
+    width = gated[0].shape[1]
+    steps, rows = held.shape[:2]
     copies = []
-    for c in range(chunks):
-        total = 0.0
-        for k in range(heads):
-            start = pl.multiple_of(source(head, k, heads) * width, width)
-            part = weights[pl.ds(start, width), :]
-            total = total + jnp.dot(gated[k][c][...], part, preferred_element_type=jnp.float32)
+    for c in range(steps):
+        here = slice(c * rows, (c + 1) * rows)
+        total = part_ref[here, :]
+        for k, g in enumerate(gated):
+            part = other_ref[k * width : (k + 1) * width, :]
+            total = total + jnp.dot(g[here, :], part, preferred_element_type=jnp.float32)
         held[c, :, :] = total.astype(jnp.bfloat16)
-        to = out_hbm.at[pl.ds(c * tok, tok), :]
-        copies.append(pltpu.make_async_copy(held.at[c], to, sems.at[c]))
+        copies.append(
+            pltpu.make_async_copy(held.at[c], out_hbm.at[pl.ds(c * rows, rows), :], sems.at[c])
+        )
         copies[-1].start()
     for copy in copies:
         copy.wait()
@@ -359,7 +385,7 @@
 
 
 def doubling_steps(n_ctx):
-    assert is_pow2(n_ctx) and n_ctx >= 4
+    assert is_pow2(n_ctx) and n_ctx >= 16
     return [1 << b for b in reversed(range(2, n_ctx.bit_length() - 1))]
 
 
@@ -389,20 +415,13 @@
             lax.ppermute(sent[k], "ctx", inner_pairs(n_ctx, inner, k)) for k in range(1, inner)
         ]
 
-    steps = doubling_steps(n_ctx)
-    order = [0]
-    w_parts = [w_out]
-
-    def double(after):
-        held = w_parts[0] if len(w_parts) == 1 else join(w_parts, after)
-        if not steps:
-            return held
-        step = steps.pop(0)
-        w_parts[:] = [held, over_ctx(held, step, step)]
+    *steps, last = doubling_steps(n_ctx)
+    order, halves = [0], [w_out]
+    for step in steps:
+        held = halves[0] if len(halves) == 1 else join(halves)
+        halves = [held, over_ctx(held, step, step)]
         order.extend([x ^ step for x in order])
-        return held
-
-    double([])
+
     gates, *sends = call(
         functools.partial(summary_kernel, inner),
         [shape((2 * gate_rows, LANES), f32)] + [message] * inner,
@@ -419,71 +438,88 @@
         plain=(0, 1, 2, 3),
     )
     blocks = in_group(sends)
-    held = double([gates])
+
+    one, other = (1, 2), (2, 1)
+    early = join(halves, [gates])
+    late = over_ctx(early, last, last)
+    first_early = over_ctx(early, *one)
+    waited = join([gates], [early], 8.0)
+    total = call(
+        functools.partial(group_total_kernel, inner, width_k), message, blocks, after=[waited]
+    )
+    totals = [
+        lax.ppermute(total, "ctx", outer_pairs(n_ctx, inner, k)) for k in far_order(outer)
+    ]
+    late = join([late], [total])
+    first_late = over_ctx(late, *one)
+    *nears, stats = call(
+        functools.partial(near_kernel, inner, width_k),
+        [shape((memory_rows, LANES), f32)] * inner + [shape((inner, 8, LANES), f32)],
+        blocks,
+        micros=8.0,
+        after=[late],
+    )
+    held = join([early, late], [stats])
+    second = over_ctx(held, *other)
+    third_early = over_ctx(join([first_early], [stats]), *other)
+    third_late = over_ctx(first_late, *other)
+    orders = []
+    for a, b in zip(one, other):
+        halves = [order, [x ^ last for x in order]]
+        orders.append(
+            [x ^ s for s in (0, b) for half in halves for x in half]
+            + [x ^ s for half in halves for s in (a, a ^ b) for x in half]
+        )
+
+    *prefixes, state = call(
+        functools.partial(far_kernel, inner, outer, width_k),
+        [shape((memory_rows, LANES), bf16)] * inner + [shape((8, LANES), f32)],
+        (stats, *totals, *nears),
+        micros=8.0,
+        after=[held],
+    )
+    parts = in_group(prefixes)
     num_in, stats_in = call(
         inside_kernel,
         [shape((tok, width_v), f32), shape((3 * gate_rows, LANES), f32)],
         (gates, gate_out, queries, keys, values),
         micros=8.0,
-        after=[held],
-    )
-    total = call(
-        functools.partial(group_total_kernel, inner, width_k), message, blocks, after=[stats_in]
-    )
-    totals = [
-        lax.ppermute(total, "ctx", outer_pairs(n_ctx, inner, k)) for k in range(1, outer)
-    ]
-    while steps:
-        double([total])
-    held = double([total])
-
-    one, other = (1, 2), (2, 1)
-    first = over_ctx(held, *one)
-    *nears, stats = call(
-        functools.partial(near_kernel, inner, width_k),
-        [shape((memory_rows, LANES), f32)] * inner + [shape((inner, 8, LANES), f32)],
-        blocks,
-        micros=8.0,
-        after=[held, stats_in],
-    )
-    again = join([held], [stats])
-    second, third = over_ctx(again, *other), over_ctx(first, *other)
-    orders = [[x ^ s for s in (0, a, b, a ^ b) for x in order] for a, b in zip(one, other)]
-    *prefixes, state = call(
-        functools.partial(far_kernel, inner, outer, width_k),
-        [shape((memory_rows, LANES), bf16)] * inner + [shape((8, LANES), f32)],
-        (stats, *totals, *nears),
-        micros=8.0,
-    )
-    parts = in_group(prefixes)
+        after=[state, third_early],
+    )
     done, lift = call(
         rescale_kernel,
         [shape((tok, width_v), f32), shape((tok, LANES), f32)],
         (state, gates, stats_in, queries, num_in),
         micros=8.0,
-        after=[first, second],
-    )
-    chunks = tok // LANES
+        after=[first_late, third_early],
+    )
     gated = call(
         functools.partial(output_kernel, inner),
-        [shape((LANES, width_v), bf16)] * chunks,
+        shape((tok, width_v), bf16),
         (queries, done, lift, *parts),
         [pltpu.VMEM((width_k, width_v), bf16)],
         micros=0.1,
+        after=[second],
     )
     others = [
-        lax.ppermute(g, "head", [(j, target(j, k, n_head)) for j in range(n_head)])
+        lax.ppermute(gated, "head", [(j, target(j, k, n_head)) for j in range(n_head)])
         for k in range(1, n_head)
-        for g in gated
     ]
+    cols_out = w_out.shape[1]
+    part, other_rows = call(
+        functools.partial(own_kernel, n_head, orders, w_out.shape[0]),
+        [shape((tok, cols_out), f32), shape(((n_head - 1) * width_v, cols_out), bf16)],
+        (gated, held, second, first_early, third_early, first_late, third_late),
+        [pltpu.VMEM((width_v, cols_out), bf16)],
+        micros=5.0,
+    )
     return call(
-        functools.partial(project_kernel, n_head, orders, w_out.shape[0], chunks),
-        shape((tok, w_out.shape[1]), bf16),
-        (*gated, *others, held, first, second, third),
+        others_kernel,
+        shape((tok, cols_out), bf16),
+        (part, other_rows, *others),
         [
-            pltpu.VMEM((n_ctx * w_out.shape[0], w_out.shape[1]), bf16),
-            pltpu.VMEM((chunks, LANES, w_out.shape[1]), bf16),
-            pltpu.SemaphoreType.DMA((chunks,)),
+            pltpu.VMEM((gate_rows, LANES, cols_out), bf16),
+            pltpu.SemaphoreType.DMA((gate_rows,)),
         ],
         micros=1.0,
         to_hbm=True,

time: 34.1 us -> 32.8 us (0.962)
  waiting for transfers between devices: 7.21 us -> 3.83 us
  starting transfers between devices: 21.3 us -> 23 us
  Pallas kernels: 5.32 us -> 5.7 us
    ppermute x5 -> x7, starting transfers between devices: 8.62 us -> 11.3 us  [over_ctx(): return lax.ppermute(held, ('ctx', 'head'), pairs)]
    ppermute x6, waiting for transfers between devices: 3.93 us -> 1.93 us  [in_group(): lax.ppermute(sent[k], 'ctx', inner_pairs(n_ctx, inner, k))]
    ppermute x3, waiting for transfers between devices: 2.14 us -> 0.7 us  [local(): lax.ppermute(total, 'ctx', outer_pairs(n_ctx, inner, k))]
    ppermute x4 -> x1, starting transfers between devices: 1.08 us -> 0.07 us  [local(): lax.ppermute(gated, 'head', [(j, target(j, k, n_head)) for j in range(n_h...]
    ppermute x5 -> x7, waiting for transfers between devices: 0.12 us -> 0.96 us  [over_ctx(): return lax.ppermute(held, ('ctx', 'head'), pairs)]
    ppermute x4 -> x1, waiting for transfers between devices: 1.02 us -> 0.24 us  [local(): lax.ppermute(gated, 'head', [(j, target(j, k, n_head)) for j in range(n_h...]
    pallas_call x11 -> x14, Pallas kernels: 5.32 us -> 5.7 us  [call(): pl.pallas_call(lambda *refs: kernel(*refs[skip:]), out_shape=out_shape, i...]
  transfers between devices with their start and end apart: 18 -> 17, of which waited for: 11 -> 5; matrix products, arithmetic and copies ran while one was open for 0% -> 0% of each run, Pallas kernels for 11% -> 14%
where the time goes in v4:
time: 32.8 us; the launch traced here: 32.7 us
  starting transfers between devices  23 us (70%)
  Pallas kernels  5.7 us (17%)
  waiting for transfers between devices  3.83 us (12%)
    ppermute x7, starting transfers between devices, over_ctx(): return lax.ppermute(held, ('ctx', 'head'), pairs)  11.3 us
    ppermute x6, starting transfers between devices, in_group(): lax.ppermute(sent[k], 'ctx', inner_pairs(n_ctx, inner, k))  7.21 us
    pallas_call x14, Pallas kernels, call(): pl.pallas_call(lambda *refs: kernel(*refs[skip:]), out_shape=out_shape, i...  5.7 us
    ppermute x3, starting transfers between devices, local(): lax.ppermute(total, 'ctx', outer_pairs(n_ctx, inner, k))  4.45 us
    ppermute x6, waiting for transfers between devices, in_group(): lax.ppermute(sent[k], 'ctx', inner_pairs(n_ctx, inner, k))  1.93 us
    ppermute x7, waiting for transfers between devices, over_ctx(): return lax.ppermute(held, ('ctx', 'head'), pairs)  0.96 us
    ppermute x3, waiting for transfers between devices, local(): lax.ppermute(total, 'ctx', outer_pairs(n_ctx, inner, k))  0.7 us
  transfers between devices with their start and end apart: 17, of which 5 were waited for; matrix products, arithmetic and copies ran while one was open for 0% of the time, Pallas kernels for 14%

profile of v4, /device:TPU:0, one launch (start us, length us, event | category | flops | bytes accessed | tf_op | source)
XLA Modules:
  0.0 32.7 jit_solution(4634545340203623757)
XLA Ops:
  0.0 4.0 %collective-permute-start = (bf16[64,512]{1,0:T(8,128)(2,1)}, bf16[64,512]{1,0:T(8,128)(2,1)S(1)}, u32[]{:S(2)}, u32[]{:S(2)}) collective-permute-start(bf16[64,512]{1,0:T(8,128)(2,1)} %refs_1_.2), channel_id=1, source_target_pairs={{0,16},{1,17},{2,18},{3,19},{4,20},{5,21},{6,22},{7,23},{8,24},{9,... | collective-permute-start | bytes 196616 | tf_op jit(solution)/shard_map/ppermute | solution.py:411
  4.0 0.0 copy-start.3
  4.0 1.6 %shard_map.73 = (f32[8,128]{1,0:T(8,128)S(1)}, bf16[272,128]{1,0:T(8,128)(2,1)S(1)}, bf16[272,128]{1,0:T(8,128)(2,1)S(1)}, bf16[272,128]{1,0:T(8,128)(2,1)S(1)}, bf16[272,128]{1,0:T(8,128)(2,1)S(1)}) custom-call(f32[4,128]{1,0:T(4,128)} %bitcast.4, f32[4,128]{1,0:T(4,128)} %bitcast.5, bf16[512,256]{1,0:T(8,128)(2,1)} %refs_5_.2, bf16[512,512]{1,0:T(8,128)(2,1)} %refs_6_.1), custom_call_target="tpu_custom_call" | custom-call | flops 2200000000 | bytes 7400000 | tf_op jit(solution)/shard_map/pallas_call | solution.py:365
  5.7 2.5 %collective-permute-start.1 = (bf16[272,128]{1,0:T(8,128)(2,1)S(1)}, bf16[272,128]{1,0:T(8,128)(2,1)S(1)}, u32[]{:S(2)}, u32[]{:S(2)}) collective-permute-start(bf16[272,128]{1,0:T(8,128)(2,1)S(1)} %get-tuple-element.28), channel_id=1, source_target_pairs={{0,6},{2,4},{4,2},{6,0},{8,14},{10,12},{12,10},{14,8},{16,22},{18,... | collective-permute-start | bytes 208904 | tf_op jit(solution)/shard_map/ppermute | solution.py:415
  8.2 0.5 %collective-permute-start.2 = (bf16[272,128]{1,0:T(8,128)(2,1)S(1)}, bf16[272,128]{1,0:T(8,128)(2,1)S(1)}, u32[]{:S(2)}, u32[]{:S(2)}) collective-permute-start(bf16[272,128]{1,0:T(8,128)(2,1)S(1)} %get-tuple-element.29), channel_id=1, source_target_pairs={{0,4},{2,6},{4,0},{6,2},{8,12},{10,14},{12,8},{14,10},{16,20},{18,... | collective-permute-start | bytes 208904 | tf_op jit(solution)/shard_map/ppermute | solution.py:415
  8.7 0.5 %collective-permute-start.3 = (bf16[272,128]{1,0:T(8,128)(2,1)S(1)}, bf16[272,128]{1,0:T(8,128)(2,1)S(1)}, u32[]{:S(2)}, u32[]{:S(2)}) collective-permute-start(bf16[272,128]{1,0:T(8,128)(2,1)S(1)} %get-tuple-element.30), channel_id=1, source_target_pairs={{0,2},{2,0},{4,6},{6,4},{8,10},{10,8},{12,14},{14,12},{16,18},{18,... | collective-permute-start | bytes 208904 | tf_op jit(solution)/shard_map/ppermute | solution.py:415
  9.2 0.0 collective-permute-done.refs_2_
  9.3 0.0 copy-done.3
  9.3 1.6 %collective-permute-start.4 = (bf16[128,512]{1,0:T(8,128)(2,1)S(1)}, bf16[128,512]{1,0:T(8,128)(2,1)S(1)}, u32[]{:S(2)}, u32[]{:S(2)}) collective-permute-start(bf16[128,512]{1,0:T(8,128)(2,1)S(1)} %shard_map.74.refs_0_.refs_1_), channel_id=1, source_target_pairs={{0,8},{1,9},{2,10},{3,11},{4,12},{5,13},{6,14},{7,15},{8,0},{9,1},... | collective-permute-start | bytes 393224 | tf_op jit(solution)/shard_map/ppermute | solution.py:411
  10.9 1.5 %collective-permute-start.7 = (bf16[128,512]{1,0:T(8,128)(2,1)S(1)}, bf16[128,512]{1,0:T(8,128)(2,1)S(1)}, u32[]{:S(2)}, u32[]{:S(2)}) collective-permute-start(bf16[128,512]{1,0:T(8,128)(2,1)S(1)} %shard_map.74.refs_0_.refs_1_), channel_id=1, source_target_pairs={{0,2},{1,5},{2,0},{3,7},{4,6},{5,1},{6,4},{7,3},{8,10},{9,13},{10,... | collective-permute-start | bytes 393224 | tf_op jit(solution)/shard_map/ppermute | solution.py:411
  12.4 0.0 collective-permute-done.1.refs_2_
  12.4 0.7 %collective-permute-done.2.refs_3_ = bf16[272,128]{1,0:T(8,128)(2,1)S(1)} collective-permute-done((bf16[272,128]{1,0:T(8,128)(2,1)S(1)}, bf16[272,128]{1,0:T(8,128)(2,1)S(1)}, u32[]{:S(2)}, u32[]{:S(2)}) %collective-permute-start.2) | collective-permute-done | bytes 69664 | tf_op jit(solution)/shard_map/ppermute | solution.py:415
  13.1 0.0 collective-permute-done.3.refs_4_
  13.1 0.1 shard_map.76.refs_0_
  13.2 1.4 %collective-permute-start.10 = (bf16[272,128]{1,0:T(8,128)(2,1)S(1)}, bf16[272,128]{1,0:T(8,128)(2,1)S(1)}, u32[]{:S(2)}, u32[]{:S(2)}) collective-permute-start(bf16[272,128]{1,0:T(8,128)(2,1)S(1)} %shard_map.76.refs_0_), channel_id=1, source_target_pairs={{0,24},{2,26},{4,28},{6,30},{8,16},{10,18},{12,20},{14,22},{16,8},... | collective-permute-start | bytes 208904 | tf_op jit(solution)/shard_map/ppermute | solution.py:451
  14.5 0.6 %collective-permute-start.11 = (bf16[272,128]{1,0:T(8,128)(2,1)S(1)}, bf16[272,128]{1,0:T(8,128)(2,1)S(1)}, u32[]{:S(2)}, u32[]{:S(2)}) collective-permute-start(bf16[272,128]{1,0:T(8,128)(2,1)S(1)} %shard_map.76.refs_0_), channel_id=1, source_target_pairs={{0,8},{2,10},{4,12},{6,14},{8,0},{10,2},{12,4},{14,6},{16,24},{18,... | collective-permute-start | bytes 208904 | tf_op jit(solution)/shard_map/ppermute | solution.py:451
  15.1 2.5 %collective-permute-start.9 = (bf16[272,128]{1,0:T(8,128)(2,1)S(1)}, bf16[272,128]{1,0:T(8,128)(2,1)S(1)}, u32[]{:S(2)}, u32[]{:S(2)}) collective-permute-start(bf16[272,128]{1,0:T(8,128)(2,1)S(1)} %shard_map.76.refs_0_), channel_id=1, source_target_pairs={{0,16},{2,18},{4,20},{6,22},{8,24},{10,26},{12,28},{14,30},{16,0},... | collective-permute-start | bytes 208904 | tf_op jit(solution)/shard_map/ppermute | solution.py:451
  17.6 0.0 collective-permute-done.4.refs_1_
  17.7 0.5 %collective-permute-start.6 = (bf16[128,512]{1,0:T(8,128)(2,1)S(1)}, bf16[128,512]{1,0:T(8,128)(2,1)S(1)}, u32[]{:S(2)}, u32[]{:S(2)}) collective-permute-start(bf16[128,512]{1,0:T(8,128)(2,1)S(1)} %shard_map.77.refs_0_.refs_2_), channel_id=1, source_target_pairs={{0,2},{1,5},{2,0},{3,7},{4,6},{5,1},{6,4},{7,3},{8,10},{9,13},{10,... | collective-permute-start | bytes 393224 | tf_op jit(solution)/shard_map/ppermute | solution.py:411
  18.2 0.2 shard_map.78
  18.4 0.0 collective-permute-done.7.refs_1_.refs_3_
  18.5 1.6 %collective-permute-start.8 = (bf16[128,512]{1,0:T(8,128)(2,1)S(1)}, bf16[128,512]{1,0:T(8,128)(2,1)S(1)}, u32[]{:S(2)}, u32[]{:S(2)}) collective-permute-start(bf16[128,512]{1,0:T(8,128)(2,1)S(1)} %shard_map.80), channel_id=1, source_target_pairs={{0,4},{1,3},{2,6},{3,1},{4,0},{5,7},{6,2},{7,5},{8,12},{9,11},{10,... | collective-permute-start | bytes 393224 | tf_op jit(solution)/shard_map/ppermute | solution.py:411
  20.1 0.0 collective-permute-done.10.refs_3_
  20.1 0.9 %collective-permute-start.5 = (bf16[256,512]{1,0:T(8,128)(2,1)S(1)}, bf16[256,512]{1,0:T(8,128)(2,1)S(1)}, u32[]{:S(2)}, u32[]{:S(2)}) collective-permute-start(bf16[256,512]{1,0:T(8,128)(2,1)S(1)} %shard_map.79.refs_0_.refs_1_), channel_id=1, source_target_pairs={{0,4},{1,3},{2,6},{3,1},{4,0},{5,7},{6,2},{7,5},{8,12},{9,11},{10,... | collective-permute-start | bytes 786440 | tf_op jit(solution)/shard_map/ppermute | solution.py:411
  21.0 0.0 collective-permute-done.11.refs_4_
  21.0 0.7 %collective-permute-done.9.refs_2_ = bf16[272,128]{1,0:T(8,128)(2,1)S(1)} collective-permute-done((bf16[272,128]{1,0:T(8,128)(2,1)S(1)}, bf16[272,128]{1,0:T(8,128)(2,1)S(1)}, u32[]{:S(2)}, u32[]{:S(2)}) %collective-permute-start.9) | collective-permute-done | bytes 69664 | tf_op jit(solution)/shard_map/ppermute | solution.py:451
  21.7 0.0 copy-start
  21.7 0.0 copy-start.1
  21.7 0.0 copy-start.2
  21.7 0.1 shard_map.81
  21.8 1.5 %collective-permute-start.12 = (bf16[256,128]{1,0:T(8,128)(2,1)S(1)}, bf16[256,128]{1,0:T(8,128)(2,1)S(1)}, u32[]{:S(2)}, u32[]{:S(2)}) collective-permute-start(bf16[256,128]{1,0:T(8,128)(2,1)S(1)} %get-tuple-element.42), channel_id=1, source_target_pairs={{0,6},{2,4},{4,2},{6,0},{8,14},{10,12},{12,10},{14,8},{16,22},{18,... | collective-permute-start | bytes 196616 | tf_op jit(solution)/shard_map/ppermute | solution.py:415
  23.4 0.6 %collective-permute-start.13 = (bf16[256,128]{1,0:T(8,128)(2,1)S(1)}, bf16[256,128]{1,0:T(8,128)(2,1)S(1)}, u32[]{:S(2)}, u32[]{:S(2)}) collective-permute-start(bf16[256,128]{1,0:T(8,128)(2,1)S(1)} %get-tuple-element.43), channel_id=1, source_target_pairs={{0,4},{2,6},{4,0},{6,2},{8,12},{10,14},{12,8},{14,10},{16,20},{18,... | collective-permute-start | bytes 196616 | tf_op jit(solution)/shard_map/ppermute | solution.py:415
  23.9 0.0 collective-permute-done.8.refs_1_.refs_4_
  23.9 0.0 copy-start.4
  23.9 1.5 %collective-permute-start.14 = (bf16[256,128]{1,0:T(8,128)(2,1)S(1)}, bf16[256,128]{1,0:T(8,128)(2,1)S(1)}, u32[]{:S(2)}, u32[]{:S(2)}) collective-permute-start(bf16[256,128]{1,0:T(8,128)(2,1)S(1)} %get-tuple-element.44), channel_id=1, source_target_pairs={{0,2},{2,0},{4,6},{6,4},{8,10},{10,8},{12,14},{14,12},{16,18},{18,... | collective-permute-start | bytes 196616 | tf_op jit(solution)/shard_map/ppermute | solution.py:415
  25.5 0.0 collective-permute-done.6.refs_0_.refs_5_
  25.5 1.1 %collective-permute-start.15 = (bf16[128,512]{1,0:T(8,128)(2,1)S(1)}, bf16[128,512]{1,0:T(8,128)(2,1)S(1)}, u32[]{:S(2)}, u32[]{:S(2)}) collective-permute-start(bf16[128,512]{1,0:T(8,128)(2,1)S(1)} %collective-permute-done.6.refs_0_.refs_5_), channel_id=1, source_target_pairs={{0,4},{1,3},{2,6},{3,1},{4,0},{5,7},{6,2},{7,5},{8,12},{9,11},{10,... | collective-permute-start | bytes 393224 | tf_op jit(solution)/shard_map/ppermute | solution.py:411
  26.6 0.0 copy-done
  26.6 0.0 copy-done.1
  26.6 0.0 copy-done.2
  26.6 0.0 copy-done.4
  26.6 0.9 %shard_map.82 = (f32[512,512]{1,0:T(8,128)S(1)}, f32[12,128]{1,0:T(8,128)S(1)}) custom-call(f32[8,128]{1,0:T(8,128)S(1)} %get-tuple-element.36.refs_0_.refs_2_, bf16[128,512]{1,0:T(8,128)(2,1)S(1)} %collective-permute-done.8.refs_1_.refs_4_, f32[8,128]{1,0:T(8,128)S(1)} %get-tuple-element.26.refs_0_.refs_1_.refs_2_.refs_3_, f32[4,128]{1,0:T(4,128)S(1)} %bitcast.3, ...), custom_call_target="tpu_custom_call" | custom-call | flops 8800000000 | bytes 29600000 | tf_op jit(solution)/shard_map/pallas_call | solution.py:365
  27.5 0.4 %shard_map.83 = (f32[512,512]{1,0:T(8,128)S(1)}, f32[512,128]{1,0:T(8,128)S(1)}) custom-call(bf16[128,512]{1,0:T(8,128)(2,1)S(1)} %collective-permute-done.6.refs_0_.refs_5_, bf16[128,512]{1,0:T(8,128)(2,1)S(1)} %collective-permute-done.8.refs_1_.refs_4_, f32[8,128]{1,0:T(8,128)S(1)} %get-tuple-element.36.refs_0_.refs_2_, ...), custom_call_target="tpu_custom_call" | custom-call | flops 8800000000 | bytes 29600000 | tf_op jit(solution)/shard_map/pallas_call | solution.py:365
  27.9 0.0 collective-permute-done.12.refs_5_
  27.9 1.3 %collective-permute-done.13.refs_6_ = bf16[256,128]{1,0:T(8,128)(2,1)S(1)} collective-permute-done((bf16[256,128]{1,0:T(8,128)(2,1)S(1)}, bf16[256,128]{1,0:T(8,128)(2,1)S(1)}, u32[]{:S(2)}, u32[]{:S(2)}) %collective-permute-start.13) | collective-permute-done | bytes 65568 | tf_op jit(solution)/shard_map/ppermute | solution.py:415
  29.2 0.0 collective-permute-done.14.refs_7_
  29.2 0.0 collective-permute-done.5.refs_0_.refs_2_
  29.2 0.4 %shard_map.84.refs_0_ = bf16[512,512]{1,0:T(8,128)(2,1)S(1)} custom-call(bf16[256,512]{1,0:T(8,128)(2,1)S(1)} %collective-permute-done.5.refs_0_.refs_2_, bf16[512,256]{1,0:T(8,128)(2,1)S(1)} %copy-done, f32[512,512]{1,0:T(8,128)S(1)} %get-tuple-element.39.refs_2_, f32[512,128]{1,0:T(8,128)S(1)} %get-tuple-element.40.refs_3_, ...), custom_call_target="tpu_custom_call" | custom-call | flops 110000000 | bytes 370000 | tf_op jit(solution)/shard_map/pallas_call | solution.py:365
  29.5 0.1 collective-permute-start.16
  29.6 0.9 %collective-permute-done.15.refs_6_ = bf16[128,512]{1,0:T(8,128)(2,1)S(1)} collective-permute-done((bf16[128,512]{1,0:T(8,128)(2,1)S(1)}, bf16[128,512]{1,0:T(8,128)(2,1)S(1)}, u32[]{:S(2)}, u32[]{:S(2)}) %collective-permute-start.15) | collective-permute-done | bytes 131104 | tf_op jit(solution)/shard_map/ppermute | solution.py:411
  30.6 0.7 %shard_map.85 = (f32[512,512]{1,0:T(8,128)S(1)}, bf16[512,512]{1,0:T(8,128)(2,1)S(1)}) custom-call(bf16[512,512]{1,0:T(8,128)(2,1)S(1)} %shard_map.84.refs_0_, bf16[256,512]{1,0:T(8,128)(2,1)S(1)} %shard_map.79.refs_0_.refs_1_, bf16[256,512]{1,0:T(8,128)(2,1)S(1)} %collective-permute-done.5.refs_0_.refs_2_, ...), custom_call_target="tpu_custom_call" | custom-call | flops 5500000256 | bytes 18500000 | tf_op jit(solution)/shard_map/pallas_call | solution.py:365
  31.3 0.2 collective-permute-done.16.refs_2_
  31.5 1.1 %shard_map.86 = bf16[512,512]{1,0:T(8,128)(2,1)} custom-call(f32[512,512]{1,0:T(8,128)S(1)} %get-tuple-element.45.refs_0_, bf16[512,512]{1,0:T(8,128)(2,1)S(1)} %get-tuple-element.46.refs_1_, bf16[512,512]{1,0:T(8,128)(2,1)S(1)} %collective-permute-done.16.refs_2_), custom_call_target="tpu_custom_call" | custom-call | flops 1100000000 | bytes 3700000 | tf_op jit(solution)/shard_map/pallas_call | solution.py:365
  (5 shorter events, 0.0 us)
Async XLA Ops:
  0.0 9.3 %collective-permute-start = (bf16[64,512]{1,0:T(8,128)(2,1)}, bf16[64,512]{1,0:T(8,128)(2,1)S(1)}, u32[]{:S(2)}, u32[]{:S(2)}) collective-permute-start(bf16[64,512]{1,0:T(8,128)(2,1)} %refs_1_.2), channel_id=1, source_target_pairs={{0,16},{1,17},{2,18},{3,19},{4,20},{5,21},{6,22},{7,23},{8,24},{9,... | collective-permute-start | bytes 196616 | tf_op jit(solution)/shard_map/ppermute | solution.py:411
  4.0 5.2 %copy-start.3 = (bf16[64,512]{1,0:T(8,128)(2,1)S(1)}, bf16[64,512]{1,0:T(8,128)(2,1)}, u32[]{:S(2)}) copy-start(bf16[64,512]{1,0:T(8,128)(2,1)} %refs_1_.2) | copy-start | bytes 196612
  5.7 6.7 %collective-permute-start.1 = (bf16[272,128]{1,0:T(8,128)(2,1)S(1)}, bf16[272,128]{1,0:T(8,128)(2,1)S(1)}, u32[]{:S(2)}, u32[]{:S(2)}) collective-permute-start(bf16[272,128]{1,0:T(8,128)(2,1)S(1)} %get-tuple-element.28), channel_id=1, source_target_pairs={{0,6},{2,4},{4,2},{6,0},{8,14},{10,12},{12,10},{14,8},{16,22},{18,... | collective-permute-start | bytes 208904 | tf_op jit(solution)/shard_map/ppermute | solution.py:415
  8.2 4.9 %collective-permute-start.2 = (bf16[272,128]{1,0:T(8,128)(2,1)S(1)}, bf16[272,128]{1,0:T(8,128)(2,1)S(1)}, u32[]{:S(2)}, u32[]{:S(2)}) collective-permute-start(bf16[272,128]{1,0:T(8,128)(2,1)S(1)} %get-tuple-element.29), channel_id=1, source_target_pairs={{0,4},{2,6},{4,0},{6,2},{8,12},{10,14},{12,8},{14,10},{16,20},{18,... | collective-permute-start | bytes 208904 | tf_op jit(solution)/shard_map/ppermute | solution.py:415
  8.7 4.4 %collective-permute-start.3 = (bf16[272,128]{1,0:T(8,128)(2,1)S(1)}, bf16[272,128]{1,0:T(8,128)(2,1)S(1)}, u32[]{:S(2)}, u32[]{:S(2)}) collective-permute-start(bf16[272,128]{1,0:T(8,128)(2,1)S(1)} %get-tuple-element.30), channel_id=1, source_target_pairs={{0,2},{2,0},{4,6},{6,4},{8,10},{10,8},{12,14},{14,12},{16,18},{18,... | collective-permute-start | bytes 208904 | tf_op jit(solution)/shard_map/ppermute | solution.py:415
  9.3 8.4 %collective-permute-start.4 = (bf16[128,512]{1,0:T(8,128)(2,1)S(1)}, bf16[128,512]{1,0:T(8,128)(2,1)S(1)}, u32[]{:S(2)}, u32[]{:S(2)}) collective-permute-start(bf16[128,512]{1,0:T(8,128)(2,1)S(1)} %shard_map.74.refs_0_.refs_1_), channel_id=1, source_target_pairs={{0,8},{1,9},{2,10},{3,11},{4,12},{5,13},{6,14},{7,15},{8,0},{9,1},... | collective-permute-start | bytes 393224 | tf_op jit(solution)/shard_map/ppermute | solution.py:411
  10.9 7.5 %collective-permute-start.7 = (bf16[128,512]{1,0:T(8,128)(2,1)S(1)}, bf16[128,512]{1,0:T(8,128)(2,1)S(1)}, u32[]{:S(2)}, u32[]{:S(2)}) collective-permute-start(bf16[128,512]{1,0:T(8,128)(2,1)S(1)} %shard_map.74.refs_0_.refs_1_), channel_id=1, source_target_pairs={{0,2},{1,5},{2,0},{3,7},{4,6},{5,1},{6,4},{7,3},{8,10},{9,13},{10,... | collective-permute-start | bytes 393224 | tf_op jit(solution)/shard_map/ppermute | solution.py:411
  13.2 6.9 %collective-permute-start.10 = (bf16[272,128]{1,0:T(8,128)(2,1)S(1)}, bf16[272,128]{1,0:T(8,128)(2,1)S(1)}, u32[]{:S(2)}, u32[]{:S(2)}) collective-permute-start(bf16[272,128]{1,0:T(8,128)(2,1)S(1)} %shard_map.76.refs_0_), channel_id=1, source_target_pairs={{0,24},{2,26},{4,28},{6,30},{8,16},{10,18},{12,20},{14,22},{16,8},... | collective-permute-start | bytes 208904 | tf_op jit(solution)/shard_map/ppermute | solution.py:451
  14.5 6.4 %collective-permute-start.11 = (bf16[272,128]{1,0:T(8,128)(2,1)S(1)}, bf16[272,128]{1,0:T(8,128)(2,1)S(1)}, u32[]{:S(2)}, u32[]{:S(2)}) collective-permute-start(bf16[272,128]{1,0:T(8,128)(2,1)S(1)} %shard_map.76.refs_0_), channel_id=1, source_target_pairs={{0,8},{2,10},{4,12},{6,14},{8,0},{10,2},{12,4},{14,6},{16,24},{18,... | collective-permute-start | bytes 208904 | tf_op jit(solution)/shard_map/ppermute | solution.py:451
  15.1 6.5 %collective-permute-start.9 = (bf16[272,128]{1,0:T(8,128)(2,1)S(1)}, bf16[272,128]{1,0:T(8,128)(2,1)S(1)}, u32[]{:S(2)}, u32[]{:S(2)}) collective-permute-start(bf16[272,128]{1,0:T(8,128)(2,1)S(1)} %shard_map.76.refs_0_), channel_id=1, source_target_pairs={{0,16},{2,18},{4,20},{6,22},{8,24},{10,26},{12,28},{14,30},{16,0},... | collective-permute-start | bytes 208904 | tf_op jit(solution)/shard_map/ppermute | solution.py:451
  17.7 7.8 %collective-permute-start.6 = (bf16[128,512]{1,0:T(8,128)(2,1)S(1)}, bf16[128,512]{1,0:T(8,128)(2,1)S(1)}, u32[]{:S(2)}, u32[]{:S(2)}) collective-permute-start(bf16[128,512]{1,0:T(8,128)(2,1)S(1)} %shard_map.77.refs_0_.refs_2_), channel_id=1, source_target_pairs={{0,2},{1,5},{2,0},{3,7},{4,6},{5,1},{6,4},{7,3},{8,10},{9,13},{10,... | collective-permute-start | bytes 393224 | tf_op jit(solution)/shard_map/ppermute | solution.py:411
  18.5 5.4 %collective-permute-start.8 = (bf16[128,512]{1,0:T(8,128)(2,1)S(1)}, bf16[128,512]{1,0:T(8,128)(2,1)S(1)}, u32[]{:S(2)}, u32[]{:S(2)}) collective-permute-start(bf16[128,512]{1,0:T(8,128)(2,1)S(1)} %shard_map.80), channel_id=1, source_target_pairs={{0,4},{1,3},{2,6},{3,1},{4,0},{5,7},{6,2},{7,5},{8,12},{9,11},{10,... | collective-permute-start | bytes 393224 | tf_op jit(solution)/shard_map/ppermute | solution.py:411
  20.1 9.1 %collective-permute-start.5 = (bf16[256,512]{1,0:T(8,128)(2,1)S(1)}, bf16[256,512]{1,0:T(8,128)(2,1)S(1)}, u32[]{:S(2)}, u32[]{:S(2)}) collective-permute-start(bf16[256,512]{1,0:T(8,128)(2,1)S(1)} %shard_map.79.refs_0_.refs_1_), channel_id=1, source_target_pairs={{0,4},{1,3},{2,6},{3,1},{4,0},{5,7},{6,2},{7,5},{8,12},{9,11},{10,... | collective-permute-start | bytes 786440 | tf_op jit(solution)/shard_map/ppermute | solution.py:411
  21.7 4.9 %copy-start = (bf16[512,256]{1,0:T(8,128)(2,1)S(1)}, bf16[512,256]{1,0:T(8,128)(2,1)}, u32[]{:S(2)}) copy-start(bf16[512,256]{1,0:T(8,128)(2,1)} %refs_1_.3) | copy-start | bytes 786436
  21.7 4.9 %copy-start.1 = (bf16[512,512]{1,0:T(8,128)(2,1)S(1)}, bf16[512,512]{1,0:T(8,128)(2,1)}, u32[]{:S(2)}) copy-start(bf16[512,512]{1,0:T(8,128)(2,1)} %refs_6_.1) | copy-start | bytes 1572868
  21.7 4.9 %copy-start.2 = (bf16[512,256]{1,0:T(8,128)(2,1)S(1)}, bf16[512,256]{1,0:T(8,128)(2,1)}, u32[]{:S(2)}) copy-start(bf16[512,256]{1,0:T(8,128)(2,1)} %refs_5_.2) | copy-start | bytes 786436
  21.8 6.1 %collective-permute-start.12 = (bf16[256,128]{1,0:T(8,128)(2,1)S(1)}, bf16[256,128]{1,0:T(8,128)(2,1)S(1)}, u32[]{:S(2)}, u32[]{:S(2)}) collective-permute-start(bf16[256,128]{1,0:T(8,128)(2,1)S(1)} %get-tuple-element.42), channel_id=1, source_target_pairs={{0,6},{2,4},{4,2},{6,0},{8,14},{10,12},{12,10},{14,8},{16,22},{18,... | collective-permute-start | bytes 196616 | tf_op jit(solution)/shard_map/ppermute | solution.py:415
  23.4 5.8 %collective-permute-start.13 = (bf16[256,128]{1,0:T(8,128)(2,1)S(1)}, bf16[256,128]{1,0:T(8,128)(2,1)S(1)}, u32[]{:S(2)}, u32[]{:S(2)}) collective-permute-start(bf16[256,128]{1,0:T(8,128)(2,1)S(1)} %get-tuple-element.43), channel_id=1, source_target_pairs={{0,4},{2,6},{4,0},{6,2},{8,12},{10,14},{12,8},{14,10},{16,20},{18,... | collective-permute-start | bytes 196616 | tf_op jit(solution)/shard_map/ppermute | solution.py:415
  23.9 2.7 %copy-start.4 = (f32[512,1]{0,1:T(1,128)S(1)}, f32[512,1]{0,1:T(1,128)}, u32[]{:S(2)}) copy-start(f32[512,1]{0,1:T(1,128)} %param.12) | copy-start | bytes 6148
  23.9 5.2 %collective-permute-start.14 = (bf16[256,128]{1,0:T(8,128)(2,1)S(1)}, bf16[256,128]{1,0:T(8,128)(2,1)S(1)}, u32[]{:S(2)}, u32[]{:S(2)}) collective-permute-start(bf16[256,128]{1,0:T(8,128)(2,1)S(1)} %get-tuple-element.44), channel_id=1, source_target_pairs={{0,2},{2,0},{4,6},{6,4},{8,10},{10,8},{12,14},{14,12},{16,18},{18,... | collective-permute-start | bytes 196616 | tf_op jit(solution)/shard_map/ppermute | solution.py:415
  25.5 5.1 %collective-permute-start.15 = (bf16[128,512]{1,0:T(8,128)(2,1)S(1)}, bf16[128,512]{1,0:T(8,128)(2,1)S(1)}, u32[]{:S(2)}, u32[]{:S(2)}) collective-permute-start(bf16[128,512]{1,0:T(8,128)(2,1)S(1)} %collective-permute-done.6.refs_0_.refs_5_), channel_id=1, source_target_pairs={{0,4},{1,3},{2,6},{3,1},{4,0},{5,7},{6,2},{7,5},{8,12},{9,11},{10,... | collective-permute-start | bytes 393224 | tf_op jit(solution)/shard_map/ppermute | solution.py:411
  29.5 2.0 %collective-permute-start.16 = (bf16[512,512]{1,0:T(8,128)(2,1)S(1)}, bf16[512,512]{1,0:T(8,128)(2,1)S(1)}, u32[]{:S(2)}, u32[]{:S(2)}) collective-permute-start(bf16[512,512]{1,0:T(8,128)(2,1)S(1)} %shard_map.84.refs_0_), channel_id=1, source_target_pairs={{0,1},{1,0},{2,3},{3,2},{4,5},{5,4},{6,7},{7,6},{8,9},{9,8},{10,11... | collective-permute-start | bytes 1572872 | tf_op jit(solution)/shard_map/ppermute | solution.py:505

commit v5 on v4

--- a/solution.py
+++ b/solution.py
@@ -132,11 +132,12 @@
     norms = jnp.dot(three, keys, preferred_element_type=jnp.float32)
     norm = jnp.concatenate(lane_blocks(norms[0:1] + norms[1:2] + norms[2:3]), axis=0)
     copies[3].wait()
-    memory[...] = jnp.dot(scaled, values_ref[...], preferred_element_type=jnp.float32)
+    whole = jnp.dot(scaled, values_ref[...], preferred_element_type=jnp.float32)
+    memory[...] = whole.astype(jnp.bfloat16)
     piece = memory.shape[0] // inner
     for k, out_ref in enumerate(outs):
         start = pl.multiple_of(target(member, k, inner) * piece, piece)
-        wide = memory[pl.ds(start, piece), :].astype(jnp.bfloat16)
+        wide = memory[pl.ds(start, piece), :]
         for i, block in enumerate(lane_blocks(wide)):
             out_ref[i * piece : (i + 1) * piece, :] = block
         write_tail(out_ref, wide.size // LANES, norm, base + top_gain, base)
@@ -430,7 +431,7 @@
             for x in (forget, gate_in, keys, values)
         ],
         [
-            pltpu.VMEM((width_k, width_v), f32),
+            pltpu.VMEM((width_k, width_v), bf16),
             *[pltpu.VMEM(x.shape, x.dtype) for x in (forget, gate_in, keys, values)],
             pltpu.SemaphoreType.DMA((4,)),
         ],

time: 32.8 us -> 32.8 us (level)
  no operation moved by 1% of the time
where the time goes in v5:
time: 32.8 us; the launch traced here: 32.7 us
  starting transfers between devices  23 us (70%)
  Pallas kernels  5.69 us (17%)
  waiting for transfers between devices  3.83 us (12%)
    ppermute x7, starting transfers between devices, over_ctx(): return lax.ppermute(held, ('ctx', 'head'), pairs)  11.3 us
    ppermute x6, starting transfers between devices, in_group(): lax.ppermute(sent[k], 'ctx', inner_pairs(n_ctx, inner, k))  7.21 us
    pallas_call x14, Pallas kernels, call(): pl.pallas_call(lambda *refs: kernel(*refs[skip:]), out_shape=out_shape, i...  5.69 us
    ppermute x3, starting transfers between devices, local(): lax.ppermute(total, 'ctx', outer_pairs(n_ctx, inner, k))  4.45 us
    ppermute x6, waiting for transfers between devices, in_group(): lax.ppermute(sent[k], 'ctx', inner_pairs(n_ctx, inner, k))  1.94 us
    ppermute x7, waiting for transfers between devices, over_ctx(): return lax.ppermute(held, ('ctx', 'head'), pairs)  0.96 us
    ppermute x3, waiting for transfers between devices, local(): lax.ppermute(total, 'ctx', outer_pairs(n_ctx, inner, k))  0.7 us
  transfers between devices with their start and end apart: 17, of which 5 were waited for; matrix products, arithmetic and copies ran while one was open for 0% of the time, Pallas kernels for 14%

profile of v5, /device:TPU:0, one launch (start us, length us, event | category | flops | bytes accessed | tf_op | source)
XLA Modules:
  0.0 32.7 jit_solution(6181563440154104943)
XLA Ops:
  0.0 4.0 %collective-permute-start = (bf16[64,512]{1,0:T(8,128)(2,1)}, bf16[64,512]{1,0:T(8,128)(2,1)S(1)}, u32[]{:S(2)}, u32[]{:S(2)}) collective-permute-start(bf16[64,512]{1,0:T(8,128)(2,1)} %refs_1_.2), channel_id=1, source_target_pairs={{0,16},{1,17},{2,18},{3,19},{4,20},{5,21},{6,22},{7,23},{8,24},{9,... | collective-permute-start | bytes 196616 | tf_op jit(solution)/shard_map/ppermute | solution.py:412
  4.0 0.0 copy-start.3
  4.0 1.6 %shard_map.73 = (f32[8,128]{1,0:T(8,128)S(1)}, bf16[272,128]{1,0:T(8,128)(2,1)S(1)}, bf16[272,128]{1,0:T(8,128)(2,1)S(1)}, bf16[272,128]{1,0:T(8,128)(2,1)S(1)}, bf16[272,128]{1,0:T(8,128)(2,1)S(1)}) custom-call(f32[4,128]{1,0:T(4,128)} %bitcast.4, f32[4,128]{1,0:T(4,128)} %bitcast.5, bf16[512,256]{1,0:T(8,128)(2,1)} %refs_5_.2, bf16[512,512]{1,0:T(8,128)(2,1)} %refs_6_.1), custom_call_target="tpu_custom_call" | custom-call | flops 2200000000 | bytes 7400000 | tf_op jit(solution)/shard_map/pallas_call | solution.py:366
  5.7 2.5 %collective-permute-start.1 = (bf16[272,128]{1,0:T(8,128)(2,1)S(1)}, bf16[272,128]{1,0:T(8,128)(2,1)S(1)}, u32[]{:S(2)}, u32[]{:S(2)}) collective-permute-start(bf16[272,128]{1,0:T(8,128)(2,1)S(1)} %get-tuple-element.28), channel_id=1, source_target_pairs={{0,6},{2,4},{4,2},{6,0},{8,14},{10,12},{12,10},{14,8},{16,22},{18,... | collective-permute-start | bytes 208904 | tf_op jit(solution)/shard_map/ppermute | solution.py:416
  8.2 0.5 %collective-permute-start.2 = (bf16[272,128]{1,0:T(8,128)(2,1)S(1)}, bf16[272,128]{1,0:T(8,128)(2,1)S(1)}, u32[]{:S(2)}, u32[]{:S(2)}) collective-permute-start(bf16[272,128]{1,0:T(8,128)(2,1)S(1)} %get-tuple-element.29), channel_id=1, source_target_pairs={{0,4},{2,6},{4,0},{6,2},{8,12},{10,14},{12,8},{14,10},{16,20},{18,... | collective-permute-start | bytes 208904 | tf_op jit(solution)/shard_map/ppermute | solution.py:416
  8.7 0.5 %collective-permute-start.3 = (bf16[272,128]{1,0:T(8,128)(2,1)S(1)}, bf16[272,128]{1,0:T(8,128)(2,1)S(1)}, u32[]{:S(2)}, u32[]{:S(2)}) collective-permute-start(bf16[272,128]{1,0:T(8,128)(2,1)S(1)} %get-tuple-element.30), channel_id=1, source_target_pairs={{0,2},{2,0},{4,6},{6,4},{8,10},{10,8},{12,14},{14,12},{16,18},{18,... | collective-permute-start | bytes 208904 | tf_op jit(solution)/shard_map/ppermute | solution.py:416
  9.2 0.0 collective-permute-done.refs_2_
  9.2 0.0 copy-done.3
  9.3 1.6 %collective-permute-start.4 = (bf16[128,512]{1,0:T(8,128)(2,1)S(1)}, bf16[128,512]{1,0:T(8,128)(2,1)S(1)}, u32[]{:S(2)}, u32[]{:S(2)}) collective-permute-start(bf16[128,512]{1,0:T(8,128)(2,1)S(1)} %shard_map.74.refs_0_.refs_1_), channel_id=1, source_target_pairs={{0,8},{1,9},{2,10},{3,11},{4,12},{5,13},{6,14},{7,15},{8,0},{9,1},... | collective-permute-start | bytes 393224 | tf_op jit(solution)/shard_map/ppermute | solution.py:412
  10.9 1.5 %collective-permute-start.7 = (bf16[128,512]{1,0:T(8,128)(2,1)S(1)}, bf16[128,512]{1,0:T(8,128)(2,1)S(1)}, u32[]{:S(2)}, u32[]{:S(2)}) collective-permute-start(bf16[128,512]{1,0:T(8,128)(2,1)S(1)} %shard_map.74.refs_0_.refs_1_), channel_id=1, source_target_pairs={{0,2},{1,5},{2,0},{3,7},{4,6},{5,1},{6,4},{7,3},{8,10},{9,13},{10,... | collective-permute-start | bytes 393224 | tf_op jit(solution)/shard_map/ppermute | solution.py:412
  12.4 0.0 collective-permute-done.1.refs_2_
  12.4 0.7 %collective-permute-done.2.refs_3_ = bf16[272,128]{1,0:T(8,128)(2,1)S(1)} collective-permute-done((bf16[272,128]{1,0:T(8,128)(2,1)S(1)}, bf16[272,128]{1,0:T(8,128)(2,1)S(1)}, u32[]{:S(2)}, u32[]{:S(2)}) %collective-permute-start.2) | collective-permute-done | bytes 69664 | tf_op jit(solution)/shard_map/ppermute | solution.py:416
  13.1 0.0 collective-permute-done.3.refs_4_
  13.1 0.1 shard_map.76.refs_0_
  13.2 1.4 %collective-permute-start.10 = (bf16[272,128]{1,0:T(8,128)(2,1)S(1)}, bf16[272,128]{1,0:T(8,128)(2,1)S(1)}, u32[]{:S(2)}, u32[]{:S(2)}) collective-permute-start(bf16[272,128]{1,0:T(8,128)(2,1)S(1)} %shard_map.76.refs_0_), channel_id=1, source_target_pairs={{0,24},{2,26},{4,28},{6,30},{8,16},{10,18},{12,20},{14,22},{16,8},... | collective-permute-start | bytes 208904 | tf_op jit(solution)/shard_map/ppermute | solution.py:452
  14.5 0.6 %collective-permute-start.11 = (bf16[272,128]{1,0:T(8,128)(2,1)S(1)}, bf16[272,128]{1,0:T(8,128)(2,1)S(1)}, u32[]{:S(2)}, u32[]{:S(2)}) collective-permute-start(bf16[272,128]{1,0:T(8,128)(2,1)S(1)} %shard_map.76.refs_0_), channel_id=1, source_target_pairs={{0,8},{2,10},{4,12},{6,14},{8,0},{10,2},{12,4},{14,6},{16,24},{18,... | collective-permute-start | bytes 208904 | tf_op jit(solution)/shard_map/ppermute | solution.py:452
  15.1 2.5 %collective-permute-start.9 = (bf16[272,128]{1,0:T(8,128)(2,1)S(1)}, bf16[272,128]{1,0:T(8,128)(2,1)S(1)}, u32[]{:S(2)}, u32[]{:S(2)}) collective-permute-start(bf16[272,128]{1,0:T(8,128)(2,1)S(1)} %shard_map.76.refs_0_), channel_id=1, source_target_pairs={{0,16},{2,18},{4,20},{6,22},{8,24},{10,26},{12,28},{14,30},{16,0},... | collective-permute-start | bytes 208904 | tf_op jit(solution)/shard_map/ppermute | solution.py:452
  17.6 0.0 collective-permute-done.4.refs_1_
  17.7 0.5 %collective-permute-start.6 = (bf16[128,512]{1,0:T(8,128)(2,1)S(1)}, bf16[128,512]{1,0:T(8,128)(2,1)S(1)}, u32[]{:S(2)}, u32[]{:S(2)}) collective-permute-start(bf16[128,512]{1,0:T(8,128)(2,1)S(1)} %shard_map.77.refs_0_.refs_2_), channel_id=1, source_target_pairs={{0,2},{1,5},{2,0},{3,7},{4,6},{5,1},{6,4},{7,3},{8,10},{9,13},{10,... | collective-permute-start | bytes 393224 | tf_op jit(solution)/shard_map/ppermute | solution.py:412
  18.2 0.2 shard_map.78
  18.4 0.0 collective-permute-done.7.refs_1_.refs_3_
  18.5 1.6 %collective-permute-start.8 = (bf16[128,512]{1,0:T(8,128)(2,1)S(1)}, bf16[128,512]{1,0:T(8,128)(2,1)S(1)}, u32[]{:S(2)}, u32[]{:S(2)}) collective-permute-start(bf16[128,512]{1,0:T(8,128)(2,1)S(1)} %shard_map.80), channel_id=1, source_target_pairs={{0,4},{1,3},{2,6},{3,1},{4,0},{5,7},{6,2},{7,5},{8,12},{9,11},{10,... | collective-permute-start | bytes 393224 | tf_op jit(solution)/shard_map/ppermute | solution.py:412
  20.1 0.0 collective-permute-done.10.refs_3_
  20.1 0.9 %collective-permute-start.5 = (bf16[256,512]{1,0:T(8,128)(2,1)S(1)}, bf16[256,512]{1,0:T(8,128)(2,1)S(1)}, u32[]{:S(2)}, u32[]{:S(2)}) collective-permute-start(bf16[256,512]{1,0:T(8,128)(2,1)S(1)} %shard_map.79.refs_0_.refs_1_), channel_id=1, source_target_pairs={{0,4},{1,3},{2,6},{3,1},{4,0},{5,7},{6,2},{7,5},{8,12},{9,11},{10,... | collective-permute-start | bytes 786440 | tf_op jit(solution)/shard_map/ppermute | solution.py:412
  21.0 0.0 collective-permute-done.11.refs_4_
  21.0 0.7 %collective-permute-done.9.refs_2_ = bf16[272,128]{1,0:T(8,128)(2,1)S(1)} collective-permute-done((bf16[272,128]{1,0:T(8,128)(2,1)S(1)}, bf16[272,128]{1,0:T(8,128)(2,1)S(1)}, u32[]{:S(2)}, u32[]{:S(2)}) %collective-permute-start.9) | collective-permute-done | bytes 69664 | tf_op jit(solution)/shard_map/ppermute | solution.py:452
  21.7 0.0 copy-start
  21.7 0.0 copy-start.1
  21.7 0.0 copy-start.2
  21.7 0.1 shard_map.81
  21.8 1.5 %collective-permute-start.12 = (bf16[256,128]{1,0:T(8,128)(2,1)S(1)}, bf16[256,128]{1,0:T(8,128)(2,1)S(1)}, u32[]{:S(2)}, u32[]{:S(2)}) collective-permute-start(bf16[256,128]{1,0:T(8,128)(2,1)S(1)} %get-tuple-element.42), channel_id=1, source_target_pairs={{0,6},{2,4},{4,2},{6,0},{8,14},{10,12},{12,10},{14,8},{16,22},{18,... | collective-permute-start | bytes 196616 | tf_op jit(solution)/shard_map/ppermute | solution.py:416
  23.4 0.6 %collective-permute-start.13 = (bf16[256,128]{1,0:T(8,128)(2,1)S(1)}, bf16[256,128]{1,0:T(8,128)(2,1)S(1)}, u32[]{:S(2)}, u32[]{:S(2)}) collective-permute-start(bf16[256,128]{1,0:T(8,128)(2,1)S(1)} %get-tuple-element.43), channel_id=1, source_target_pairs={{0,4},{2,6},{4,0},{6,2},{8,12},{10,14},{12,8},{14,10},{16,20},{18,... | collective-permute-start | bytes 196616 | tf_op jit(solution)/shard_map/ppermute | solution.py:416
  23.9 0.0 collective-permute-done.8.refs_1_.refs_4_
  23.9 0.0 copy-start.4
  23.9 1.5 %collective-permute-start.14 = (bf16[256,128]{1,0:T(8,128)(2,1)S(1)}, bf16[256,128]{1,0:T(8,128)(2,1)S(1)}, u32[]{:S(2)}, u32[]{:S(2)}) collective-permute-start(bf16[256,128]{1,0:T(8,128)(2,1)S(1)} %get-tuple-element.44), channel_id=1, source_target_pairs={{0,2},{2,0},{4,6},{6,4},{8,10},{10,8},{12,14},{14,12},{16,18},{18,... | collective-permute-start | bytes 196616 | tf_op jit(solution)/shard_map/ppermute | solution.py:416
  25.5 0.0 collective-permute-done.6.refs_0_.refs_5_
  25.5 1.1 %collective-permute-start.15 = (bf16[128,512]{1,0:T(8,128)(2,1)S(1)}, bf16[128,512]{1,0:T(8,128)(2,1)S(1)}, u32[]{:S(2)}, u32[]{:S(2)}) collective-permute-start(bf16[128,512]{1,0:T(8,128)(2,1)S(1)} %collective-permute-done.6.refs_0_.refs_5_), channel_id=1, source_target_pairs={{0,4},{1,3},{2,6},{3,1},{4,0},{5,7},{6,2},{7,5},{8,12},{9,11},{10,... | collective-permute-start | bytes 393224 | tf_op jit(solution)/shard_map/ppermute | solution.py:412
  26.6 0.0 copy-done
  26.6 0.0 copy-done.1
  26.6 0.0 copy-done.2
  26.6 0.0 copy-done.4
  26.6 0.9 %shard_map.82 = (f32[512,512]{1,0:T(8,128)S(1)}, f32[12,128]{1,0:T(8,128)S(1)}) custom-call(f32[8,128]{1,0:T(8,128)S(1)} %get-tuple-element.36.refs_0_.refs_2_, bf16[128,512]{1,0:T(8,128)(2,1)S(1)} %collective-permute-done.8.refs_1_.refs_4_, f32[8,128]{1,0:T(8,128)S(1)} %get-tuple-element.26.refs_0_.refs_1_.refs_2_.refs_3_, f32[4,128]{1,0:T(4,128)S(1)} %bitcast.3, ...), custom_call_target="tpu_custom_call" | custom-call | flops 8800000000 | bytes 29600000 | tf_op jit(solution)/shard_map/pallas_call | solution.py:366
  27.5 0.4 %shard_map.83 = (f32[512,512]{1,0:T(8,128)S(1)}, f32[512,128]{1,0:T(8,128)S(1)}) custom-call(bf16[128,512]{1,0:T(8,128)(2,1)S(1)} %collective-permute-done.6.refs_0_.refs_5_, bf16[128,512]{1,0:T(8,128)(2,1)S(1)} %collective-permute-done.8.refs_1_.refs_4_, f32[8,128]{1,0:T(8,128)S(1)} %get-tuple-element.36.refs_0_.refs_2_, ...), custom_call_target="tpu_custom_call" | custom-call | flops 8800000000 | bytes 29600000 | tf_op jit(solution)/shard_map/pallas_call | solution.py:366
  27.9 0.0 collective-permute-done.12.refs_5_
  27.9 1.3 %collective-permute-done.13.refs_6_ = bf16[256,128]{1,0:T(8,128)(2,1)S(1)} collective-permute-done((bf16[256,128]{1,0:T(8,128)(2,1)S(1)}, bf16[256,128]{1,0:T(8,128)(2,1)S(1)}, u32[]{:S(2)}, u32[]{:S(2)}) %collective-permute-start.13) | collective-permute-done | bytes 65568 | tf_op jit(solution)/shard_map/ppermute | solution.py:416
  29.2 0.0 collective-permute-done.14.refs_7_
  29.2 0.0 collective-permute-done.5.refs_0_.refs_2_
  29.2 0.4 %shard_map.84.refs_0_ = bf16[512,512]{1,0:T(8,128)(2,1)S(1)} custom-call(bf16[256,512]{1,0:T(8,128)(2,1)S(1)} %collective-permute-done.5.refs_0_.refs_2_, bf16[512,256]{1,0:T(8,128)(2,1)S(1)} %copy-done, f32[512,512]{1,0:T(8,128)S(1)} %get-tuple-element.39.refs_2_, f32[512,128]{1,0:T(8,128)S(1)} %get-tuple-element.40.refs_3_, ...), custom_call_target="tpu_custom_call" | custom-call | flops 110000000 | bytes 370000 | tf_op jit(solution)/shard_map/pallas_call | solution.py:366
  29.5 0.1 collective-permute-start.16
  29.6 0.9 %collective-permute-done.15.refs_6_ = bf16[128,512]{1,0:T(8,128)(2,1)S(1)} collective-permute-done((bf16[128,512]{1,0:T(8,128)(2,1)S(1)}, bf16[128,512]{1,0:T(8,128)(2,1)S(1)}, u32[]{:S(2)}, u32[]{:S(2)}) %collective-permute-start.15) | collective-permute-done | bytes 131104 | tf_op jit(solution)/shard_map/ppermute | solution.py:412
  30.6 0.7 %shard_map.85 = (f32[512,512]{1,0:T(8,128)S(1)}, bf16[512,512]{1,0:T(8,128)(2,1)S(1)}) custom-call(bf16[512,512]{1,0:T(8,128)(2,1)S(1)} %shard_map.84.refs_0_, bf16[256,512]{1,0:T(8,128)(2,1)S(1)} %shard_map.79.refs_0_.refs_1_, bf16[256,512]{1,0:T(8,128)(2,1)S(1)} %collective-permute-done.5.refs_0_.refs_2_, ...), custom_call_target="tpu_custom_call" | custom-call | flops 5500000256 | bytes 18500000 | tf_op jit(solution)/shard_map/pallas_call | solution.py:366
  31.3 0.2 collective-permute-done.16.refs_2_
  31.5 1.1 %shard_map.86 = bf16[512,512]{1,0:T(8,128)(2,1)} custom-call(f32[512,512]{1,0:T(8,128)S(1)} %get-tuple-element.45.refs_0_, bf16[512,512]{1,0:T(8,128)(2,1)S(1)} %get-tuple-element.46.refs_1_, bf16[512,512]{1,0:T(8,128)(2,1)S(1)} %collective-permute-done.16.refs_2_), custom_call_target="tpu_custom_call" | custom-call | flops 1100000000 | bytes 3700000 | tf_op jit(solution)/shard_map/pallas_call | solution.py:366
  (5 shorter events, 0.0 us)
Async XLA Ops:
  0.0 9.2 %collective-permute-start = (bf16[64,512]{1,0:T(8,128)(2,1)}, bf16[64,512]{1,0:T(8,128)(2,1)S(1)}, u32[]{:S(2)}, u32[]{:S(2)}) collective-permute-start(bf16[64,512]{1,0:T(8,128)(2,1)} %refs_1_.2), channel_id=1, source_target_pairs={{0,16},{1,17},{2,18},{3,19},{4,20},{5,21},{6,22},{7,23},{8,24},{9,... | collective-permute-start | bytes 196616 | tf_op jit(solution)/shard_map/ppermute | solution.py:412
  4.0 5.2 %copy-start.3 = (bf16[64,512]{1,0:T(8,128)(2,1)S(1)}, bf16[64,512]{1,0:T(8,128)(2,1)}, u32[]{:S(2)}) copy-start(bf16[64,512]{1,0:T(8,128)(2,1)} %refs_1_.2) | copy-start | bytes 196612
  5.7 6.7 %collective-permute-start.1 = (bf16[272,128]{1,0:T(8,128)(2,1)S(1)}, bf16[272,128]{1,0:T(8,128)(2,1)S(1)}, u32[]{:S(2)}, u32[]{:S(2)}) collective-permute-start(bf16[272,128]{1,0:T(8,128)(2,1)S(1)} %get-tuple-element.28), channel_id=1, source_target_pairs={{0,6},{2,4},{4,2},{6,0},{8,14},{10,12},{12,10},{14,8},{16,22},{18,... | collective-permute-start | bytes 208904 | tf_op jit(solution)/shard_map/ppermute | solution.py:416
  8.2 4.9 %collective-permute-start.2 = (bf16[272,128]{1,0:T(8,128)(2,1)S(1)}, bf16[272,128]{1,0:T(8,128)(2,1)S(1)}, u32[]{:S(2)}, u32[]{:S(2)}) collective-permute-start(bf16[272,128]{1,0:T(8,128)(2,1)S(1)} %get-tuple-element.29), channel_id=1, source_target_pairs={{0,4},{2,6},{4,0},{6,2},{8,12},{10,14},{12,8},{14,10},{16,20},{18,... | collective-permute-start | bytes 208904 | tf_op jit(solution)/shard_map/ppermute | solution.py:416
  8.7 4.4 %collective-permute-start.3 = (bf16[272,128]{1,0:T(8,128)(2,1)S(1)}, bf16[272,128]{1,0:T(8,128)(2,1)S(1)}, u32[]{:S(2)}, u32[]{:S(2)}) collective-permute-start(bf16[272,128]{1,0:T(8,128)(2,1)S(1)} %get-tuple-element.30), channel_id=1, source_target_pairs={{0,2},{2,0},{4,6},{6,4},{8,10},{10,8},{12,14},{14,12},{16,18},{18,... | collective-permute-start | bytes 208904 | tf_op jit(solution)/shard_map/ppermute | solution.py:416
  9.3 8.4 %collective-permute-start.4 = (bf16[128,512]{1,0:T(8,128)(2,1)S(1)}, bf16[128,512]{1,0:T(8,128)(2,1)S(1)}, u32[]{:S(2)}, u32[]{:S(2)}) collective-permute-start(bf16[128,512]{1,0:T(8,128)(2,1)S(1)} %shard_map.74.refs_0_.refs_1_), channel_id=1, source_target_pairs={{0,8},{1,9},{2,10},{3,11},{4,12},{5,13},{6,14},{7,15},{8,0},{9,1},... | collective-permute-start | bytes 393224 | tf_op jit(solution)/shard_map/ppermute | solution.py:412
  10.9 7.5 %collective-permute-start.7 = (bf16[128,512]{1,0:T(8,128)(2,1)S(1)}, bf16[128,512]{1,0:T(8,128)(2,1)S(1)}, u32[]{:S(2)}, u32[]{:S(2)}) collective-permute-start(bf16[128,512]{1,0:T(8,128)(2,1)S(1)} %shard_map.74.refs_0_.refs_1_), channel_id=1, source_target_pairs={{0,2},{1,5},{2,0},{3,7},{4,6},{5,1},{6,4},{7,3},{8,10},{9,13},{10,... | collective-permute-start | bytes 393224 | tf_op jit(solution)/shard_map/ppermute | solution.py:412
  13.2 6.9 %collective-permute-start.10 = (bf16[272,128]{1,0:T(8,128)(2,1)S(1)}, bf16[272,128]{1,0:T(8,128)(2,1)S(1)}, u32[]{:S(2)}, u32[]{:S(2)}) collective-permute-start(bf16[272,128]{1,0:T(8,128)(2,1)S(1)} %shard_map.76.refs_0_), channel_id=1, source_target_pairs={{0,24},{2,26},{4,28},{6,30},{8,16},{10,18},{12,20},{14,22},{16,8},... | collective-permute-start | bytes 208904 | tf_op jit(solution)/shard_map/ppermute | solution.py:452
  14.5 6.4 %collective-permute-start.11 = (bf16[272,128]{1,0:T(8,128)(2,1)S(1)}, bf16[272,128]{1,0:T(8,128)(2,1)S(1)}, u32[]{:S(2)}, u32[]{:S(2)}) collective-permute-start(bf16[272,128]{1,0:T(8,128)(2,1)S(1)} %shard_map.76.refs_0_), channel_id=1, source_target_pairs={{0,8},{2,10},{4,12},{6,14},{8,0},{10,2},{12,4},{14,6},{16,24},{18,... | collective-permute-start | bytes 208904 | tf_op jit(solution)/shard_map/ppermute | solution.py:452
  15.1 6.5 %collective-permute-start.9 = (bf16[272,128]{1,0:T(8,128)(2,1)S(1)}, bf16[272,128]{1,0:T(8,128)(2,1)S(1)}, u32[]{:S(2)}, u32[]{:S(2)}) collective-permute-start(bf16[272,128]{1,0:T(8,128)(2,1)S(1)} %shard_map.76.refs_0_), channel_id=1, source_target_pairs={{0,16},{2,18},{4,20},{6,22},{8,24},{10,26},{12,28},{14,30},{16,0},... | collective-permute-start | bytes 208904 | tf_op jit(solution)/shard_map/ppermute | solution.py:452
  17.7 7.8 %collective-permute-start.6 = (bf16[128,512]{1,0:T(8,128)(2,1)S(1)}, bf16[128,512]{1,0:T(8,128)(2,1)S(1)}, u32[]{:S(2)}, u32[]{:S(2)}) collective-permute-start(bf16[128,512]{1,0:T(8,128)(2,1)S(1)} %shard_map.77.refs_0_.refs_2_), channel_id=1, source_target_pairs={{0,2},{1,5},{2,0},{3,7},{4,6},{5,1},{6,4},{7,3},{8,10},{9,13},{10,... | collective-permute-start | bytes 393224 | tf_op jit(solution)/shard_map/ppermute | solution.py:412
  18.5 5.5 %collective-permute-start.8 = (bf16[128,512]{1,0:T(8,128)(2,1)S(1)}, bf16[128,512]{1,0:T(8,128)(2,1)S(1)}, u32[]{:S(2)}, u32[]{:S(2)}) collective-permute-start(bf16[128,512]{1,0:T(8,128)(2,1)S(1)} %shard_map.80), channel_id=1, source_target_pairs={{0,4},{1,3},{2,6},{3,1},{4,0},{5,7},{6,2},{7,5},{8,12},{9,11},{10,... | collective-permute-start | bytes 393224 | tf_op jit(solution)/shard_map/ppermute | solution.py:412
  20.1 9.1 %collective-permute-start.5 = (bf16[256,512]{1,0:T(8,128)(2,1)S(1)}, bf16[256,512]{1,0:T(8,128)(2,1)S(1)}, u32[]{:S(2)}, u32[]{:S(2)}) collective-permute-start(bf16[256,512]{1,0:T(8,128)(2,1)S(1)} %shard_map.79.refs_0_.refs_1_), channel_id=1, source_target_pairs={{0,4},{1,3},{2,6},{3,1},{4,0},{5,7},{6,2},{7,5},{8,12},{9,11},{10,... | collective-permute-start | bytes 786440 | tf_op jit(solution)/shard_map/ppermute | solution.py:412
  21.7 4.9 %copy-start = (bf16[512,256]{1,0:T(8,128)(2,1)S(1)}, bf16[512,256]{1,0:T(8,128)(2,1)}, u32[]{:S(2)}) copy-start(bf16[512,256]{1,0:T(8,128)(2,1)} %refs_1_.3) | copy-start | bytes 786436
  21.7 4.9 %copy-start.1 = (bf16[512,512]{1,0:T(8,128)(2,1)S(1)}, bf16[512,512]{1,0:T(8,128)(2,1)}, u32[]{:S(2)}) copy-start(bf16[512,512]{1,0:T(8,128)(2,1)} %refs_6_.1) | copy-start | bytes 1572868
  21.7 4.9 %copy-start.2 = (bf16[512,256]{1,0:T(8,128)(2,1)S(1)}, bf16[512,256]{1,0:T(8,128)(2,1)}, u32[]{:S(2)}) copy-start(bf16[512,256]{1,0:T(8,128)(2,1)} %refs_5_.2) | copy-start | bytes 786436
  21.8 6.1 %collective-permute-start.12 = (bf16[256,128]{1,0:T(8,128)(2,1)S(1)}, bf16[256,128]{1,0:T(8,128)(2,1)S(1)}, u32[]{:S(2)}, u32[]{:S(2)}) collective-permute-start(bf16[256,128]{1,0:T(8,128)(2,1)S(1)} %get-tuple-element.42), channel_id=1, source_target_pairs={{0,6},{2,4},{4,2},{6,0},{8,14},{10,12},{12,10},{14,8},{16,22},{18,... | collective-permute-start | bytes 196616 | tf_op jit(solution)/shard_map/ppermute | solution.py:416
  23.4 5.8 %collective-permute-start.13 = (bf16[256,128]{1,0:T(8,128)(2,1)S(1)}, bf16[256,128]{1,0:T(8,128)(2,1)S(1)}, u32[]{:S(2)}, u32[]{:S(2)}) collective-permute-start(bf16[256,128]{1,0:T(8,128)(2,1)S(1)} %get-tuple-element.43), channel_id=1, source_target_pairs={{0,4},{2,6},{4,0},{6,2},{8,12},{10,14},{12,8},{14,10},{16,20},{18,... | collective-permute-start | bytes 196616 | tf_op jit(solution)/shard_map/ppermute | solution.py:416
  23.9 2.7 %copy-start.4 = (f32[512,1]{0,1:T(1,128)S(1)}, f32[512,1]{0,1:T(1,128)}, u32[]{:S(2)}) copy-start(f32[512,1]{0,1:T(1,128)} %param.12) | copy-start | bytes 6148
  23.9 5.2 %collective-permute-start.14 = (bf16[256,128]{1,0:T(8,128)(2,1)S(1)}, bf16[256,128]{1,0:T(8,128)(2,1)S(1)}, u32[]{:S(2)}, u32[]{:S(2)}) collective-permute-start(bf16[256,128]{1,0:T(8,128)(2,1)S(1)} %get-tuple-element.44), channel_id=1, source_target_pairs={{0,2},{2,0},{4,6},{6,4},{8,10},{10,8},{12,14},{14,12},{16,18},{18,... | collective-permute-start | bytes 196616 | tf_op jit(solution)/shard_map/ppermute | solution.py:416
  25.5 5.1 %collective-permute-start.15 = (bf16[128,512]{1,0:T(8,128)(2,1)S(1)}, bf16[128,512]{1,0:T(8,128)(2,1)S(1)}, u32[]{:S(2)}, u32[]{:S(2)}) collective-permute-start(bf16[128,512]{1,0:T(8,128)(2,1)S(1)} %collective-permute-done.6.refs_0_.refs_5_), channel_id=1, source_target_pairs={{0,4},{1,3},{2,6},{3,1},{4,0},{5,7},{6,2},{7,5},{8,12},{9,11},{10,... | collective-permute-start | bytes 393224 | tf_op jit(solution)/shard_map/ppermute | solution.py:412
  29.5 2.0 %collective-permute-start.16 = (bf16[512,512]{1,0:T(8,128)(2,1)S(1)}, bf16[512,512]{1,0:T(8,128)(2,1)S(1)}, u32[]{:S(2)}, u32[]{:S(2)}) collective-permute-start(bf16[512,512]{1,0:T(8,128)(2,1)S(1)} %shard_map.84.refs_0_), channel_id=1, source_target_pairs={{0,1},{1,0},{2,3},{3,2},{4,5},{5,4},{6,7},{7,6},{8,9},{9,8},{10,11... | collective-permute-start | bytes 1572872 | tf_op jit(solution)/shard_map/ppermute | solution.py:506

commit v6 on v5

--- a/solution.py
+++ b/solution.py
@@ -140,7 +140,12 @@
         wide = memory[pl.ds(start, piece), :]
         for i, block in enumerate(lane_blocks(wide)):
             out_ref[i * piece : (i + 1) * piece, :] = block
-        write_tail(out_ref, wide.size // LANES, norm, base + top_gain, base)
+        at = wide.size // LANES
+        if k == 0:
+            write_tail(out_ref, at, norm, base + top_gain, base)
+            tail = out_ref[at:, :]
+        else:
+            out_ref[at:, :] = tail
 
 
 def chain_logs(where, tops, decays, end):

time: 32.8 us -> 32.8 us (level)
  no operation moved by 1% of the time
where the time goes in v6:
time: 32.8 us; the launch traced here: 32.7 us
  starting transfers between devices  23 us (70%)
  Pallas kernels  5.69 us (17%)
  waiting for transfers between devices  3.83 us (12%)
    ppermute x7, starting transfers between devices, over_ctx(): return lax.ppermute(held, ('ctx', 'head'), pairs)  11.3 us
    ppermute x6, starting transfers between devices, in_group(): lax.ppermute(sent[k], 'ctx', inner_pairs(n_ctx, inner, k))  7.21 us
    pallas_call x14, Pallas kernels, call(): pl.pallas_call(lambda *refs: kernel(*refs[skip:]), out_shape=out_shape, i...  5.69 us
    ppermute x3, starting transfers between devices, local(): lax.ppermute(total, 'ctx', outer_pairs(n_ctx, inner, k))  4.45 us
    ppermute x6, waiting for transfers between devices, in_group(): lax.ppermute(sent[k], 'ctx', inner_pairs(n_ctx, inner, k))  1.94 us
    ppermute x7, waiting for transfers between devices, over_ctx(): return lax.ppermute(held, ('ctx', 'head'), pairs)  0.96 us
    ppermute x3, waiting for transfers between devices, local(): lax.ppermute(total, 'ctx', outer_pairs(n_ctx, inner, k))  0.7 us
  transfers between devices with their start and end apart: 17, of which 5 were waited for; matrix products, arithmetic and copies ran while one was open for 0% of the time, Pallas kernels for 14%

profile of v6, /device:TPU:0, one launch (start us, length us, event | category | flops | bytes accessed | tf_op | source)
XLA Modules:
  0.0 32.7 jit_solution(17631710860901067072)
XLA Ops:
  0.0 4.0 %collective-permute-start = (bf16[64,512]{1,0:T(8,128)(2,1)}, bf16[64,512]{1,0:T(8,128)(2,1)S(1)}, u32[]{:S(2)}, u32[]{:S(2)}) collective-permute-start(bf16[64,512]{1,0:T(8,128)(2,1)} %refs_1_.2), channel_id=1, source_target_pairs={{0,16},{1,17},{2,18},{3,19},{4,20},{5,21},{6,22},{7,23},{8,24},{9,... | collective-permute-start | bytes 196616 | tf_op jit(solution)/shard_map/ppermute | solution.py:417
  4.0 0.0 copy-start.3
  4.0 1.6 %shard_map.73 = (f32[8,128]{1,0:T(8,128)S(1)}, bf16[272,128]{1,0:T(8,128)(2,1)S(1)}, bf16[272,128]{1,0:T(8,128)(2,1)S(1)}, bf16[272,128]{1,0:T(8,128)(2,1)S(1)}, bf16[272,128]{1,0:T(8,128)(2,1)S(1)}) custom-call(f32[4,128]{1,0:T(4,128)} %bitcast.4, f32[4,128]{1,0:T(4,128)} %bitcast.5, bf16[512,256]{1,0:T(8,128)(2,1)} %refs_5_.2, bf16[512,512]{1,0:T(8,128)(2,1)} %refs_6_.1), custom_call_target="tpu_custom_call" | custom-call | flops 2200000000 | bytes 7400000 | tf_op jit(solution)/shard_map/pallas_call | solution.py:371
  5.7 2.5 %collective-permute-start.1 = (bf16[272,128]{1,0:T(8,128)(2,1)S(1)}, bf16[272,128]{1,0:T(8,128)(2,1)S(1)}, u32[]{:S(2)}, u32[]{:S(2)}) collective-permute-start(bf16[272,128]{1,0:T(8,128)(2,1)S(1)} %get-tuple-element.28), channel_id=1, source_target_pairs={{0,6},{2,4},{4,2},{6,0},{8,14},{10,12},{12,10},{14,8},{16,22},{18,... | collective-permute-start | bytes 208904 | tf_op jit(solution)/shard_map/ppermute | solution.py:421
  8.2 0.5 %collective-permute-start.2 = (bf16[272,128]{1,0:T(8,128)(2,1)S(1)}, bf16[272,128]{1,0:T(8,128)(2,1)S(1)}, u32[]{:S(2)}, u32[]{:S(2)}) collective-permute-start(bf16[272,128]{1,0:T(8,128)(2,1)S(1)} %get-tuple-element.29), channel_id=1, source_target_pairs={{0,4},{2,6},{4,0},{6,2},{8,12},{10,14},{12,8},{14,10},{16,20},{18,... | collective-permute-start | bytes 208904 | tf_op jit(solution)/shard_map/ppermute | solution.py:421
  8.7 0.5 %collective-permute-start.3 = (bf16[272,128]{1,0:T(8,128)(2,1)S(1)}, bf16[272,128]{1,0:T(8,128)(2,1)S(1)}, u32[]{:S(2)}, u32[]{:S(2)}) collective-permute-start(bf16[272,128]{1,0:T(8,128)(2,1)S(1)} %get-tuple-element.30), channel_id=1, source_target_pairs={{0,2},{2,0},{4,6},{6,4},{8,10},{10,8},{12,14},{14,12},{16,18},{18,... | collective-permute-start | bytes 208904 | tf_op jit(solution)/shard_map/ppermute | solution.py:421
  9.2 0.0 collective-permute-done.refs_2_
  9.2 0.0 copy-done.3
  9.3 1.6 %collective-permute-start.4 = (bf16[128,512]{1,0:T(8,128)(2,1)S(1)}, bf16[128,512]{1,0:T(8,128)(2,1)S(1)}, u32[]{:S(2)}, u32[]{:S(2)}) collective-permute-start(bf16[128,512]{1,0:T(8,128)(2,1)S(1)} %shard_map.74.refs_0_.refs_1_), channel_id=1, source_target_pairs={{0,8},{1,9},{2,10},{3,11},{4,12},{5,13},{6,14},{7,15},{8,0},{9,1},... | collective-permute-start | bytes 393224 | tf_op jit(solution)/shard_map/ppermute | solution.py:417
  10.9 1.5 %collective-permute-start.7 = (bf16[128,512]{1,0:T(8,128)(2,1)S(1)}, bf16[128,512]{1,0:T(8,128)(2,1)S(1)}, u32[]{:S(2)}, u32[]{:S(2)}) collective-permute-start(bf16[128,512]{1,0:T(8,128)(2,1)S(1)} %shard_map.74.refs_0_.refs_1_), channel_id=1, source_target_pairs={{0,2},{1,5},{2,0},{3,7},{4,6},{5,1},{6,4},{7,3},{8,10},{9,13},{10,... | collective-permute-start | bytes 393224 | tf_op jit(solution)/shard_map/ppermute | solution.py:417
  12.4 0.0 collective-permute-done.1.refs_2_
  12.4 0.7 %collective-permute-done.2.refs_3_ = bf16[272,128]{1,0:T(8,128)(2,1)S(1)} collective-permute-done((bf16[272,128]{1,0:T(8,128)(2,1)S(1)}, bf16[272,128]{1,0:T(8,128)(2,1)S(1)}, u32[]{:S(2)}, u32[]{:S(2)}) %collective-permute-start.2) | collective-permute-done | bytes 69664 | tf_op jit(solution)/shard_map/ppermute | solution.py:421
  13.1 0.0 collective-permute-done.3.refs_4_
  13.1 0.1 shard_map.76.refs_0_
  13.2 1.3 %collective-permute-start.10 = (bf16[272,128]{1,0:T(8,128)(2,1)S(1)}, bf16[272,128]{1,0:T(8,128)(2,1)S(1)}, u32[]{:S(2)}, u32[]{:S(2)}) collective-permute-start(bf16[272,128]{1,0:T(8,128)(2,1)S(1)} %shard_map.76.refs_0_), channel_id=1, source_target_pairs={{0,24},{2,26},{4,28},{6,30},{8,16},{10,18},{12,20},{14,22},{16,8},... | collective-permute-start | bytes 208904 | tf_op jit(solution)/shard_map/ppermute | solution.py:457
  14.5 0.6 %collective-permute-start.11 = (bf16[272,128]{1,0:T(8,128)(2,1)S(1)}, bf16[272,128]{1,0:T(8,128)(2,1)S(1)}, u32[]{:S(2)}, u32[]{:S(2)}) collective-permute-start(bf16[272,128]{1,0:T(8,128)(2,1)S(1)} %shard_map.76.refs_0_), channel_id=1, source_target_pairs={{0,8},{2,10},{4,12},{6,14},{8,0},{10,2},{12,4},{14,6},{16,24},{18,... | collective-permute-start | bytes 208904 | tf_op jit(solution)/shard_map/ppermute | solution.py:457
  15.1 2.5 %collective-permute-start.9 = (bf16[272,128]{1,0:T(8,128)(2,1)S(1)}, bf16[272,128]{1,0:T(8,128)(2,1)S(1)}, u32[]{:S(2)}, u32[]{:S(2)}) collective-permute-start(bf16[272,128]{1,0:T(8,128)(2,1)S(1)} %shard_map.76.refs_0_), channel_id=1, source_target_pairs={{0,16},{2,18},{4,20},{6,22},{8,24},{10,26},{12,28},{14,30},{16,0},... | collective-permute-start | bytes 208904 | tf_op jit(solution)/shard_map/ppermute | solution.py:457
  17.6 0.0 collective-permute-done.4.refs_1_
  17.7 0.5 %collective-permute-start.6 = (bf16[128,512]{1,0:T(8,128)(2,1)S(1)}, bf16[128,512]{1,0:T(8,128)(2,1)S(1)}, u32[]{:S(2)}, u32[]{:S(2)}) collective-permute-start(bf16[128,512]{1,0:T(8,128)(2,1)S(1)} %shard_map.77.refs_0_.refs_2_), channel_id=1, source_target_pairs={{0,2},{1,5},{2,0},{3,7},{4,6},{5,1},{6,4},{7,3},{8,10},{9,13},{10,... | collective-permute-start | bytes 393224 | tf_op jit(solution)/shard_map/ppermute | solution.py:417
  18.2 0.2 shard_map.78
  18.4 0.0 collective-permute-done.7.refs_1_.refs_3_
  18.5 1.6 %collective-permute-start.8 = (bf16[128,512]{1,0:T(8,128)(2,1)S(1)}, bf16[128,512]{1,0:T(8,128)(2,1)S(1)}, u32[]{:S(2)}, u32[]{:S(2)}) collective-permute-start(bf16[128,512]{1,0:T(8,128)(2,1)S(1)} %shard_map.80), channel_id=1, source_target_pairs={{0,4},{1,3},{2,6},{3,1},{4,0},{5,7},{6,2},{7,5},{8,12},{9,11},{10,... | collective-permute-start | bytes 393224 | tf_op jit(solution)/shard_map/ppermute | solution.py:417
  20.1 0.0 collective-permute-done.10.refs_3_
  20.1 0.9 %collective-permute-start.5 = (bf16[256,512]{1,0:T(8,128)(2,1)S(1)}, bf16[256,512]{1,0:T(8,128)(2,1)S(1)}, u32[]{:S(2)}, u32[]{:S(2)}) collective-permute-start(bf16[256,512]{1,0:T(8,128)(2,1)S(1)} %shard_map.79.refs_0_.refs_1_), channel_id=1, source_target_pairs={{0,4},{1,3},{2,6},{3,1},{4,0},{5,7},{6,2},{7,5},{8,12},{9,11},{10,... | collective-permute-start | bytes 786440 | tf_op jit(solution)/shard_map/ppermute | solution.py:417
  21.0 0.0 collective-permute-done.11.refs_4_
  21.0 0.7 %collective-permute-done.9.refs_2_ = bf16[272,128]{1,0:T(8,128)(2,1)S(1)} collective-permute-done((bf16[272,128]{1,0:T(8,128)(2,1)S(1)}, bf16[272,128]{1,0:T(8,128)(2,1)S(1)}, u32[]{:S(2)}, u32[]{:S(2)}) %collective-permute-start.9) | collective-permute-done | bytes 69664 | tf_op jit(solution)/shard_map/ppermute | solution.py:457
  21.7 0.0 copy-start
  21.7 0.0 copy-start.1
  21.7 0.0 copy-start.2
  21.7 0.1 shard_map.81
  21.8 1.5 %collective-permute-start.12 = (bf16[256,128]{1,0:T(8,128)(2,1)S(1)}, bf16[256,128]{1,0:T(8,128)(2,1)S(1)}, u32[]{:S(2)}, u32[]{:S(2)}) collective-permute-start(bf16[256,128]{1,0:T(8,128)(2,1)S(1)} %get-tuple-element.42), channel_id=1, source_target_pairs={{0,6},{2,4},{4,2},{6,0},{8,14},{10,12},{12,10},{14,8},{16,22},{18,... | collective-permute-start | bytes 196616 | tf_op jit(solution)/shard_map/ppermute | solution.py:421
  23.4 0.6 %collective-permute-start.13 = (bf16[256,128]{1,0:T(8,128)(2,1)S(1)}, bf16[256,128]{1,0:T(8,128)(2,1)S(1)}, u32[]{:S(2)}, u32[]{:S(2)}) collective-permute-start(bf16[256,128]{1,0:T(8,128)(2,1)S(1)} %get-tuple-element.43), channel_id=1, source_target_pairs={{0,4},{2,6},{4,0},{6,2},{8,12},{10,14},{12,8},{14,10},{16,20},{18,... | collective-permute-start | bytes 196616 | tf_op jit(solution)/shard_map/ppermute | solution.py:421
  23.9 0.0 collective-permute-done.8.refs_1_.refs_4_
  23.9 0.0 copy-start.4
  23.9 1.5 %collective-permute-start.14 = (bf16[256,128]{1,0:T(8,128)(2,1)S(1)}, bf16[256,128]{1,0:T(8,128)(2,1)S(1)}, u32[]{:S(2)}, u32[]{:S(2)}) collective-permute-start(bf16[256,128]{1,0:T(8,128)(2,1)S(1)} %get-tuple-element.44), channel_id=1, source_target_pairs={{0,2},{2,0},{4,6},{6,4},{8,10},{10,8},{12,14},{14,12},{16,18},{18,... | collective-permute-start | bytes 196616 | tf_op jit(solution)/shard_map/ppermute | solution.py:421
  25.5 0.0 collective-permute-done.6.refs_0_.refs_5_
  25.5 1.1 %collective-permute-start.15 = (bf16[128,512]{1,0:T(8,128)(2,1)S(1)}, bf16[128,512]{1,0:T(8,128)(2,1)S(1)}, u32[]{:S(2)}, u32[]{:S(2)}) collective-permute-start(bf16[128,512]{1,0:T(8,128)(2,1)S(1)} %collective-permute-done.6.refs_0_.refs_5_), channel_id=1, source_target_pairs={{0,4},{1,3},{2,6},{3,1},{4,0},{5,7},{6,2},{7,5},{8,12},{9,11},{10,... | collective-permute-start | bytes 393224 | tf_op jit(solution)/shard_map/ppermute | solution.py:417
  26.6 0.0 copy-done
  26.6 0.0 copy-done.1
  26.6 0.0 copy-done.2
  26.6 0.0 copy-done.4
  26.6 0.9 %shard_map.82 = (f32[512,512]{1,0:T(8,128)S(1)}, f32[12,128]{1,0:T(8,128)S(1)}) custom-call(f32[8,128]{1,0:T(8,128)S(1)} %get-tuple-element.36.refs_0_.refs_2_, bf16[128,512]{1,0:T(8,128)(2,1)S(1)} %collective-permute-done.8.refs_1_.refs_4_, f32[8,128]{1,0:T(8,128)S(1)} %get-tuple-element.26.refs_0_.refs_1_.refs_2_.refs_3_, f32[4,128]{1,0:T(4,128)S(1)} %bitcast.3, ...), custom_call_target="tpu_custom_call" | custom-call | flops 8800000000 | bytes 29600000 | tf_op jit(solution)/shard_map/pallas_call | solution.py:371
  27.5 0.4 %shard_map.83 = (f32[512,512]{1,0:T(8,128)S(1)}, f32[512,128]{1,0:T(8,128)S(1)}) custom-call(bf16[128,512]{1,0:T(8,128)(2,1)S(1)} %collective-permute-done.6.refs_0_.refs_5_, bf16[128,512]{1,0:T(8,128)(2,1)S(1)} %collective-permute-done.8.refs_1_.refs_4_, f32[8,128]{1,0:T(8,128)S(1)} %get-tuple-element.36.refs_0_.refs_2_, ...), custom_call_target="tpu_custom_call" | custom-call | flops 8800000000 | bytes 29600000 | tf_op jit(solution)/shard_map/pallas_call | solution.py:371
  27.9 0.0 collective-permute-done.12.refs_5_
  27.9 1.3 %collective-permute-done.13.refs_6_ = bf16[256,128]{1,0:T(8,128)(2,1)S(1)} collective-permute-done((bf16[256,128]{1,0:T(8,128)(2,1)S(1)}, bf16[256,128]{1,0:T(8,128)(2,1)S(1)}, u32[]{:S(2)}, u32[]{:S(2)}) %collective-permute-start.13) | collective-permute-done | bytes 65568 | tf_op jit(solution)/shard_map/ppermute | solution.py:421
  29.2 0.0 collective-permute-done.14.refs_7_
  29.2 0.0 collective-permute-done.5.refs_0_.refs_2_
  29.2 0.4 %shard_map.84.refs_0_ = bf16[512,512]{1,0:T(8,128)(2,1)S(1)} custom-call(bf16[256,512]{1,0:T(8,128)(2,1)S(1)} %collective-permute-done.5.refs_0_.refs_2_, bf16[512,256]{1,0:T(8,128)(2,1)S(1)} %copy-done, f32[512,512]{1,0:T(8,128)S(1)} %get-tuple-element.39.refs_2_, f32[512,128]{1,0:T(8,128)S(1)} %get-tuple-element.40.refs_3_, ...), custom_call_target="tpu_custom_call" | custom-call | flops 110000000 | bytes 370000 | tf_op jit(solution)/shard_map/pallas_call | solution.py:371
  29.5 0.1 collective-permute-start.16
  29.6 0.9 %collective-permute-done.15.refs_6_ = bf16[128,512]{1,0:T(8,128)(2,1)S(1)} collective-permute-done((bf16[128,512]{1,0:T(8,128)(2,1)S(1)}, bf16[128,512]{1,0:T(8,128)(2,1)S(1)}, u32[]{:S(2)}, u32[]{:S(2)}) %collective-permute-start.15) | collective-permute-done | bytes 131104 | tf_op jit(solution)/shard_map/ppermute | solution.py:417
  30.6 0.7 %shard_map.85 = (f32[512,512]{1,0:T(8,128)S(1)}, bf16[512,512]{1,0:T(8,128)(2,1)S(1)}) custom-call(bf16[512,512]{1,0:T(8,128)(2,1)S(1)} %shard_map.84.refs_0_, bf16[256,512]{1,0:T(8,128)(2,1)S(1)} %shard_map.79.refs_0_.refs_1_, bf16[256,512]{1,0:T(8,128)(2,1)S(1)} %collective-permute-done.5.refs_0_.refs_2_, ...), custom_call_target="tpu_custom_call" | custom-call | flops 5500000256 | bytes 18500000 | tf_op jit(solution)/shard_map/pallas_call | solution.py:371
  31.3 0.2 collective-permute-done.16.refs_2_
  31.5 1.1 %shard_map.86 = bf16[512,512]{1,0:T(8,128)(2,1)} custom-call(f32[512,512]{1,0:T(8,128)S(1)} %get-tuple-element.45.refs_0_, bf16[512,512]{1,0:T(8,128)(2,1)S(1)} %get-tuple-element.46.refs_1_, bf16[512,512]{1,0:T(8,128)(2,1)S(1)} %collective-permute-done.16.refs_2_), custom_call_target="tpu_custom_call" | custom-call | flops 1100000000 | bytes 3700000 | tf_op jit(solution)/shard_map/pallas_call | solution.py:371
  (5 shorter events, 0.0 us)
Async XLA Ops:
  0.0 9.2 %collective-permute-start = (bf16[64,512]{1,0:T(8,128)(2,1)}, bf16[64,512]{1,0:T(8,128)(2,1)S(1)}, u32[]{:S(2)}, u32[]{:S(2)}) collective-permute-start(bf16[64,512]{1,0:T(8,128)(2,1)} %refs_1_.2), channel_id=1, source_target_pairs={{0,16},{1,17},{2,18},{3,19},{4,20},{5,21},{6,22},{7,23},{8,24},{9,... | collective-permute-start | bytes 196616 | tf_op jit(solution)/shard_map/ppermute | solution.py:417
  4.0 5.2 %copy-start.3 = (bf16[64,512]{1,0:T(8,128)(2,1)S(1)}, bf16[64,512]{1,0:T(8,128)(2,1)}, u32[]{:S(2)}) copy-start(bf16[64,512]{1,0:T(8,128)(2,1)} %refs_1_.2) | copy-start | bytes 196612
  5.7 6.7 %collective-permute-start.1 = (bf16[272,128]{1,0:T(8,128)(2,1)S(1)}, bf16[272,128]{1,0:T(8,128)(2,1)S(1)}, u32[]{:S(2)}, u32[]{:S(2)}) collective-permute-start(bf16[272,128]{1,0:T(8,128)(2,1)S(1)} %get-tuple-element.28), channel_id=1, source_target_pairs={{0,6},{2,4},{4,2},{6,0},{8,14},{10,12},{12,10},{14,8},{16,22},{18,... | collective-permute-start | bytes 208904 | tf_op jit(solution)/shard_map/ppermute | solution.py:421
  8.2 4.9 %collective-permute-start.2 = (bf16[272,128]{1,0:T(8,128)(2,1)S(1)}, bf16[272,128]{1,0:T(8,128)(2,1)S(1)}, u32[]{:S(2)}, u32[]{:S(2)}) collective-permute-start(bf16[272,128]{1,0:T(8,128)(2,1)S(1)} %get-tuple-element.29), channel_id=1, source_target_pairs={{0,4},{2,6},{4,0},{6,2},{8,12},{10,14},{12,8},{14,10},{16,20},{18,... | collective-permute-start | bytes 208904 | tf_op jit(solution)/shard_map/ppermute | solution.py:421
  8.7 4.4 %collective-permute-start.3 = (bf16[272,128]{1,0:T(8,128)(2,1)S(1)}, bf16[272,128]{1,0:T(8,128)(2,1)S(1)}, u32[]{:S(2)}, u32[]{:S(2)}) collective-permute-start(bf16[272,128]{1,0:T(8,128)(2,1)S(1)} %get-tuple-element.30), channel_id=1, source_target_pairs={{0,2},{2,0},{4,6},{6,4},{8,10},{10,8},{12,14},{14,12},{16,18},{18,... | collective-permute-start | bytes 208904 | tf_op jit(solution)/shard_map/ppermute | solution.py:421
  9.3 8.4 %collective-permute-start.4 = (bf16[128,512]{1,0:T(8,128)(2,1)S(1)}, bf16[128,512]{1,0:T(8,128)(2,1)S(1)}, u32[]{:S(2)}, u32[]{:S(2)}) collective-permute-start(bf16[128,512]{1,0:T(8,128)(2,1)S(1)} %shard_map.74.refs_0_.refs_1_), channel_id=1, source_target_pairs={{0,8},{1,9},{2,10},{3,11},{4,12},{5,13},{6,14},{7,15},{8,0},{9,1},... | collective-permute-start | bytes 393224 | tf_op jit(solution)/shard_map/ppermute | solution.py:417
  10.9 7.5 %collective-permute-start.7 = (bf16[128,512]{1,0:T(8,128)(2,1)S(1)}, bf16[128,512]{1,0:T(8,128)(2,1)S(1)}, u32[]{:S(2)}, u32[]{:S(2)}) collective-permute-start(bf16[128,512]{1,0:T(8,128)(2,1)S(1)} %shard_map.74.refs_0_.refs_1_), channel_id=1, source_target_pairs={{0,2},{1,5},{2,0},{3,7},{4,6},{5,1},{6,4},{7,3},{8,10},{9,13},{10,... | collective-permute-start | bytes 393224 | tf_op jit(solution)/shard_map/ppermute | solution.py:417
  13.2 6.9 %collective-permute-start.10 = (bf16[272,128]{1,0:T(8,128)(2,1)S(1)}, bf16[272,128]{1,0:T(8,128)(2,1)S(1)}, u32[]{:S(2)}, u32[]{:S(2)}) collective-permute-start(bf16[272,128]{1,0:T(8,128)(2,1)S(1)} %shard_map.76.refs_0_), channel_id=1, source_target_pairs={{0,24},{2,26},{4,28},{6,30},{8,16},{10,18},{12,20},{14,22},{16,8},... | collective-permute-start | bytes 208904 | tf_op jit(solution)/shard_map/ppermute | solution.py:457
  14.5 6.4 %collective-permute-start.11 = (bf16[272,128]{1,0:T(8,128)(2,1)S(1)}, bf16[272,128]{1,0:T(8,128)(2,1)S(1)}, u32[]{:S(2)}, u32[]{:S(2)}) collective-permute-start(bf16[272,128]{1,0:T(8,128)(2,1)S(1)} %shard_map.76.refs_0_), channel_id=1, source_target_pairs={{0,8},{2,10},{4,12},{6,14},{8,0},{10,2},{12,4},{14,6},{16,24},{18,... | collective-permute-start | bytes 208904 | tf_op jit(solution)/shard_map/ppermute | solution.py:457
  15.1 6.5 %collective-permute-start.9 = (bf16[272,128]{1,0:T(8,128)(2,1)S(1)}, bf16[272,128]{1,0:T(8,128)(2,1)S(1)}, u32[]{:S(2)}, u32[]{:S(2)}) collective-permute-start(bf16[272,128]{1,0:T(8,128)(2,1)S(1)} %shard_map.76.refs_0_), channel_id=1, source_target_pairs={{0,16},{2,18},{4,20},{6,22},{8,24},{10,26},{12,28},{14,30},{16,0},... | collective-permute-start | bytes 208904 | tf_op jit(solution)/shard_map/ppermute | solution.py:457
  17.7 7.8 %collective-permute-start.6 = (bf16[128,512]{1,0:T(8,128)(2,1)S(1)}, bf16[128,512]{1,0:T(8,128)(2,1)S(1)}, u32[]{:S(2)}, u32[]{:S(2)}) collective-permute-start(bf16[128,512]{1,0:T(8,128)(2,1)S(1)} %shard_map.77.refs_0_.refs_2_), channel_id=1, source_target_pairs={{0,2},{1,5},{2,0},{3,7},{4,6},{5,1},{6,4},{7,3},{8,10},{9,13},{10,... | collective-permute-start | bytes 393224 | tf_op jit(solution)/shard_map/ppermute | solution.py:417
  18.5 5.5 %collective-permute-start.8 = (bf16[128,512]{1,0:T(8,128)(2,1)S(1)}, bf16[128,512]{1,0:T(8,128)(2,1)S(1)}, u32[]{:S(2)}, u32[]{:S(2)}) collective-permute-start(bf16[128,512]{1,0:T(8,128)(2,1)S(1)} %shard_map.80), channel_id=1, source_target_pairs={{0,4},{1,3},{2,6},{3,1},{4,0},{5,7},{6,2},{7,5},{8,12},{9,11},{10,... | collective-permute-start | bytes 393224 | tf_op jit(solution)/shard_map/ppermute | solution.py:417
  20.1 9.1 %collective-permute-start.5 = (bf16[256,512]{1,0:T(8,128)(2,1)S(1)}, bf16[256,512]{1,0:T(8,128)(2,1)S(1)}, u32[]{:S(2)}, u32[]{:S(2)}) collective-permute-start(bf16[256,512]{1,0:T(8,128)(2,1)S(1)} %shard_map.79.refs_0_.refs_1_), channel_id=1, source_target_pairs={{0,4},{1,3},{2,6},{3,1},{4,0},{5,7},{6,2},{7,5},{8,12},{9,11},{10,... | collective-permute-start | bytes 786440 | tf_op jit(solution)/shard_map/ppermute | solution.py:417
  21.7 4.9 %copy-start = (bf16[512,256]{1,0:T(8,128)(2,1)S(1)}, bf16[512,256]{1,0:T(8,128)(2,1)}, u32[]{:S(2)}) copy-start(bf16[512,256]{1,0:T(8,128)(2,1)} %refs_1_.3) | copy-start | bytes 786436
  21.7 4.9 %copy-start.1 = (bf16[512,512]{1,0:T(8,128)(2,1)S(1)}, bf16[512,512]{1,0:T(8,128)(2,1)}, u32[]{:S(2)}) copy-start(bf16[512,512]{1,0:T(8,128)(2,1)} %refs_6_.1) | copy-start | bytes 1572868
  21.7 4.9 %copy-start.2 = (bf16[512,256]{1,0:T(8,128)(2,1)S(1)}, bf16[512,256]{1,0:T(8,128)(2,1)}, u32[]{:S(2)}) copy-start(bf16[512,256]{1,0:T(8,128)(2,1)} %refs_5_.2) | copy-start | bytes 786436
  21.8 6.1 %collective-permute-start.12 = (bf16[256,128]{1,0:T(8,128)(2,1)S(1)}, bf16[256,128]{1,0:T(8,128)(2,1)S(1)}, u32[]{:S(2)}, u32[]{:S(2)}) collective-permute-start(bf16[256,128]{1,0:T(8,128)(2,1)S(1)} %get-tuple-element.42), channel_id=1, source_target_pairs={{0,6},{2,4},{4,2},{6,0},{8,14},{10,12},{12,10},{14,8},{16,22},{18,... | collective-permute-start | bytes 196616 | tf_op jit(solution)/shard_map/ppermute | solution.py:421
  23.4 5.8 %collective-permute-start.13 = (bf16[256,128]{1,0:T(8,128)(2,1)S(1)}, bf16[256,128]{1,0:T(8,128)(2,1)S(1)}, u32[]{:S(2)}, u32[]{:S(2)}) collective-permute-start(bf16[256,128]{1,0:T(8,128)(2,1)S(1)} %get-tuple-element.43), channel_id=1, source_target_pairs={{0,4},{2,6},{4,0},{6,2},{8,12},{10,14},{12,8},{14,10},{16,20},{18,... | collective-permute-start | bytes 196616 | tf_op jit(solution)/shard_map/ppermute | solution.py:421
  23.9 2.7 %copy-start.4 = (f32[512,1]{0,1:T(1,128)S(1)}, f32[512,1]{0,1:T(1,128)}, u32[]{:S(2)}) copy-start(f32[512,1]{0,1:T(1,128)} %param.12) | copy-start | bytes 6148
  23.9 5.2 %collective-permute-start.14 = (bf16[256,128]{1,0:T(8,128)(2,1)S(1)}, bf16[256,128]{1,0:T(8,128)(2,1)S(1)}, u32[]{:S(2)}, u32[]{:S(2)}) collective-permute-start(bf16[256,128]{1,0:T(8,128)(2,1)S(1)} %get-tuple-element.44), channel_id=1, source_target_pairs={{0,2},{2,0},{4,6},{6,4},{8,10},{10,8},{12,14},{14,12},{16,18},{18,... | collective-permute-start | bytes 196616 | tf_op jit(solution)/shard_map/ppermute | solution.py:421
  25.5 5.1 %collective-permute-start.15 = (bf16[128,512]{1,0:T(8,128)(2,1)S(1)}, bf16[128,512]{1,0:T(8,128)(2,1)S(1)}, u32[]{:S(2)}, u32[]{:S(2)}) collective-permute-start(bf16[128,512]{1,0:T(8,128)(2,1)S(1)} %collective-permute-done.6.refs_0_.refs_5_), channel_id=1, source_target_pairs={{0,4},{1,3},{2,6},{3,1},{4,0},{5,7},{6,2},{7,5},{8,12},{9,11},{10,... | collective-permute-start | bytes 393224 | tf_op jit(solution)/shard_map/ppermute | solution.py:417
  29.5 2.0 %collective-permute-start.16 = (bf16[512,512]{1,0:T(8,128)(2,1)S(1)}, bf16[512,512]{1,0:T(8,128)(2,1)S(1)}, u32[]{:S(2)}, u32[]{:S(2)}) collective-permute-start(bf16[512,512]{1,0:T(8,128)(2,1)S(1)} %shard_map.84.refs_0_), channel_id=1, source_target_pairs={{0,1},{1,0},{2,3},{3,2},{4,5},{5,4},{6,7},{7,6},{8,9},{9,8},{10,11... | collective-permute-start | bytes 1572872 | tf_op jit(solution)/shard_map/ppermute | solution.py:511
